TPU v7x, 1024 devices: a whole 8x8x8 slice. The times are simulated.
1024 devices in a mesh: node: 32 (over y, x_lo), expert: 32 (over z, x_hi, core).
Axes of the slice: x: 8 (x_hi: 2, x_lo: 4; x = x_hi * 4 + x_lo), y: 8, z: 8, core: 2. Of those that a mesh axis runs over, the one named last changes fastest.
Arguments:
- grad_out: bfloat16 [8192, 7168], P(('node', 'expert')), may hold values from -6 to 6
- cross_rows: int32 [32, 32, 32, 1], P('node', 'expert'), may hold values from 0 to 7, as said below
- slot_rows: int32 [32, 32, 4, 16], P('node', 'expert'), may hold values from -1 to 31, as said below
- route_prob: float32 [32, 32, 4, 16], P('node', 'expert'), may hold values from 0.05 to 1
- w_down: bfloat16 [32, 32, 1024, 896], P('node', 'expert'), may hold values from -0.1875 to 0.1875
- gate_pre: bfloat16 [32, 32, 32, 16, 128], P('node', 'expert'), may hold values from -6 to 6
- up_pre: bfloat16 [32, 32, 32, 16, 128], P('node', 'expert'), may hold values from -6 to 6
Outputs:
- grad_gate: bfloat16 [32, 32, 32, 16, 128], P('node', 'expert')
- grad_up: bfloat16 [32, 32, 32, 16, 128], P('node', 'expert')
Inputs may be any that keep to these rules, and one draw needn't show every extreme that they name: cross_rows[n, j, g, :] names distinct tokens of device (n, j) and has no empty place; every token of a device is named in exactly 4 of its device's 32 lists. The entries of slot_rows[g, j, e, :] that are not -1 are distinct and come before its -1 entries; they count from 4 to 16.
All inputs are finite; a program needn't handle non-finite values.
Results may differ from a plain program's by a relative error of at most 0.0049.
Values may be sent and summed in bfloat16 or wider, within the bound.
No kernel may reach another device: no remote copies, remote signals or barrier semaphores. Data moves between devices by JAX's collectives and lax.ppermute only.
A program may use at most 32 MiB of HBM per device.

v0:
```python
import jax
import jax.numpy as jnp
from jax import lax
from jax.sharding import PartitionSpec as P


def swapped(value, axis, distance):
    mask = 2**distance
    pairs = [(source, source ^ mask) for source in range(lax.axis_size(axis))]
    return lax.ppermute(value, axis, pairs)


def on_device(grad_out, cross_rows, slot_rows, route_prob, w_down, gate_pre, up_pre):
    token_count = grad_out.shape[0]
    width = grad_out.shape[1]
    source_lists = cross_rows[0, 0]
    group_count = source_lists.shape[0]
    capacity = source_lists.shape[1]
    picker = (
        source_lists[:, :, None] == jnp.arange(token_count, dtype=jnp.int32)[None, None, :]
    ).astype(jnp.bfloat16)
    outgoing = jnp.einsum(
        "gct,td->gcd", picker, grad_out, preferred_element_type=jnp.float32
    ).astype(jnp.bfloat16)
    received = lax.all_to_all(outgoing, "node", split_axis=0, concat_axis=0, tiled=True)
    gateway_rows = group_count * capacity
    pieces = w_down.shape[3]
    splits = width // pieces
    buffer_rows = received.reshape(gateway_rows, splits, pieces)
    slot_list = slot_rows[0, 0]
    slot_total = slot_list.shape[1]
    chooser = (
        slot_list[:, :, None] == jnp.arange(gateway_rows, dtype=jnp.int32)[None, None, :]
    ).astype(jnp.bfloat16)
    selected = jnp.einsum("esp,pkd->eksd", chooser, buffer_rows, preferred_element_type=jnp.float32)
    scaled = (selected * route_prob[0, 0][:, None, :, None]).astype(jnp.bfloat16)
    outbound = scaled.reshape(slot_list.shape[0] * splits, slot_total, pieces)
    arrived = lax.all_to_all(outbound, "expert", split_axis=0, concat_axis=0, tiled=True)
    row_count = arrived.shape[0] * arrived.shape[1]
    partial_value = lax.dot_general(
        arrived.reshape(row_count, pieces),
        w_down[0, 0],
        (((1,), (1,)), ((), ())),
        preferred_element_type=jnp.float32,
    )
    share_width = partial_value.shape[1] // splits
    position = lax.axis_index("expert") % splits
    levels = splits.bit_length() - 1
    combined = partial_value
    for level in range(levels):
        combined = combined + swapped(combined, "expert", level)
    share = lax.dynamic_slice_in_dim(combined, position * share_width, share_width, 1)
    gate_vals = gate_pre[0, 0].reshape(row_count, share_width).astype(jnp.float32)
    up_vals = up_pre[0, 0].reshape(row_count, share_width).astype(jnp.float32)
    sigma = jax.nn.sigmoid(gate_vals)
    grad_up_rows = (share * gate_vals * sigma).astype(jnp.bfloat16)
    grad_gate_rows = (share * up_vals * sigma * (1.0 + gate_vals * (1.0 - sigma))).astype(
        jnp.bfloat16
    )
    return (grad_gate_rows.reshape(gate_pre.shape), grad_up_rows.reshape(up_pre.shape))


def solution(mesh):
    placed = (
        P(("node", "expert"), None),
        P("node", "expert", None, None),
        P("node", "expert", None, None),
        P("node", "expert", None, None),
        P("node", "expert", None, None),
        P("node", "expert", None, None, None),
        P("node", "expert", None, None, None),
    )
    return jax.shard_map(
        on_device,
        mesh=mesh,
        in_specs=placed,
        out_specs=(P("node", "expert", None, None, None), P("node", "expert", None, None, None)),
        check_vma=False,
    )
```

profile of v0, /device:TPU:2, one launch (start us, length us, event | category | flops | bytes accessed | tf_op | source)
XLA Modules:
  0.0 242.3 jit_solution(13717444774368883550)
XLA Ops:
  0.6 0.0 copy-start
  0.6 1.4 fusion
  2.0 0.5 broadcast.17
  2.5 0.9 reduce.1
  3.4 0.3 reshape.53
  3.8 0.0 copy-start.3
  3.8 0.0 copy-start.4
  3.8 27.7 %all_to_all.10 = bf16[32,2,3584]{2,1,0:T(2,128)(2,1)S(1)} all-to-all(bf16[32,2,3584]{2,1,0:T(2,128)(2,1)S(1)} %reshape.53), channel_id=1, replica_groups=mesh['node'=32,'expert'=32] {'node'}, dimensions={0} | all-to-all | bytes 917504 | tf_op jit(solution)/shard_map/all_to_all | solution.py:25
  31.5 0.4 reshape.54
  31.9 2.7 %reduce = bf16[32,7168]{1,0:T(8,128)(2,1)S(1)} reduce(bf16[32,1,7168]{2,1,0:T(2,128)(2,1)S(1)} %reshape.54, bf16[]{:T(256)} %constant.31), dimensions={1}, to_apply=%all_to_all.6.reduce_sub_computation | reduce | bytes 917506 | tf_op jit(solution)/shard_map/all_to_all | solution.py:25
  34.6 0.1 copy.20
  34.7 0.0 copy-done.3
  34.7 0.0 copy-done.4
  34.7 0.4 fusion.3
  35.1 0.1 copy.16
  35.2 48.4 %all_to_all.11 = bf16[32,16,896]{2,1,0:T(8,128)(2,1)S(1)} all-to-all(bf16[32,16,896]{2,1,0:T(8,128)(2,1)S(1)} %bitcast.30), channel_id=1, replica_groups=mesh['node'=32,'expert'=32] {'expert'}, dimensions={0} | all-to-all | bytes 1835008 | tf_op jit(solution)/shard_map/all_to_all | solution.py:38
  83.6 0.0 copy-done
  83.6 1.3 fusion.1
  84.9 1.9 collective-permute-start
  86.9 4.1 %collective-permute-done = f32[512,1024]{1,0:T(8,128)S(1)} collective-permute-done((f32[512,1024]{1,0:T(8,128)S(1)}, f32[512,1024]{1,0:T(8,128)S(1)}, u32[]{:S(2)}, u32[]{:S(2)}) %collective-permute-start) | collective-permute-done | bytes 2097184 | tf_op jit(solution)/shard_map/ppermute | solution.py:10
  91.0 0.6 add.22
  91.5 0.0 copy-start.1
  91.6 0.0 copy-start.2
  91.6 3.6 %collective-permute-start.1 = (f32[512,1024]{1,0:T(8,128)S(1)}, f32[512,1024]{1,0:T(8,128)S(1)}, u32[]{:S(2)}, u32[]{:S(2)}) collective-permute-start(f32[512,1024]{1,0:T(8,128)S(1)} %add.22), channel_id=1, source_target_pairs={{0,2},{1,3},{2,0},{3,1},{4,6},{5,7},{6,4},{7,5},{8,10},{9,11},{10,... | collective-permute-start | bytes 6291464 | tf_op jit(solution)/shard_map/ppermute | solution.py:10
  95.2 93.8 %collective-permute-done.1 = f32[512,1024]{1,0:T(8,128)S(1)} collective-permute-done((f32[512,1024]{1,0:T(8,128)S(1)}, f32[512,1024]{1,0:T(8,128)S(1)}, u32[]{:S(2)}, u32[]{:S(2)}) %collective-permute-start.1) | collective-permute-done | bytes 2097184 | tf_op jit(solution)/shard_map/ppermute | solution.py:10
  189.0 1.7 add.23
  190.7 1.9 collective-permute-start.2
  192.6 47.8 %collective-permute-done.2 = f32[512,1024]{1,0:T(8,128)} collective-permute-done((f32[512,1024]{1,0:T(8,128)}, f32[512,1024]{1,0:T(8,128)}, u32[]{:S(2)}, u32[]{:S(2)}) %collective-permute-start.2) | collective-permute-done | bytes 2097184 | tf_op jit(solution)/shard_map/ppermute | solution.py:10
  240.4 0.0 copy-done.1
  240.4 0.0 copy-done.2
  240.5 1.9 fusion.12
Async XLA Ops:
  0.6 83.0 %copy-start = (bf16[1,1,1024,896]{3,2,1,0:T(8,128)(2,1)S(1)}, bf16[1,1,1024,896]{3,2,1,0:T(8,128)(2,1)}, u32[]{:S(2)}) copy-start(bf16[1,1,1024,896]{3,2,1,0:T(8,128)(2,1)} %param.11) | copy-start | bytes 5505028
  3.8 30.9 %copy-start.3 = (f32[1,1,4,16]{3,2,1,0:T(4,128)S(1)}, f32[1,1,4,16]{3,2,1,0:T(4,128)}, u32[]{:S(2)}) copy-start(f32[1,1,4,16]{3,2,1,0:T(4,128)} %param.10) | copy-start | bytes 772
  3.8 30.9 %copy-start.4 = (s32[1,1,4,16]{3,2,1,0:T(4,128)S(1)}, s32[1,1,4,16]{3,2,1,0:T(4,128)}, u32[]{:S(2)}) copy-start(s32[1,1,4,16]{3,2,1,0:T(4,128)} %param.9) | copy-start | bytes 772
  84.9 6.1 %collective-permute-start = (f32[512,1024]{1,0:T(8,128)S(1)}, f32[512,1024]{1,0:T(8,128)S(1)}, u32[]{:S(2)}, u32[]{:S(2)}) collective-permute-start(f32[512,1024]{1,0:T(8,128)S(1)} %fusion.1), channel_id=1, source_target_pairs={{0,1},{1,0},{2,3},{3,2},{4,5},{5,4},{6,7},{7,6},{8,9},{9,8},{10,11... | collective-permute-start | bytes 6291464 | tf_op jit(solution)/shard_map/ppermute | solution.py:10
  91.5 148.9 %copy-start.1 = (bf16[1,1,32,16,128]{4,3,2,1,0:T(8,128)(2,1)S(1)}, bf16[1,1,32,16,128]{4,3,2,1,0:T(8,128)(2,1)}, u32[]{:S(2)}) copy-start(bf16[1,1,32,16,128]{4,3,2,1,0:T(8,128)(2,1)} %param.12) | copy-start | bytes 393220
  91.6 148.9 %copy-start.2 = (bf16[1,1,32,16,128]{4,3,2,1,0:T(8,128)(2,1)S(1)}, bf16[1,1,32,16,128]{4,3,2,1,0:T(8,128)(2,1)}, u32[]{:S(2)}) copy-start(bf16[1,1,32,16,128]{4,3,2,1,0:T(8,128)(2,1)} %param.13) | copy-start | bytes 393220
  91.6 97.4 %collective-permute-start.1 = (f32[512,1024]{1,0:T(8,128)S(1)}, f32[512,1024]{1,0:T(8,128)S(1)}, u32[]{:S(2)}, u32[]{:S(2)}) collective-permute-start(f32[512,1024]{1,0:T(8,128)S(1)} %add.22), channel_id=1, source_target_pairs={{0,2},{1,3},{2,0},{3,1},{4,6},{5,7},{6,4},{7,5},{8,10},{9,11},{10,... | collective-permute-start | bytes 6291464 | tf_op jit(solution)/shard_map/ppermute | solution.py:10
  190.7 49.8 %collective-permute-start.2 = (f32[512,1024]{1,0:T(8,128)}, f32[512,1024]{1,0:T(8,128)}, u32[]{:S(2)}, u32[]{:S(2)}) collective-permute-start(f32[512,1024]{1,0:T(8,128)} %add.23), channel_id=1, source_target_pairs={{0,4},{1,5},{2,6},{3,7},{4,0},{5,1},{6,2},{7,3},{8,12},{9,13},{10,... | collective-permute-start | bytes 6291464 | tf_op jit(solution)/shard_map/ppermute | solution.py:10
where the time goes:
time: 243 us; the launch traced here: 242 us
  waiting for transfers between devices  146 us (60%)
  blocking collectives  76.1 us (31%)
  other arithmetic  7.81 us (3%)
  starting transfers between devices  7.44 us (3%)
  matrix products  3.09 us (1%)
    ppermute x3, waiting for transfers between devices, swapped(): return lax.ppermute(value, axis, pairs)  146 us
    all_to_all x1, blocking collectives, on_device(): lax.all_to_all(outbound, 'expert', split_axis=0, concat_axis=0, tiled=True)  48.4 us
    all_to_all x1, blocking collectives, on_device(): lax.all_to_all(outgoing, 'node', split_axis=0, concat_axis=0, tiled=True)  27.7 us
    ppermute x3, starting transfers between devices, swapped(): return lax.ppermute(value, axis, pairs)  7.44 us
  transfers between devices with their start and end apart: 3, of which 3 were waited for; matrix products, arithmetic and copies ran while one was open for 0% of the time, Pallas kernels for 0%

commit v1 on v0

v1 whole, which is shorter than its diff:
```python
import jax
import jax.numpy as jnp
from jax import lax
from jax.experimental import pallas as pl
from jax.experimental.pallas import tpu as pltpu
from jax.sharding import Mesh, PartitionSpec as P

NAMES = ("y", "xlo", "zhi", "zlo", "xhi", "core")
EXTENTS = (8, 4, 4, 2, 2, 2)
SWAP = ((0, 1), (1, 0))
STEPS = (0, 2, 1, 3)


def finish(place, keep, got, gate_factor, up_factor, grad_gate, grad_up):
    zhi, core = place[0], place[1]
    for piece, step in enumerate(STEPS):
        at = lax.rem(zhi + 4 - step, 4)
        for rows, whose in ((keep, core), (got, 1 - core)):
            value = rows[piece]
            grad_gate[at, :, whose] = (value * gate_factor[at, :, whose]).astype(grad_gate.dtype)
            grad_up[at, :, whose] = (value * up_factor[at, :, whose]).astype(grad_up.dtype)


def on_device(grad_out, cross_rows, slot_rows, route_prob, w_down, gate_pre, up_pre):
    bf16, f32 = jnp.bfloat16, jnp.float32
    tokens, width = grad_out.shape
    groups = cross_rows.shape[2]
    experts, slots = slot_rows.shape[2:]
    hidden, cols = w_down.shape[2:]
    block = gate_pre.shape[-1]
    core = lax.axis_index("core")

    w_own = w_down[0, 0]
    w_sib = lax.ppermute(w_own, "core", SWAP)

    tok = grad_out.reshape(tokens, 4, 2, cols)
    tok = jnp.where(core == 0, tok, tok[:, :, ::-1])
    picker = (
        cross_rows[0, 0, :, :] == jnp.arange(tokens, dtype=jnp.int32)[None, :]
    ).astype(bf16)
    outgoing = jnp.dot(
        picker, tok.reshape(tokens, width), preferred_element_type=f32
    ).astype(bf16)
    received = lax.all_to_all(
        outgoing.reshape(groups * 4, 2, cols),
        ("y", "xlo", "zlo", "xhi"),
        split_axis=0,
        concat_axis=0,
        tiled=True,
    ).reshape(groups, 4, 2 * cols)

    info = jnp.stack([slot_rows[0, 0].astype(f32), route_prob[0, 0]])
    info_z = lax.ppermute(info, "zlo", SWAP)
    zlo = lax.axis_index("zlo")
    info = jnp.where(zlo == 0, jnp.stack([info, info_z]), jnp.stack([info_z, info]))
    info_x = lax.ppermute(info, "xhi", SWAP)
    xhi = lax.axis_index("xhi")
    info = jnp.where(
        xhi == 0, jnp.stack([info, info_x], 1), jnp.stack([info_x, info], 1)
    ).reshape(4, 2, experts, slots)
    chosen = info[:, 0].astype(jnp.int32)
    prob = info[:, 1]
    chooser = (
        chosen[..., None] == jnp.arange(groups, dtype=jnp.int32)
    ).astype(bf16)
    selected = jnp.einsum("jesn,njd->ejsd", chooser, received, preferred_element_type=f32)
    scaled = (selected * jnp.transpose(prob, (1, 0, 2))[..., None]).astype(bf16)
    scaled = scaled.reshape(experts, 4 * slots, 2 * cols)

    zhi = lax.axis_index("zhi")
    pieces = [lax.dynamic_index_in_dim(scaled, zhi, 0, keepdims=False)]
    for step in STEPS[1:]:
        pairs = [(i, (i + step) % 4) for i in range(4)]
        out = lax.dynamic_index_in_dim(scaled, (zhi + step) % 4, 0, keepdims=False)
        pieces.append(lax.ppermute(out, "zhi", pairs))
    x = jnp.concatenate(pieces, 0)
    dims = (((1,), (1,)), ((), ()))
    half, quarter = hidden // 2, hidden // 4

    def product(start):
        own = lax.dynamic_slice_in_dim(w_own, start, half, 0)
        sib = lax.dynamic_slice_in_dim(w_sib, start, half, 0)
        value = lax.dot_general(x[:, :cols], own, dims, preferred_element_type=f32)
        return value + lax.dot_general(x[:, cols:], sib, dims, preferred_element_type=f32)

    give = product((1 - zlo) * half).astype(bf16)
    got = lax.ppermute(give, "zlo", SWAP)
    part = product(zlo * half) + got.astype(f32)
    give = lax.dynamic_slice_in_dim(part, (1 - xhi) * quarter, quarter, 1).astype(bf16)
    got = lax.ppermute(give, "xhi", SWAP)
    keep = lax.dynamic_slice_in_dim(part, xhi * quarter, quarter, 1)
    part = keep + got.astype(f32)
    give = lax.dynamic_slice_in_dim(part, (1 - core) * block, block, 1)
    keep = lax.dynamic_slice_in_dim(part, core * block, block, 1)
    got = lax.ppermute(give, "core", SWAP)

    gate_vals = gate_pre.astype(f32)
    up_vals = up_pre.astype(f32)
    sigma = jax.nn.sigmoid(gate_vals)
    up_factor = gate_vals * sigma
    gate_factor = up_vals * sigma * (1.0 + gate_vals * (1.0 - sigma))
    deep = (4, 4, 2, slots, block)
    place = jnp.stack([zhi, core]).astype(jnp.int32)
    grad_gate, grad_up = pl.pallas_call(
        finish,
        out_shape=[jax.ShapeDtypeStruct(deep, bf16)] * 2,
        in_specs=[pl.BlockSpec(memory_space=pltpu.SMEM)]
        + [pl.BlockSpec(memory_space=pltpu.VMEM)] * 4,
        out_specs=[pl.BlockSpec(memory_space=pltpu.VMEM)] * 2,
        compiler_params=pltpu.CompilerParams(vmem_limit_bytes=16 << 20),
    )(
        place,
        keep.reshape(4, 4, slots, block),
        got.reshape(4, 4, slots, block),
        gate_factor.reshape(deep),
        up_factor.reshape(deep),
    )
    return grad_gate.reshape(gate_pre.shape), grad_up.reshape(up_pre.shape)


def solution(mesh):
    fine = Mesh(mesh.devices.reshape(EXTENTS), NAMES)
    node, expert = NAMES[:2], NAMES[2:]
    flat = P(node, expert, None, None)
    deep = P(node, expert, None, None, None)
    return jax.shard_map(
        on_device,
        mesh=fine,
        in_specs=(P(node + expert, None), flat, flat, flat, flat, deep, deep),
        out_specs=(deep, deep),
        check_vma=False,
    )
```

time: 243 us -> 108 us (0.44)
  the two profiles are of different devices: /device:TPU:2 before, /device:TPU:1 now
where the time goes in v1:
time: 108 us; the launch traced here: 107 us
  starting transfers between devices  65.7 us (61%)
  waiting for transfers between devices  27.6 us (26%)
  matrix products  5.66 us (5%)
  other arithmetic  3.35 us (3%)
  local copies, waits for them, and re-layouts  2.31 us (2%)
  Pallas kernels  1.29 us (1%)
    ppermute x3, starting transfers between devices, on_device(): pieces.append(lax.ppermute(out, 'zhi', pairs))  20.3 us
    all_to_all x1, starting transfers between devices, on_device(): lax.all_to_all(outgoing.reshape(groups * 4, 2, cols), ('y', 'xlo', 'zlo',...  18 us
    ppermute x3, waiting for transfers between devices, on_device(): pieces.append(lax.ppermute(out, 'zhi', pairs))  14 us
    ppermute x1, starting transfers between devices, on_device(): got = lax.ppermute(give, 'core', SWAP)  6.68 us
    ppermute x1, starting transfers between devices, on_device(): info_x = lax.ppermute(info, 'xhi', SWAP)  6.51 us
    ppermute x1, starting transfers between devices, on_device(): got = lax.ppermute(give, 'xhi', SWAP)  5.44 us
    ppermute x1, waiting for transfers between devices, on_device(): got = lax.ppermute(give, 'zlo', SWAP)  5.36 us
    ppermute x1, waiting for transfers between devices, on_device(): got = lax.ppermute(give, 'xhi', SWAP)  4.26 us
  transfers between devices with their start and end apart: 10, of which 6 were waited for; matrix products, arithmetic and copies ran while one was open for 4% of the time, Pallas kernels for 0%

profile of v1, /device:TPU:1, one launch (start us, length us, event | category | flops | bytes accessed | tf_op | source)
XLA Modules:
  0.0 107.0 jit_solution(15733131480476282391)
XLA Ops:
  0.6 0.0 copy-start
  0.6 0.0 copy-start.2
  0.7 0.0 copy-start.3
  0.7 1.1 %reverse_select_fusion = bf16[8,4,2,896]{3,0,2,1:T(8,128)(2,1)S(1)} fusion(bf16[8,4,2,896]{3,0,2,1:T(8,128)(2,1)} %bitcast.62, pred[]{:T(512)S(6)} %eq.45), kind=kLoop, calls=%fused_computation.36 | loop fusion | flops 57344 | bytes 229377 | tf_op jit(solution)/shard_map/jit(_where)/select_n | solution.py:37
  1.8 1.0 convolution_convert_fusion
  2.8 1.1 %reshape.124 = bf16[128,2,896]{2,1,0:T(2,128)(2,1)} reshape(bf16[32,7168]{1,0:T(8,128)(2,1)S(1)} %convolution_convert_fusion) | data formatting | bytes 917504 | tf_op jit(solution)/shard_map/reshape | solution.py:45
  3.9 18.0 %all-to-all-start = ((bf16[128,2,896]{2,1,0:T(2,128)(2,1)}), bf16[128,2,896]{2,1,0:T(2,128)(2,1)S(1)}, u32[]{:S(2)}, u32[]{:S(2)}) async-start(bf16[128,2,896]{2,1,0:T(2,128)(2,1)} %reshape.124), calls=%async_computation | async-start | bytes 917504 | tf_op jit(solution)/shard_map/all_to_all | solution.py:44
  21.9 0.0 copy-done
  21.9 4.2 %collective-permute-start.5 = (bf16[1024,896]{1,0:T(8,128)(2,1)S(1)}, bf16[1024,896]{1,0:T(8,128)(2,1)}, u32[]{:S(2)}, u32[]{:S(2)}) collective-permute-start(bf16[1024,896]{1,0:T(8,128)(2,1)S(1)} %bitcast.59), channel_id=1, source_target_pairs={{0,1},{1,0},{2,3},{3,2},{4,5},{5,4},{6,7},{7,6},{8,9},{9,8},{10,11... | collective-permute-start | bytes 5505032 | tf_op jit(solution)/shard_map/ppermute | solution.py:34
  26.1 0.0 copy-done.2
  26.1 0.0 copy-done.3
  26.2 2.7 %collective-permute-start = (f32[2,4,16]{2,1,0:T(4,128)S(1)}, f32[2,4,16]{2,1,0:T(4,128)S(1)}, u32[]{:S(2)}, u32[]{:S(2)}) collective-permute-start(f32[2,4,16]{2,1,0:T(4,128)S(1)} %get-tuple-element.18), channel_id=1, source_target_pairs={{0,4},{4,0},{1,5},{5,1},{2,6},{6,2},{3,7},{7,3},{8,12},{12,8},{9,1... | collective-permute-start | bytes 1544 | tf_op jit(solution)/shard_map/ppermute | solution.py:53
  28.9 2.0 %collective-permute-done = f32[2,4,16]{2,1,0:T(4,128)S(1)} collective-permute-done((f32[2,4,16]{2,1,0:T(4,128)S(1)}, f32[2,4,16]{2,1,0:T(4,128)S(1)}, u32[]{:S(2)}, u32[]{:S(2)}) %collective-permute-start) | collective-permute-done | bytes 544 | tf_op jit(solution)/shard_map/ppermute | solution.py:53
  30.9 6.5 %collective-permute-start.1 = (f32[2,2,4,16]{3,2,1,0:T(4,128)S(1)}, f32[2,2,4,16]{3,2,1,0:T(4,128)S(1)}, u32[]{:S(2)}, u32[]{:S(2)}) collective-permute-start(f32[2,2,4,16]{3,2,1,0:T(4,128)S(1)} %maximum_select_fusion.2), channel_id=1, source_target_pairs={{0,2},{2,0},{1,3},{3,1},{4,6},{6,4},{5,7},{7,5},{8,10},{10,8},{9,1... | collective-permute-start | bytes 3080 | tf_op jit(solution)/shard_map/ppermute | solution.py:56
  37.4 2.0 %collective-permute-done.1 = f32[2,2,4,16]{3,2,1,0:T(4,128)S(1)} collective-permute-done((f32[2,2,4,16]{3,2,1,0:T(4,128)S(1)}, f32[2,2,4,16]{3,2,1,0:T(4,128)S(1)}, u32[]{:S(2)}, u32[]{:S(2)}) %collective-permute-start.1) | collective-permute-done | bytes 1056 | tf_op jit(solution)/shard_map/ppermute | solution.py:56
  39.5 0.0 all-to-all-done
  39.5 0.3 reshape.125
  39.8 0.5 fusion.1
  40.2 0.1 copy.12
  40.3 0.1 dynamic-slice_bitcast_fusion.3
  40.4 12.6 %collective-permute-start.2 = (bf16[64,1792]{1,0:T(8,128)(2,1)S(1)}, bf16[64,1792]{1,0:T(8,128)(2,1)S(1)}, u32[]{:S(2)}, u32[]{:S(2)}) collective-permute-start(bf16[64,1792]{1,0:T(8,128)(2,1)S(1)} %get-tuple-element.9), channel_id=1, source_target_pairs={{0,16},{8,24},{16,0},{24,8},{1,17},{9,25},{17,1},{25,9},{2,18},{10... | collective-permute-start | bytes 688136 | tf_op jit(solution)/shard_map/ppermute | solution.py:75
  53.0 5.8 %collective-permute-start.3 = (bf16[64,1792]{1,0:T(8,128)(2,1)S(1)}, bf16[64,1792]{1,0:T(8,128)(2,1)S(1)}, u32[]{:S(2)}, u32[]{:S(2)}) collective-permute-start(bf16[64,1792]{1,0:T(8,128)(2,1)S(1)} %get-tuple-element.8), channel_id=1, source_target_pairs={{0,8},{8,16},{16,24},{24,0},{1,9},{9,17},{17,25},{25,1},{2,10},{10... | collective-permute-start | bytes 688136 | tf_op jit(solution)/shard_map/ppermute | solution.py:75
  58.8 1.9 %collective-permute-start.4 = (bf16[64,1792]{1,0:T(8,128)(2,1)S(1)}, bf16[64,1792]{1,0:T(8,128)(2,1)S(1)}, u32[]{:S(2)}, u32[]{:S(2)}) collective-permute-start(bf16[64,1792]{1,0:T(8,128)(2,1)S(1)} %get-tuple-element.7), channel_id=1, source_target_pairs={{0,24},{8,0},{16,8},{24,16},{1,25},{9,1},{17,9},{25,17},{2,26},{10... | collective-permute-start | bytes 688136 | tf_op jit(solution)/shard_map/ppermute | solution.py:75
  60.7 0.0 collective-permute-done.2
  60.7 10.1 %collective-permute-done.3 = bf16[64,1792]{1,0:T(8,128)(2,1)S(1)} collective-permute-done((bf16[64,1792]{1,0:T(8,128)(2,1)S(1)}, bf16[64,1792]{1,0:T(8,128)(2,1)S(1)}, u32[]{:S(2)}, u32[]{:S(2)}) %collective-permute-start.3) | collective-permute-done | bytes 229408 | tf_op jit(solution)/shard_map/ppermute | solution.py:75
  70.8 3.9 %collective-permute-done.4 = bf16[64,1792]{1,0:T(8,128)(2,1)S(1)} collective-permute-done((bf16[64,1792]{1,0:T(8,128)(2,1)S(1)}, bf16[64,1792]{1,0:T(8,128)(2,1)S(1)}, u32[]{:S(2)}, u32[]{:S(2)}) %collective-permute-start.4) | collective-permute-done | bytes 229408 | tf_op jit(solution)/shard_map/ppermute | solution.py:75
  74.7 0.0 copy-start.1
  74.7 0.7 copy-done.1
  75.4 1.0 pad_maximum_fusion
  76.4 0.0 collective-permute-done.5
  76.4 1.6 %fusion.6 = f32[256,512]{1,0:T(8,128)S(1)} fusion(bf16[1024,896]{1,0:T(8,128)(2,1)} %collective-permute-done.5, s32[]{:T(128)S(6)} %select_n.104, bf16[256,1792]{1,0:T(8,128)(2,1)S(1)} %pad_maximum_fusion), kind=kOutput, calls=%fused_computation.11 | convolution fusion | flops 234881024 | bytes 1900548 | tf_op jit(solution)/shard_map/dot_general | solution.py:84
  78.1 0.5 fusion.3
  78.5 1.9 %collective-permute-start.6 = (bf16[256,512]{1,0:T(8,128)(2,1)S(1)}, bf16[256,512]{1,0:T(8,128)(2,1)S(1)}, u32[]{:S(2)}, u32[]{:S(2)}) collective-permute-start(bf16[256,512]{1,0:T(8,128)(2,1)S(1)} %fusion.3), channel_id=1, source_target_pairs={{0,4},{4,0},{1,5},{5,1},{2,6},{6,2},{3,7},{7,3},{8,12},{12,8},{9,1... | collective-permute-start | bytes 786440 | tf_op jit(solution)/shard_map/ppermute | solution.py:87
  80.5 1.6 %fusion.9 = f32[256,512]{1,0:T(8,128)S(1)} fusion(bf16[1024,896]{1,0:T(8,128)(2,1)} %collective-permute-done.5, s32[]{:T(128)S(6)} %select_n.103, bf16[256,1792]{1,0:T(8,128)(2,1)S(1)} %pad_maximum_fusion), kind=kOutput, calls=%fused_computation.14 | convolution fusion | flops 234881024 | bytes 1900548 | tf_op jit(solution)/shard_map/dot_general | solution.py:84
  82.1 5.4 %collective-permute-done.6 = bf16[256,512]{1,0:T(8,128)(2,1)S(1)} collective-permute-done((bf16[256,512]{1,0:T(8,128)(2,1)S(1)}, bf16[256,512]{1,0:T(8,128)(2,1)S(1)}, u32[]{:S(2)}, u32[]{:S(2)}) %collective-permute-start.6) | collective-permute-done | bytes 262176 | tf_op jit(solution)/shard_map/ppermute | solution.py:87
  87.5 0.5 fusion.2
  88.0 5.4 %collective-permute-start.7 = (bf16[256,256]{1,0:T(8,128)(2,1)S(1)}, bf16[256,256]{1,0:T(8,128)(2,1)S(1)}, u32[]{:S(2)}, u32[]{:S(2)}) collective-permute-start(bf16[256,256]{1,0:T(8,128)(2,1)S(1)} %dynamic-slice_convert_fusion), channel_id=1, source_target_pairs={{0,2},{2,0},{1,3},{3,1},{4,6},{6,4},{5,7},{7,5},{8,10},{10,8},{9,1... | collective-permute-start | bytes 393224 | tf_op jit(solution)/shard_map/ppermute | solution.py:90
  93.5 4.3 %collective-permute-done.7 = bf16[256,256]{1,0:T(8,128)(2,1)S(1)} collective-permute-done((bf16[256,256]{1,0:T(8,128)(2,1)S(1)}, bf16[256,256]{1,0:T(8,128)(2,1)S(1)}, u32[]{:S(2)}, u32[]{:S(2)}) %collective-permute-start.7) | collective-permute-done | bytes 131104 | tf_op jit(solution)/shard_map/ppermute | solution.py:90
  97.8 6.7 %collective-permute-start.8 = (f32[256,128]{1,0:T(8,128)S(1)}, f32[256,128]{1,0:T(8,128)S(1)}, u32[]{:S(2)}, u32[]{:S(2)}) collective-permute-start(f32[256,128]{1,0:T(8,128)S(1)} %get-tuple-element.10), channel_id=1, source_target_pairs={{0,1},{1,0},{2,3},{3,2},{4,5},{5,4},{6,7},{7,6},{8,9},{9,8},{10,11... | collective-permute-start | bytes 393224 | tf_op jit(solution)/shard_map/ppermute | solution.py:95
  104.5 1.1 %convert_multiply_fusion = (f32[1,1,32,16,128]{4,3,2,1,0:T(8,128)S(1)}, f32[1,1,32,16,128]{4,3,2,1,0:T(8,128)S(1)}) fusion(bf16[1,1,32,16,128]{4,3,2,1,0:T(8,128)(2,1)} %param.12, bf16[1,1,32,16,128]{4,3,2,1,0:T(8,128)(2,1)} %param.13), kind=kLoop, calls=%fused_computation.22 | loop fusion | flops 720896 | bytes 786432 | tf_op jit(solution)/shard_map/mul | solution.py:100
  105.6 0.1 pad_add_fusion.place
  105.7 0.0 collective-permute-done.8
  105.7 1.3 %shard_map.86 = (bf16[4,4,2,16,128]{4,3,2,1,0:T(8,128)(2,1)}, bf16[4,4,2,16,128]{4,3,2,1,0:T(8,128)(2,1)}) custom-call(s32[2]{0:T(128)S(1)} %pad_add_fusion.place, f32[4,4,16,128]{3,2,1,0:T(8,128)S(1)} %bitcast.56, f32[4,4,16,128]{3,2,1,0:T(8,128)S(1)} %bitcast.57, f32[4,4,2,16,128]{4,3,2,1,0:T(8,128)S(1)} %bitcast.55, f32[4,4,2,16,128]{4,3,2,1,0:T(8,128)S(1)} %bitcast.54), custom_call_target="tpu_custom_call" | custom-call | tf_op jit(solution)/shard_map/pallas_call | solution.py:104
  (9 shorter events, 0.1 us)
Async XLA Ops:
  0.6 21.2 %copy-start = (bf16[1,1,1024,896]{3,2,1,0:T(8,128)(2,1)S(1)}, bf16[1,1,1024,896]{3,2,1,0:T(8,128)(2,1)}, u32[]{:S(2)}) copy-start(bf16[1,1,1024,896]{3,2,1,0:T(8,128)(2,1)} %param.11) | copy-start | bytes 5505028
  0.6 25.5 %copy-start.2 = (s32[1,1,4,16]{3,2,1,0:T(4,128)S(1)}, s32[1,1,4,16]{3,2,1,0:T(4,128)}, u32[]{:S(2)}) copy-start(s32[1,1,4,16]{3,2,1,0:T(4,128)} %param.9) | copy-start | bytes 772
  0.7 25.5 %copy-start.3 = (f32[1,1,4,16]{3,2,1,0:T(4,128)S(1)}, f32[1,1,4,16]{3,2,1,0:T(4,128)}, u32[]{:S(2)}) copy-start(f32[1,1,4,16]{3,2,1,0:T(4,128)} %param.10) | copy-start | bytes 772
  3.9 35.6 %all-to-all-start = ((bf16[128,2,896]{2,1,0:T(2,128)(2,1)}), bf16[128,2,896]{2,1,0:T(2,128)(2,1)S(1)}, u32[]{:S(2)}, u32[]{:S(2)}) async-start(bf16[128,2,896]{2,1,0:T(2,128)(2,1)} %reshape.124), calls=%async_computation | async-start | bytes 917504 | tf_op jit(solution)/shard_map/all_to_all | solution.py:44
  21.9 54.5 %collective-permute-start.5 = (bf16[1024,896]{1,0:T(8,128)(2,1)S(1)}, bf16[1024,896]{1,0:T(8,128)(2,1)}, u32[]{:S(2)}, u32[]{:S(2)}) collective-permute-start(bf16[1024,896]{1,0:T(8,128)(2,1)S(1)} %bitcast.59), channel_id=1, source_target_pairs={{0,1},{1,0},{2,3},{3,2},{4,5},{5,4},{6,7},{7,6},{8,9},{9,8},{10,11... | collective-permute-start | bytes 5505032 | tf_op jit(solution)/shard_map/ppermute | solution.py:34
  26.2 4.7 %collective-permute-start = (f32[2,4,16]{2,1,0:T(4,128)S(1)}, f32[2,4,16]{2,1,0:T(4,128)S(1)}, u32[]{:S(2)}, u32[]{:S(2)}) collective-permute-start(f32[2,4,16]{2,1,0:T(4,128)S(1)} %get-tuple-element.18), channel_id=1, source_target_pairs={{0,4},{4,0},{1,5},{5,1},{2,6},{6,2},{3,7},{7,3},{8,12},{12,8},{9,1... | collective-permute-start | bytes 1544 | tf_op jit(solution)/shard_map/ppermute | solution.py:53
  30.9 8.6 %collective-permute-start.1 = (f32[2,2,4,16]{3,2,1,0:T(4,128)S(1)}, f32[2,2,4,16]{3,2,1,0:T(4,128)S(1)}, u32[]{:S(2)}, u32[]{:S(2)}) collective-permute-start(f32[2,2,4,16]{3,2,1,0:T(4,128)S(1)} %maximum_select_fusion.2), channel_id=1, source_target_pairs={{0,2},{2,0},{1,3},{3,1},{4,6},{6,4},{5,7},{7,5},{8,10},{10,8},{9,1... | collective-permute-start | bytes 3080 | tf_op jit(solution)/shard_map/ppermute | solution.py:56
  40.4 20.3 %collective-permute-start.2 = (bf16[64,1792]{1,0:T(8,128)(2,1)S(1)}, bf16[64,1792]{1,0:T(8,128)(2,1)S(1)}, u32[]{:S(2)}, u32[]{:S(2)}) collective-permute-start(bf16[64,1792]{1,0:T(8,128)(2,1)S(1)} %get-tuple-element.9), channel_id=1, source_target_pairs={{0,16},{8,24},{16,0},{24,8},{1,17},{9,25},{17,1},{25,9},{2,18},{10... | collective-permute-start | bytes 688136 | tf_op jit(solution)/shard_map/ppermute | solution.py:75
  53.0 17.8 %collective-permute-start.3 = (bf16[64,1792]{1,0:T(8,128)(2,1)S(1)}, bf16[64,1792]{1,0:T(8,128)(2,1)S(1)}, u32[]{:S(2)}, u32[]{:S(2)}) collective-permute-start(bf16[64,1792]{1,0:T(8,128)(2,1)S(1)} %get-tuple-element.8), channel_id=1, source_target_pairs={{0,8},{8,16},{16,24},{24,0},{1,9},{9,17},{17,25},{25,1},{2,10},{10... | collective-permute-start | bytes 688136 | tf_op jit(solution)/shard_map/ppermute | solution.py:75
  58.8 15.9 %collective-permute-start.4 = (bf16[64,1792]{1,0:T(8,128)(2,1)S(1)}, bf16[64,1792]{1,0:T(8,128)(2,1)S(1)}, u32[]{:S(2)}, u32[]{:S(2)}) collective-permute-start(bf16[64,1792]{1,0:T(8,128)(2,1)S(1)} %get-tuple-element.7), channel_id=1, source_target_pairs={{0,24},{8,0},{16,8},{24,16},{1,25},{9,1},{17,9},{25,17},{2,26},{10... | collective-permute-start | bytes 688136 | tf_op jit(solution)/shard_map/ppermute | solution.py:75
  74.7 0.7 copy-start.1
  78.5 8.9 %collective-permute-start.6 = (bf16[256,512]{1,0:T(8,128)(2,1)S(1)}, bf16[256,512]{1,0:T(8,128)(2,1)S(1)}, u32[]{:S(2)}, u32[]{:S(2)}) collective-permute-start(bf16[256,512]{1,0:T(8,128)(2,1)S(1)} %fusion.3), channel_id=1, source_target_pairs={{0,4},{4,0},{1,5},{5,1},{2,6},{6,2},{3,7},{7,3},{8,12},{12,8},{9,1... | collective-permute-start | bytes 786440 | tf_op jit(solution)/shard_map/ppermute | solution.py:87
  88.0 9.7 %collective-permute-start.7 = (bf16[256,256]{1,0:T(8,128)(2,1)S(1)}, bf16[256,256]{1,0:T(8,128)(2,1)S(1)}, u32[]{:S(2)}, u32[]{:S(2)}) collective-permute-start(bf16[256,256]{1,0:T(8,128)(2,1)S(1)} %dynamic-slice_convert_fusion), channel_id=1, source_target_pairs={{0,2},{2,0},{1,3},{3,1},{4,6},{6,4},{5,7},{7,5},{8,10},{10,8},{9,1... | collective-permute-start | bytes 393224 | tf_op jit(solution)/shard_map/ppermute | solution.py:90
  97.8 7.9 %collective-permute-start.8 = (f32[256,128]{1,0:T(8,128)S(1)}, f32[256,128]{1,0:T(8,128)S(1)}, u32[]{:S(2)}, u32[]{:S(2)}) collective-permute-start(f32[256,128]{1,0:T(8,128)S(1)} %get-tuple-element.10), channel_id=1, source_target_pairs={{0,1},{1,0},{2,3},{3,2},{4,5},{5,4},{6,7},{7,6},{8,9},{9,8},{10,11... | collective-permute-start | bytes 393224 | tf_op jit(solution)/shard_map/ppermute | solution.py:95

commit v2 on v1

v2 whole, which is shorter than its diff:
```python
import jax
import jax.numpy as jnp
from jax import lax
from jax.experimental import pallas as pl
from jax.experimental.pallas import tpu as pltpu
from jax.sharding import Mesh, PartitionSpec as P

NAMES = ("y", "xlo", "zhi", "zlo", "xhi", "core")
EXTENTS = (8, 4, 4, 2, 2, 2)
SWAP = ((0, 1), (1, 0))
STEPS = (0, 2, 1, 3)
SMEM = pl.BlockSpec(memory_space=pltpu.SMEM)
VMEM = pl.BlockSpec(memory_space=pltpu.VMEM)


def pack(crossing_in, slots_in, weights_in, tokens_in, packed, *held):
    arrivals = held[4]
    sources = (crossing_in, slots_in, weights_in, tokens_in)
    copies = [
        pltpu.make_async_copy(source, held[index], arrivals.at[index])
        for index, source in enumerate(sources)
    ]
    for copy in copies:
        copy.start()
    for copy in copies:
        copy.wait()
    crossing, slot_rows, weights, tokens = held[:4]
    f32, bf16 = jnp.float32, jnp.bfloat16
    count, cols = tokens.shape[0], tokens.shape[1] // 8
    groups, span = crossing.shape[1], packed.shape[3]
    weight = weights[...]
    high = weight.astype(bf16).astype(f32)
    middle = (weight - high).astype(bf16).astype(f32)
    low = weight - high - middle
    parts = jnp.concatenate([slot_rows[...].astype(f32), high, middle, low], 0).astype(bf16)
    lines, slots = parts.shape
    behind = span - cols
    spread = (
        lax.broadcasted_iota(jnp.int32, (slots, behind), 1) % slots
        == lax.broadcasted_iota(jnp.int32, (slots, behind), 0)
    ).astype(bf16)
    spread = jnp.dot(parts, spread, preferred_element_type=f32)
    line = lax.broadcasted_iota(jnp.int32, (lines, behind), 0)
    place = lax.broadcasted_iota(jnp.int32, (lines, behind), 1) // slots
    table = [
        jnp.sum(
            jnp.where(line == place + side * lines // 2, spread, 0.0), axis=0, keepdims=True
        ).astype(bf16)
        for side in range(2)
    ]
    at = lax.broadcasted_iota(jnp.int32, (count, groups), 0)
    picker = (crossing[...] == at).astype(bf16)
    for pair in range(4):
        sides = []
        for side in range(2):
            start = (2 * pair + side) * cols
            value = lax.dot_general(
                picker,
                tokens[:, start : start + cols],
                (((0,), (0,)), ((), ())),
                preferred_element_type=f32,
            )
            behind_it = jnp.broadcast_to(table[side], (groups, behind))
            sides.append(jnp.concatenate([value.astype(bf16), behind_it], 1)[:, None, :])
        packed[:, pair, :, :] = jnp.concatenate(sides, 1)


def choose(place, rows, *outs_and_held):
    outs, held = outs_and_held[:4], outs_and_held[4]
    zhi, node = place[0], place[4]
    total, span = rows.shape[0], rows.shape[1] // 2
    cols = outs[0].shape[1] // 2
    slots = held.shape[1]
    wide = 4 * slots
    f32, bf16 = jnp.float32, jnp.bfloat16
    lane = lax.broadcasted_iota(jnp.int32, (8, total), 1)
    line = lax.broadcasted_iota(jnp.int32, (8, total), 0)
    own = (lane == node * 4 + line).astype(bf16)
    first = jnp.dot(own, rows[:, cols:span], preferred_element_type=f32)
    second = jnp.dot(own, rows[:, span + cols :], preferred_element_type=f32)
    at = lax.broadcasted_iota(jnp.int32, (total, wide), 0)
    dims = (((0,), (0,)), ((), ()))
    for gate in range(4):
        slot = first[gate : gate + 1, :wide].astype(jnp.int32)
        match = at == slot * 4 + gate
        weights = (first[gate : gate + 1, wide:], second[gate : gate + 1, :wide], second[gate : gate + 1, wide:])
        pickers = [jnp.where(match, part, 0.0).astype(bf16) for part in weights]
        for side in range(2):
            block = rows[:, side * span : side * span + cols]
            value = sum(
                lax.dot_general(p, block, dims, preferred_element_type=f32) for p in pickers
            ).astype(bf16)
            for expert in range(4):
                held[gate * 4 + expert, :, side * cols : (side + 1) * cols] = value[
                    expert * slots : (expert + 1) * slots
                ]
    for out, step in zip(outs, STEPS):
        expert = lax.rem(zhi + step, 4)
        for gate in range(4):
            out[gate * slots : (gate + 1) * slots, :] = held[gate * 4 + expert]


def arrange(place, w_own, w_sib, blocks):
    core, zlo, xhi = place[1], place[2], place[3]
    size, cols = blocks.shape[1], w_own.shape[1]
    own_at = pl.multiple_of(core * cols, 128)
    sib_at = pl.multiple_of((1 - core) * cols, 128)
    for index in range(4):
        z = 1 - zlo if index < 2 else zlo
        x = 1 - xhi if index % 2 == 0 else xhi
        rows = pl.ds(pl.multiple_of((z * 2 + x) * size, size), size)
        blocks[index, :, pl.ds(own_at, cols)] = w_own[rows, :]
        blocks[index, :, pl.ds(sib_at, cols)] = w_sib[rows, :]


def products(which, first, second, blocks, out):
    size = blocks.shape[1]
    both = jnp.concatenate([first[...], second[...]], 0)
    dims = (((1,), (1,)), ((), ()))
    for index, block in enumerate(which):
        value = lax.dot_general(both, blocks[block], dims, preferred_element_type=jnp.float32)
        out[:, index * size : (index + 1) * size] = value.astype(out.dtype)


def later_products(which, first, second, blocks, keep, got, out, kept):
    size = kept.shape[1]
    total = keep[...] + got[...].astype(jnp.float32)
    out[:, :size] = total[:, :size].astype(out.dtype)
    kept[...] = total[:, size:]
    products(which, first, second, blocks, out.at[:, size:])


def finish(place, keep, got, gate_factor, up_factor, grad_gate, grad_up):
    zhi, core = place[0], place[1]
    for piece, step in enumerate(STEPS):
        at = lax.rem(zhi + 4 - step, 4)
        for rows, whose in ((keep, core), (got, 1 - core)):
            value = rows[piece]
            grad_gate[at, :, whose] = (value * gate_factor[at, :, whose]).astype(grad_gate.dtype)
            grad_up[at, :, whose] = (value * up_factor[at, :, whose]).astype(grad_up.dtype)


def on_device(grad_out, cross_rows, slot_rows, route_prob, w_down, gate_pre, up_pre):
    bf16, f32 = jnp.bfloat16, jnp.float32
    groups = cross_rows.shape[2]
    experts, slots = slot_rows.shape[2:]
    hidden, cols = w_down.shape[2:]
    block = gate_pre.shape[-1]
    zhi, zlo = lax.axis_index("zhi"), lax.axis_index("zlo")
    xhi, core = lax.axis_index("xhi"), lax.axis_index("core")
    node = lax.axis_index("y") * EXTENTS[1] + lax.axis_index("xlo")
    w_own = w_down[0, 0]

    behind = 2 * experts * slots
    span = cols + behind
    inputs = (cross_rows.reshape(1, groups), slot_rows[0, 0], route_prob[0, 0], grad_out)
    outgoing = pl.pallas_call(
        pack,
        out_shape=jax.ShapeDtypeStruct((groups, 4, 2, span), bf16),
        in_specs=[pl.BlockSpec(memory_space=pl.ANY)] * 4,
        out_specs=VMEM,
        scratch_shapes=[pltpu.VMEM(v.shape, v.dtype) for v in inputs]
        + [pltpu.SemaphoreType.DMA((4,))],
        compiler_params=pltpu.CompilerParams(vmem_limit_bytes=56 << 20),
    )(*inputs)
    outgoing = outgoing.reshape(groups * 4, 2, span)
    place = jnp.stack([zhi, core, zlo, xhi, node]).astype(jnp.int32)
    received = lax.all_to_all(
        outgoing,
        ("y", "xlo", "zlo", "xhi"),
        split_axis=0,
        concat_axis=0,
        tiled=True,
    ).reshape(groups * 4, 2 * span)

    w_sib = lax.ppermute(w_own, "core", SWAP)
    size = (4 * slots, 2 * cols)
    chosen = pl.pallas_call(
        choose,
        out_shape=[jax.ShapeDtypeStruct(size, bf16)] * 4,
        in_specs=[SMEM, VMEM],
        out_specs=[VMEM] * 4,
        scratch_shapes=[pltpu.VMEM((4 * experts, slots, 2 * cols), bf16)],
        compiler_params=pltpu.CompilerParams(vmem_limit_bytes=12 << 20),
    )(place, received)
    pieces = [chosen[0]]
    for step, out in zip(STEPS[1:], chosen[1:]):
        pairs = [(i, (i + step) % 4) for i in range(4)]
        pieces.append(lax.ppermute(out, "zhi", pairs))
    rows = 2 * size[0]
    half, quarter = hidden // 2, hidden // 4

    blocks = pl.pallas_call(
        arrange,
        out_shape=jax.ShapeDtypeStruct((4, quarter, 2 * cols), bf16),
        in_specs=[SMEM] + [VMEM] * 2,
        out_specs=VMEM,
        compiler_params=pltpu.CompilerParams(vmem_limit_bytes=12 << 20),
    )(place, w_own, w_sib)

    def multiply(first, second, which, kind):
        return pl.pallas_call(
            lambda *refs: products(which, *refs),
            out_shape=jax.ShapeDtypeStruct((rows, half), kind),
            in_specs=[VMEM] * 3,
            out_specs=VMEM,
            compiler_params=pltpu.CompilerParams(vmem_limit_bytes=12 << 20),
            cost_estimate=pl.CostEstimate(
                flops=2 * rows * half * 2 * cols, bytes_accessed=3 << 20, transcendentals=0
            ),
        )(first, second, blocks)

    give = multiply(pieces[0], pieces[1], (0, 2), bf16)
    got = lax.ppermute(give, "xhi", SWAP)
    keep = multiply(pieces[0], pieces[1], (1, 3), f32)
    third, fourth, _, _ = lax.optimization_barrier((pieces[2], pieces[3], give, keep))
    give, keep_a = pl.pallas_call(
        lambda *refs: later_products((0, 1), *refs),
        out_shape=[
            jax.ShapeDtypeStruct((rows, quarter + half), bf16),
            jax.ShapeDtypeStruct((rows, quarter), f32),
        ],
        in_specs=[VMEM] * 5,
        out_specs=[VMEM] * 2,
        compiler_params=pltpu.CompilerParams(vmem_limit_bytes=12 << 20),
    )(third, fourth, blocks, keep, got)
    got = lax.ppermute(give, "zlo", SWAP)
    keep = multiply(third, fourth, (2, 3), f32)
    give = (keep[:, :quarter] + got[:, quarter:half].astype(f32)).astype(bf16)
    keep_b = keep[:, quarter:] + got[:, half:].astype(f32)
    keep_a = keep_a + got[:, :quarter].astype(f32)
    got = lax.ppermute(give, "xhi", SWAP)
    keep_b = keep_b + got.astype(f32)
    total = jnp.concatenate([keep_a, keep_b], 0)
    give = lax.dynamic_slice_in_dim(total, (1 - core) * block, block, 1)
    keep = lax.dynamic_slice_in_dim(total, core * block, block, 1)
    got = lax.ppermute(give, "core", SWAP)

    gate_vals = gate_pre.astype(f32)
    up_vals = up_pre.astype(f32)
    sigma = jax.nn.sigmoid(gate_vals)
    up_factor = gate_vals * sigma
    gate_factor = up_vals * sigma * (1.0 + gate_vals * (1.0 - sigma))
    deep = (4, 4, 2, slots, block)
    part = (4, 4, slots, block)
    grad_gate, grad_up = pl.pallas_call(
        finish,
        out_shape=[jax.ShapeDtypeStruct(deep, bf16)] * 2,
        in_specs=[SMEM] + [VMEM] * 4,
        out_specs=[VMEM] * 2,
        compiler_params=pltpu.CompilerParams(vmem_limit_bytes=8 << 20),
    )(
        place,
        keep.reshape(part),
        got.reshape(part),
        gate_factor.reshape(deep),
        up_factor.reshape(deep),
    )
    return grad_gate.reshape(gate_pre.shape), grad_up.reshape(up_pre.shape)


def solution(mesh):
    fine = Mesh(mesh.devices.reshape(EXTENTS), NAMES)
    node, expert = NAMES[:2], NAMES[2:]
    flat = P(node, expert, None, None)
    deep = P(node, expert, None, None, None)
    return jax.shard_map(
        on_device,
        mesh=fine,
        in_specs=(P(node + expert, None), flat, flat, flat, flat, deep, deep),
        out_specs=(deep, deep),
        check_vma=False,
    )
```

time: 108 us -> 106 us (0.981)
  Pallas kernels: 1.29 us -> 10.7 us
  waiting for transfers between devices: 27.6 us -> 34.6 us
  starting transfers between devices: 65.7 us -> 59.4 us
  matrix products: 5.66 us -> 0 us
  other arithmetic: 3.35 us -> 0.19 us
  local copies, waits for them, and re-layouts: 2.31 us -> 0.22 us
    all_to_all x1, waiting for transfers between devices: 0.01 us -> 19.3 us  [on_device(): lax.all_to_all(outgoing, ('y', 'xlo', 'zlo', 'xhi'), split_axis=0, concat...]
    ppermute x1, starting transfers between devices: 4.24 us -> 16.2 us  [on_device(): w_sib = lax.ppermute(w_own, 'core', SWAP)]
    all_to_all x1, starting transfers between devices: 18 us -> 6.18 us  [on_device(): lax.all_to_all(outgoing, ('y', 'xlo', 'zlo', 'xhi'), split_axis=0, concat...]
    pallas_call x0 -> x7, Pallas kernels: none -> 9.4 us  [the longest x1 2.85 us: on_device(): pl.pallas_call(pack, out_shape=jax.ShapeDtypeStruct((groups, 4, 2, span),...]
    ppermute x2 -> x0, starting transfers between devices: 9.17 us -> none  [the longest x1 6.51 us: on_device(): info_x = lax.ppermute(info, 'xhi', SWAP)]
    ppermute x3, waiting for transfers between devices: 14 us -> 5.47 us  [on_device(): pieces.append(lax.ppermute(out, 'zhi', pairs))]
    dot_general x6 -> x0, matrix products: 5.66 us -> none  [the longest x2 3.29 us: product(): lax.dot_general(x[:, cols:], sib, dims, preferred_element_type=f32)]
    ppermute x2 -> x0, waiting for transfers between devices: 4.02 us -> none  [the longest x1 2.05 us: on_device(): info_x = lax.ppermute(info, 'xhi', SWAP)]
  transfers between devices with their start and end apart: 10 -> 9, of which waited for: 6 -> 7; matrix products, arithmetic and copies ran while one was open for 4% -> 0% of each run, Pallas kernels for 0% -> 8%
where the time goes in v2:
time: 106 us
  starting transfers between devices  59.4 us (56%)
  waiting for transfers between devices  34.6 us (33%)
  Pallas kernels  10.7 us (10%)
    all_to_all x1, waiting for transfers between devices, on_device(): lax.all_to_all(outgoing, ('y', 'xlo', 'zlo', 'xhi'), split_axis=0, concat...  19.3 us
    ppermute x3, starting transfers between devices, on_device(): pieces.append(lax.ppermute(out, 'zhi', pairs))  18.8 us
    ppermute x1, starting transfers between devices, on_device(): w_sib = lax.ppermute(w_own, 'core', SWAP)  16.2 us
    ppermute x2, starting transfers between devices, on_device(): got = lax.ppermute(give, 'xhi', SWAP)  8.41 us
    ppermute x1, starting transfers between devices, on_device(): got = lax.ppermute(give, 'core', SWAP)  7.72 us
    all_to_all x1, starting transfers between devices, on_device(): lax.all_to_all(outgoing, ('y', 'xlo', 'zlo', 'xhi'), split_axis=0, concat...  6.18 us
    ppermute x3, waiting for transfers between devices, on_device(): pieces.append(lax.ppermute(out, 'zhi', pairs))  5.47 us
    ppermute x2, waiting for transfers between devices, on_device(): got = lax.ppermute(give, 'xhi', SWAP)  5.27 us
  transfers between devices with their start and end apart: 9, of which 7 were waited for; matrix products, arithmetic and copies ran while one was open for 0% of the time, Pallas kernels for 8%

profile of v2, /device:TPU:1, one launch (start us, length us, event | category | flops | bytes accessed | tf_op | source)
XLA Modules:
  0.0 106.0 jit_solution(10362394787072845980)
XLA Ops:
  0.6 0.0 copy-start
  0.6 16.2 %collective-permute-start.3 = (bf16[1024,896]{1,0:T(8,128)(2,1)}, bf16[1024,896]{1,0:T(8,128)(2,1)}, u32[]{:S(2)}, u32[]{:S(2)}) collective-permute-start(bf16[1024,896]{1,0:T(8,128)(2,1)} %bitcast.19), channel_id=1, source_target_pairs={{0,1},{1,0},{2,3},{3,2},{4,5},{5,4},{6,7},{7,6},{8,9},{9,8},{10,11... | collective-permute-start | bytes 5505032 | tf_op jit(solution)/shard_map/ppermute | solution.py:176
  16.8 2.9 %shard_map.86 = bf16[32,4,2,1024]{3,2,1,0:T(2,128)(2,1)} custom-call(s32[1,32]{1,0:T(1,128)} %bitcast.29, s32[4,16]{1,0:T(4,128)} %bitcast.27, f32[4,16]{1,0:T(4,128)} %bitcast.28, bf16[8,7168]{1,0:T(8,128)(2,1)} %tokens_in.1), custom_call_target="tpu_custom_call" | custom-call | tf_op jit(solution)/shard_map/pallas_call | solution.py:157
  19.7 6.2 %all-to-all-start = ((bf16[128,2,1024]{2,1,0:T(2,128)(2,1)}), bf16[128,2,1024]{2,1,0:T(2,128)(2,1)S(1)}, u32[]{:S(2)}, u32[]{:S(2)}) async-start(bf16[128,2,1024]{2,1,0:T(2,128)(2,1)} %bitcast.26), calls=%async_computation | async-start | bytes 1048576 | tf_op jit(solution)/shard_map/all_to_all | solution.py:168
  25.9 0.1 stack.23.place
  26.0 19.3 %all-to-all-done = bf16[128,2,1024]{2,1,0:T(2,128)(2,1)S(1)} async-done(((bf16[128,2,1024]{2,1,0:T(2,128)(2,1)}), bf16[128,2,1024]{2,1,0:T(2,128)(2,1)S(1)}, u32[]{:S(2)}, u32[]{:S(2)}) %all-to-all-start) | async-done | bytes 524320 | tf_op jit(solution)/shard_map/all_to_all | solution.py:168
  45.3 0.1 copy.9
  45.4 1.9 %shard_map.87 = (bf16[64,1792]{1,0:T(8,128)(2,1)S(1)}, bf16[64,1792]{1,0:T(8,128)(2,1)S(1)}, bf16[64,1792]{1,0:T(8,128)(2,1)S(1)}, bf16[64,1792]{1,0:T(8,128)(2,1)S(1)}) custom-call(s32[5]{0:T(128)S(1)} %stack.23.place, bf16[128,2048]{1,0:T(8,128)(2,1)S(1)} %bitcast.18), custom_call_target="tpu_custom_call" | custom-call | tf_op jit(solution)/shard_map/pallas_call | solution.py:178
  47.3 11.1 %collective-permute-start.2 = (bf16[64,1792]{1,0:T(8,128)(2,1)S(1)}, bf16[64,1792]{1,0:T(8,128)(2,1)S(1)}, u32[]{:S(2)}, u32[]{:S(2)}) collective-permute-start(bf16[64,1792]{1,0:T(8,128)(2,1)S(1)} %get-tuple-element.15), channel_id=1, source_target_pairs={{0,16},{8,24},{16,0},{24,8},{1,17},{9,25},{17,1},{25,9},{2,18},{10... | collective-permute-start | bytes 688136 | tf_op jit(solution)/shard_map/ppermute | solution.py:189
  58.4 5.8 %collective-permute-start = (bf16[64,1792]{1,0:T(8,128)(2,1)S(1)}, bf16[64,1792]{1,0:T(8,128)(2,1)S(1)}, u32[]{:S(2)}, u32[]{:S(2)}) collective-permute-start(bf16[64,1792]{1,0:T(8,128)(2,1)S(1)} %get-tuple-element.12), channel_id=1, source_target_pairs={{0,8},{8,16},{16,24},{24,0},{1,9},{9,17},{17,25},{25,1},{2,10},{10... | collective-permute-start | bytes 688136 | tf_op jit(solution)/shard_map/ppermute | solution.py:189
  64.2 1.9 %collective-permute-start.1 = (bf16[64,1792]{1,0:T(8,128)(2,1)S(1)}, bf16[64,1792]{1,0:T(8,128)(2,1)S(1)}, u32[]{:S(2)}, u32[]{:S(2)}) collective-permute-start(bf16[64,1792]{1,0:T(8,128)(2,1)S(1)} %get-tuple-element.13), channel_id=1, source_target_pairs={{0,24},{8,0},{16,8},{24,16},{1,25},{9,1},{17,9},{25,17},{2,26},{10... | collective-permute-start | bytes 688136 | tf_op jit(solution)/shard_map/ppermute | solution.py:189
  66.2 0.0 collective-permute-done.3.w_sib
  66.2 0.0 copy-done
  66.2 1.8 %shard_map.88.refs_2_ = bf16[4,256,1792]{2,1,0:T(8,128)(2,1)S(1)} custom-call(s32[5]{0:T(128)S(1)} %stack.23.place, bf16[1024,896]{1,0:T(8,128)(2,1)S(1)} %bitcast.20, bf16[1024,896]{1,0:T(8,128)(2,1)} %collective-permute-done.3.w_sib), custom_call_target="tpu_custom_call" | custom-call | tf_op jit(solution)/shard_map/pallas_call | solution.py:193
  68.0 0.0 collective-permute-done.2.refs_1_
  68.0 0.7 shard_map.89
  68.7 4.3 %collective-permute-start.4 = (bf16[128,512]{1,0:T(8,128)(2,1)S(1)}, bf16[128,512]{1,0:T(8,128)(2,1)S(1)}, u32[]{:S(2)}, u32[]{:S(2)}) collective-permute-start(bf16[128,512]{1,0:T(8,128)(2,1)S(1)} %shard_map.89), channel_id=1, source_target_pairs={{0,2},{2,0},{1,3},{3,1},{4,6},{6,4},{5,7},{7,5},{8,10},{10,8},{9,1... | collective-permute-start | bytes 393224 | tf_op jit(solution)/shard_map/ppermute | solution.py:214
  73.0 0.7 shard_map.90.refs_3_
  73.7 3.6 %collective-permute-done.refs_0_ = bf16[64,1792]{1,0:T(8,128)(2,1)S(1)} collective-permute-done((bf16[64,1792]{1,0:T(8,128)(2,1)S(1)}, bf16[64,1792]{1,0:T(8,128)(2,1)S(1)}, u32[]{:S(2)}, u32[]{:S(2)}) %collective-permute-start) | collective-permute-done | bytes 229408 | tf_op jit(solution)/shard_map/ppermute | solution.py:189
  77.3 1.9 %collective-permute-done.1.refs_1_ = bf16[64,1792]{1,0:T(8,128)(2,1)S(1)} collective-permute-done((bf16[64,1792]{1,0:T(8,128)(2,1)S(1)}, bf16[64,1792]{1,0:T(8,128)(2,1)S(1)}, u32[]{:S(2)}, u32[]{:S(2)}) %collective-permute-start.1) | collective-permute-done | bytes 229408 | tf_op jit(solution)/shard_map/ppermute | solution.py:189
  79.2 0.4 collective-permute-done.4.refs_4_
  79.6 0.7 shard_map.91
  80.3 0.0 copy-start.1
  80.4 0.0 copy-start.2
  80.4 2.1 %collective-permute-start.5 = (bf16[128,768]{1,0:T(8,128)(2,1)S(1)}, bf16[128,768]{1,0:T(8,128)(2,1)S(1)}, u32[]{:S(2)}, u32[]{:S(2)}) collective-permute-start(bf16[128,768]{1,0:T(8,128)(2,1)S(1)} %get-tuple-element.19), channel_id=1, source_target_pairs={{0,4},{4,0},{1,5},{5,1},{2,6},{6,2},{3,7},{7,3},{8,12},{12,8},{9,1... | collective-permute-start | bytes 589832 | tf_op jit(solution)/shard_map/ppermute | solution.py:227
  82.4 0.7 shard_map.92
  83.1 3.8 %collective-permute-done.5 = bf16[128,768]{1,0:T(8,128)(2,1)S(1)} collective-permute-done((bf16[128,768]{1,0:T(8,128)(2,1)S(1)}, bf16[128,768]{1,0:T(8,128)(2,1)S(1)}, u32[]{:S(2)}, u32[]{:S(2)}) %collective-permute-start.5) | collective-permute-done | bytes 196640 | tf_op jit(solution)/shard_map/ppermute | solution.py:227
  86.9 4.1 %collective-permute-start.6 = (bf16[128,256]{1,0:T(8,128)(2,1)S(1)}, bf16[128,256]{1,0:T(8,128)(2,1)S(1)}, u32[]{:S(2)}, u32[]{:S(2)}) collective-permute-start(bf16[128,256]{1,0:T(8,128)(2,1)S(1)} %fusion.7), channel_id=1, source_target_pairs={{0,2},{2,0},{1,3},{3,1},{4,6},{6,4},{5,7},{7,5},{8,10},{10,8},{9,1... | collective-permute-start | bytes 196616 | tf_op jit(solution)/shard_map/ppermute | solution.py:232
  91.1 4.9 %collective-permute-done.6 = bf16[128,256]{1,0:T(8,128)(2,1)S(1)} collective-permute-done((bf16[128,256]{1,0:T(8,128)(2,1)S(1)}, bf16[128,256]{1,0:T(8,128)(2,1)S(1)}, u32[]{:S(2)}, u32[]{:S(2)}) %collective-permute-start.6) | collective-permute-done | bytes 65568 | tf_op jit(solution)/shard_map/ppermute | solution.py:232
  96.0 7.7 %collective-permute-start.7 = (f32[256,128]{1,0:T(8,128)S(1)}, f32[256,128]{1,0:T(8,128)S(1)}, u32[]{:S(2)}, u32[]{:S(2)}) collective-permute-start(f32[256,128]{1,0:T(8,128)S(1)} %get-tuple-element.22), channel_id=1, source_target_pairs={{0,1},{1,0},{2,3},{3,2},{4,5},{5,4},{6,7},{7,6},{8,9},{9,8},{10,11... | collective-permute-start | bytes 393224 | tf_op jit(solution)/shard_map/ppermute | solution.py:237
  103.7 0.0 copy-done.1
  103.7 0.0 copy-done.2
  103.7 0.1 convert_multiply_fusion
  103.9 0.8 collective-permute-done.7
  104.7 1.3 %shard_map.93 = (bf16[4,4,2,16,128]{4,3,2,1,0:T(8,128)(2,1)}, bf16[4,4,2,16,128]{4,3,2,1,0:T(8,128)(2,1)}) custom-call(s32[5]{0:T(128)S(1)} %stack.23.place, f32[4,4,16,128]{3,2,1,0:T(8,128)S(1)} %bitcast.23, f32[4,4,16,128]{3,2,1,0:T(8,128)S(1)} %bitcast.24, f32[4,4,2,16,128]{4,3,2,1,0:T(8,128)S(1)} %bitcast.22, f32[4,4,2,16,128]{4,3,2,1,0:T(8,128)S(1)} %bitcast.21), custom_call_target="tpu_custom_call" | custom-call | tf_op jit(solution)/shard_map/pallas_call | solution.py:246
  (3 shorter events, 0.1 us)
Async XLA Ops:
  0.6 65.5 %copy-start = (bf16[1,1,1024,896]{3,2,1,0:T(8,128)(2,1)S(1)}, bf16[1,1,1024,896]{3,2,1,0:T(8,128)(2,1)}, u32[]{:S(2)}) copy-start(bf16[1,1,1024,896]{3,2,1,0:T(8,128)(2,1)} %param.11) | copy-start | bytes 5505028
  0.6 65.5 %collective-permute-start.3 = (bf16[1024,896]{1,0:T(8,128)(2,1)}, bf16[1024,896]{1,0:T(8,128)(2,1)}, u32[]{:S(2)}, u32[]{:S(2)}) collective-permute-start(bf16[1024,896]{1,0:T(8,128)(2,1)} %bitcast.19), channel_id=1, source_target_pairs={{0,1},{1,0},{2,3},{3,2},{4,5},{5,4},{6,7},{7,6},{8,9},{9,8},{10,11... | collective-permute-start | bytes 5505032 | tf_op jit(solution)/shard_map/ppermute | solution.py:176
  19.7 25.6 %all-to-all-start = ((bf16[128,2,1024]{2,1,0:T(2,128)(2,1)}), bf16[128,2,1024]{2,1,0:T(2,128)(2,1)S(1)}, u32[]{:S(2)}, u32[]{:S(2)}) async-start(bf16[128,2,1024]{2,1,0:T(2,128)(2,1)} %bitcast.26), calls=%async_computation | async-start | bytes 1048576 | tf_op jit(solution)/shard_map/all_to_all | solution.py:168
  47.3 20.7 %collective-permute-start.2 = (bf16[64,1792]{1,0:T(8,128)(2,1)S(1)}, bf16[64,1792]{1,0:T(8,128)(2,1)S(1)}, u32[]{:S(2)}, u32[]{:S(2)}) collective-permute-start(bf16[64,1792]{1,0:T(8,128)(2,1)S(1)} %get-tuple-element.15), channel_id=1, source_target_pairs={{0,16},{8,24},{16,0},{24,8},{1,17},{9,25},{17,1},{25,9},{2,18},{10... | collective-permute-start | bytes 688136 | tf_op jit(solution)/shard_map/ppermute | solution.py:189
  58.4 18.9 %collective-permute-start = (bf16[64,1792]{1,0:T(8,128)(2,1)S(1)}, bf16[64,1792]{1,0:T(8,128)(2,1)S(1)}, u32[]{:S(2)}, u32[]{:S(2)}) collective-permute-start(bf16[64,1792]{1,0:T(8,128)(2,1)S(1)} %get-tuple-element.12), channel_id=1, source_target_pairs={{0,8},{8,16},{16,24},{24,0},{1,9},{9,17},{17,25},{25,1},{2,10},{10... | collective-permute-start | bytes 688136 | tf_op jit(solution)/shard_map/ppermute | solution.py:189
  64.2 15.0 %collective-permute-start.1 = (bf16[64,1792]{1,0:T(8,128)(2,1)S(1)}, bf16[64,1792]{1,0:T(8,128)(2,1)S(1)}, u32[]{:S(2)}, u32[]{:S(2)}) collective-permute-start(bf16[64,1792]{1,0:T(8,128)(2,1)S(1)} %get-tuple-element.13), channel_id=1, source_target_pairs={{0,24},{8,0},{16,8},{24,16},{1,25},{9,1},{17,9},{25,17},{2,26},{10... | collective-permute-start | bytes 688136 | tf_op jit(solution)/shard_map/ppermute | solution.py:189
  68.7 10.9 %collective-permute-start.4 = (bf16[128,512]{1,0:T(8,128)(2,1)S(1)}, bf16[128,512]{1,0:T(8,128)(2,1)S(1)}, u32[]{:S(2)}, u32[]{:S(2)}) collective-permute-start(bf16[128,512]{1,0:T(8,128)(2,1)S(1)} %shard_map.89), channel_id=1, source_target_pairs={{0,2},{2,0},{1,3},{3,1},{4,6},{6,4},{5,7},{7,5},{8,10},{10,8},{9,1... | collective-permute-start | bytes 393224 | tf_op jit(solution)/shard_map/ppermute | solution.py:214
  80.3 23.4 %copy-start.1 = (bf16[1,1,32,16,128]{4,3,2,1,0:T(8,128)(2,1)S(1)}, bf16[1,1,32,16,128]{4,3,2,1,0:T(8,128)(2,1)}, u32[]{:S(2)}) copy-start(bf16[1,1,32,16,128]{4,3,2,1,0:T(8,128)(2,1)} %param.12) | copy-start | bytes 393220
  80.4 23.4 %copy-start.2 = (bf16[1,1,32,16,128]{4,3,2,1,0:T(8,128)(2,1)S(1)}, bf16[1,1,32,16,128]{4,3,2,1,0:T(8,128)(2,1)}, u32[]{:S(2)}) copy-start(bf16[1,1,32,16,128]{4,3,2,1,0:T(8,128)(2,1)} %param.13) | copy-start | bytes 393220
  80.4 6.5 %collective-permute-start.5 = (bf16[128,768]{1,0:T(8,128)(2,1)S(1)}, bf16[128,768]{1,0:T(8,128)(2,1)S(1)}, u32[]{:S(2)}, u32[]{:S(2)}) collective-permute-start(bf16[128,768]{1,0:T(8,128)(2,1)S(1)} %get-tuple-element.19), channel_id=1, source_target_pairs={{0,4},{4,0},{1,5},{5,1},{2,6},{6,2},{3,7},{7,3},{8,12},{12,8},{9,1... | collective-permute-start | bytes 589832 | tf_op jit(solution)/shard_map/ppermute | solution.py:227
  86.9 9.0 %collective-permute-start.6 = (bf16[128,256]{1,0:T(8,128)(2,1)S(1)}, bf16[128,256]{1,0:T(8,128)(2,1)S(1)}, u32[]{:S(2)}, u32[]{:S(2)}) collective-permute-start(bf16[128,256]{1,0:T(8,128)(2,1)S(1)} %fusion.7), channel_id=1, source_target_pairs={{0,2},{2,0},{1,3},{3,1},{4,6},{6,4},{5,7},{7,5},{8,10},{10,8},{9,1... | collective-permute-start | bytes 196616 | tf_op jit(solution)/shard_map/ppermute | solution.py:232
  96.0 8.7 %collective-permute-start.7 = (f32[256,128]{1,0:T(8,128)S(1)}, f32[256,128]{1,0:T(8,128)S(1)}, u32[]{:S(2)}, u32[]{:S(2)}) collective-permute-start(f32[256,128]{1,0:T(8,128)S(1)} %get-tuple-element.22), channel_id=1, source_target_pairs={{0,1},{1,0},{2,3},{3,2},{4,5},{5,4},{6,7},{7,6},{8,9},{9,8},{10,11... | collective-permute-start | bytes 393224 | tf_op jit(solution)/shard_map/ppermute | solution.py:237

commit v3 on v2

--- a/solution.py
+++ b/solution.py
@@ -65,8 +65,8 @@
         packed[:, pair, :, :] = jnp.concatenate(sides, 1)
 
 
-def choose(place, rows, *outs_and_held):
-    outs, held = outs_and_held[:4], outs_and_held[4]
+def choose(place, rows, *outs_and_scratch):
+    outs, (held, tables) = outs_and_scratch[:4], outs_and_scratch[4:]
     zhi, node = place[0], place[4]
     total, span = rows.shape[0], rows.shape[1] // 2
     cols = outs[0].shape[1] // 2
@@ -78,26 +78,29 @@
     own = (lane == node * 4 + line).astype(bf16)
     first = jnp.dot(own, rows[:, cols:span], preferred_element_type=f32)
     second = jnp.dot(own, rows[:, span + cols :], preferred_element_type=f32)
-    at = lax.broadcasted_iota(jnp.int32, (total, wide), 0)
+    parts = (first[:, :wide], first[:, wide:], second[:, :wide], second[:, wide:])
+    for gate in range(4):
+        for part in range(4):
+            tables[part : part + 1, gate * wide : (gate + 1) * wide] = parts[part][
+                gate : gate + 1
+            ]
+    at = lax.broadcasted_iota(jnp.int32, (total, 4 * wide), 0)
+    gate = lax.broadcasted_iota(jnp.int32, (1, 4 * wide), 1) // wide
+    match = at == tables[0:1, :].astype(jnp.int32) * 4 + gate
+    pickers = [
+        jnp.where(match, tables[part : part + 1, :], 0.0).astype(bf16) for part in range(1, 4)
+    ]
     dims = (((0,), (0,)), ((), ()))
-    for gate in range(4):
-        slot = first[gate : gate + 1, :wide].astype(jnp.int32)
-        match = at == slot * 4 + gate
-        weights = (first[gate : gate + 1, wide:], second[gate : gate + 1, :wide], second[gate : gate + 1, wide:])
-        pickers = [jnp.where(match, part, 0.0).astype(bf16) for part in weights]
-        for side in range(2):
-            block = rows[:, side * span : side * span + cols]
-            value = sum(
-                lax.dot_general(p, block, dims, preferred_element_type=f32) for p in pickers
-            ).astype(bf16)
-            for expert in range(4):
-                held[gate * 4 + expert, :, side * cols : (side + 1) * cols] = value[
-                    expert * slots : (expert + 1) * slots
-                ]
+    for side in range(2):
+        block = rows[:, side * span : side * span + cols]
+        value = sum(lax.dot_general(p, block, dims, preferred_element_type=f32) for p in pickers)
+        held[:, :, side * cols : (side + 1) * cols] = value.astype(bf16).reshape(
+            held.shape[0], slots, cols
+        )
     for out, step in zip(outs, STEPS):
         expert = lax.rem(zhi + step, 4)
-        for gate in range(4):
-            out[gate * slots : (gate + 1) * slots, :] = held[gate * 4 + expert]
+        for gate_at in range(4):
+            out[gate_at * slots : (gate_at + 1) * slots, :] = held[gate_at * 4 + expert]
 
 
 def arrange(place, w_own, w_sib, blocks):
@@ -120,14 +123,6 @@
     for index, block in enumerate(which):
         value = lax.dot_general(both, blocks[block], dims, preferred_element_type=jnp.float32)
         out[:, index * size : (index + 1) * size] = value.astype(out.dtype)
-
-
-def later_products(which, first, second, blocks, keep, got, out, kept):
-    size = kept.shape[1]
-    total = keep[...] + got[...].astype(jnp.float32)
-    out[:, :size] = total[:, :size].astype(out.dtype)
-    kept[...] = total[:, size:]
-    products(which, first, second, blocks, out.at[:, size:])
 
 
 def finish(place, keep, got, gate_factor, up_factor, grad_gate, grad_up):
@@ -180,7 +175,10 @@
         out_shape=[jax.ShapeDtypeStruct(size, bf16)] * 4,
         in_specs=[SMEM, VMEM],
         out_specs=[VMEM] * 4,
-        scratch_shapes=[pltpu.VMEM((4 * experts, slots, 2 * cols), bf16)],
+        scratch_shapes=[
+            pltpu.VMEM((4 * experts, slots, 2 * cols), bf16),
+            pltpu.VMEM((4, 4 * experts * slots), f32),
+        ],
         compiler_params=pltpu.CompilerParams(vmem_limit_bytes=12 << 20),
     )(place, received)
     pieces = [chosen[0]]
@@ -210,28 +208,23 @@
             ),
         )(first, second, blocks)
 
-    give = multiply(pieces[0], pieces[1], (0, 2), bf16)
-    got = lax.ppermute(give, "xhi", SWAP)
-    keep = multiply(pieces[0], pieces[1], (1, 3), f32)
-    third, fourth, _, _ = lax.optimization_barrier((pieces[2], pieces[3], give, keep))
-    give, keep_a = pl.pallas_call(
-        lambda *refs: later_products((0, 1), *refs),
-        out_shape=[
-            jax.ShapeDtypeStruct((rows, quarter + half), bf16),
-            jax.ShapeDtypeStruct((rows, quarter), f32),
-        ],
-        in_specs=[VMEM] * 5,
-        out_specs=[VMEM] * 2,
-        compiler_params=pltpu.CompilerParams(vmem_limit_bytes=12 << 20),
-    )(third, fourth, blocks, keep, got)
-    got = lax.ppermute(give, "zlo", SWAP)
-    keep = multiply(third, fourth, (2, 3), f32)
-    give = (keep[:, :quarter] + got[:, quarter:half].astype(f32)).astype(bf16)
-    keep_b = keep[:, quarter:] + got[:, half:].astype(f32)
-    keep_a = keep_a + got[:, :quarter].astype(f32)
-    got = lax.ppermute(give, "xhi", SWAP)
-    keep_b = keep_b + got.astype(f32)
-    total = jnp.concatenate([keep_a, keep_b], 0)
+    give_a = multiply(pieces[0], pieces[1], (0, 2), bf16)
+    got_a = lax.ppermute(give_a, "xhi", SWAP)
+    keep_a = multiply(pieces[0], pieces[1], (1, 3), f32)
+    third, fourth, give_a, keep_a = lax.optimization_barrier(
+        (pieces[2], pieces[3], give_a, keep_a)
+    )
+    give_b = multiply(third, fourth, (0, 1), bf16)
+    got_b = lax.ppermute(give_b, "zlo", SWAP)
+    give_a = (keep_a[:, :quarter] + got_a[:, :quarter].astype(f32)).astype(bf16)
+    keep_a = keep_a[:, quarter:] + got_a[:, quarter:].astype(f32)
+    third, give_a = lax.optimization_barrier((third, give_a))
+    got_a = lax.ppermute(give_a, "zlo", SWAP)
+    keep_b = multiply(third, fourth, (2, 3), f32)
+    give_b = (keep_b[:, :quarter] + got_b[:, :quarter].astype(f32)).astype(bf16)
+    keep_b = keep_b[:, quarter:] + got_b[:, quarter:].astype(f32)
+    got_b = lax.ppermute(give_b, "xhi", SWAP)
+    total = jnp.concatenate([keep_a + got_a.astype(f32), keep_b + got_b.astype(f32)], 0)
     give = lax.dynamic_slice_in_dim(total, (1 - core) * block, block, 1)
     keep = lax.dynamic_slice_in_dim(total, core * block, block, 1)
     got = lax.ppermute(give, "core", SWAP)

time: 106 us -> 104 us (0.981); the launches traced: 106 us -> 103 us
  waiting for transfers between devices: 34.6 us -> 31 us
    ppermute x3 -> x4, waiting for transfers between devices: 9.03 us -> 5.34 us  [the longest x1 2.72 us: on_device(): got_b = lax.ppermute(give_b, 'zlo', SWAP)]
    ppermute x3 -> x4, starting transfers between devices: 10.5 us -> 13.4 us  [the longest x1 4.52 us: on_device(): got_b = lax.ppermute(give_b, 'xhi', SWAP)]
    ppermute x1, starting transfers between devices: 7.72 us -> 5.48 us  [on_device(): got = lax.ppermute(give, 'core', SWAP)]
    pallas_call x3 -> x4, Pallas kernels: 2.14 us -> 2.87 us  [multiply(): pl.pallas_call(lambda *refs: products(which, *refs), out_shape=jax.ShapeD...]
  transfers between devices with their start and end apart: 9 -> 10, of which waited for: 7 -> 7; matrix products, arithmetic and copies ran while one was open for 0% -> 0% of each run, Pallas kernels for 8% -> 9%
where the time goes in v3:
time: 104 us; the launch traced here: 103 us
  starting transfers between devices  60 us (58%)
  waiting for transfers between devices  31 us (30%)
  Pallas kernels  10.5 us (10%)
    all_to_all x1, waiting for transfers between devices, on_device(): lax.all_to_all(outgoing, ('y', 'xlo', 'zlo', 'xhi'), split_axis=0, concat...  19.3 us
    ppermute x3, starting transfers between devices, on_device(): pieces.append(lax.ppermute(out, 'zhi', pairs))  18.8 us
    ppermute x1, starting transfers between devices, on_device(): w_sib = lax.ppermute(w_own, 'core', SWAP)  16.2 us
    all_to_all x1, starting transfers between devices, on_device(): lax.all_to_all(outgoing, ('y', 'xlo', 'zlo', 'xhi'), split_axis=0, concat...  6.19 us
    ppermute x3, waiting for transfers between devices, on_device(): pieces.append(lax.ppermute(out, 'zhi', pairs))  5.51 us
    ppermute x1, starting transfers between devices, on_device(): got = lax.ppermute(give, 'core', SWAP)  5.48 us
    ppermute x1, starting transfers between devices, on_device(): got_b = lax.ppermute(give_b, 'xhi', SWAP)  4.52 us
    ppermute x1, starting transfers between devices, on_device(): got_a = lax.ppermute(give_a, 'xhi', SWAP)  4.28 us
  transfers between devices with their start and end apart: 10, of which 7 were waited for; matrix products, arithmetic and copies ran while one was open for 0% of the time, Pallas kernels for 9%

profile of v3, /device:TPU:1, one launch (start us, length us, event | category | flops | bytes accessed | tf_op | source)
XLA Modules:
  0.0 102.9 jit_solution(2812564017819220161)
XLA Ops:
  0.6 0.0 copy-start
  0.6 16.2 %collective-permute-start.3 = (bf16[1024,896]{1,0:T(8,128)(2,1)}, bf16[1024,896]{1,0:T(8,128)(2,1)}, u32[]{:S(2)}, u32[]{:S(2)}) collective-permute-start(bf16[1024,896]{1,0:T(8,128)(2,1)} %bitcast.19), channel_id=1, source_target_pairs={{0,1},{1,0},{2,3},{3,2},{4,5},{5,4},{6,7},{7,6},{8,9},{9,8},{10,11... | collective-permute-start | bytes 5505032 | tf_op jit(solution)/shard_map/ppermute | solution.py:171
  16.8 2.9 %shard_map.86 = bf16[32,4,2,1024]{3,2,1,0:T(2,128)(2,1)} custom-call(s32[1,32]{1,0:T(1,128)} %bitcast.29, s32[4,16]{1,0:T(4,128)} %bitcast.27, f32[4,16]{1,0:T(4,128)} %bitcast.28, bf16[8,7168]{1,0:T(8,128)(2,1)} %tokens_in.1), custom_call_target="tpu_custom_call" | custom-call | tf_op jit(solution)/shard_map/pallas_call | solution.py:152
  19.7 6.2 %all-to-all-start = ((bf16[128,2,1024]{2,1,0:T(2,128)(2,1)}), bf16[128,2,1024]{2,1,0:T(2,128)(2,1)S(1)}, u32[]{:S(2)}, u32[]{:S(2)}) async-start(bf16[128,2,1024]{2,1,0:T(2,128)(2,1)} %bitcast.26), calls=%async_computation | async-start | bytes 1048576 | tf_op jit(solution)/shard_map/all_to_all | solution.py:163
  25.9 0.1 stack.23.place
  26.0 19.3 %all-to-all-done = bf16[128,2,1024]{2,1,0:T(2,128)(2,1)S(1)} async-done(((bf16[128,2,1024]{2,1,0:T(2,128)(2,1)}), bf16[128,2,1024]{2,1,0:T(2,128)(2,1)S(1)}, u32[]{:S(2)}, u32[]{:S(2)}) %all-to-all-start) | async-done | bytes 524320 | tf_op jit(solution)/shard_map/all_to_all | solution.py:163
  45.3 0.1 copy.9
  45.4 1.7 %shard_map.87 = (bf16[64,1792]{1,0:T(8,128)(2,1)S(1)}, bf16[64,1792]{1,0:T(8,128)(2,1)S(1)}, bf16[64,1792]{1,0:T(8,128)(2,1)S(1)}, bf16[64,1792]{1,0:T(8,128)(2,1)S(1)}) custom-call(s32[5]{0:T(128)S(1)} %stack.23.place, bf16[128,2048]{1,0:T(8,128)(2,1)S(1)} %bitcast.18), custom_call_target="tpu_custom_call" | custom-call | tf_op jit(solution)/shard_map/pallas_call | solution.py:173
  47.2 11.1 %collective-permute-start.2 = (bf16[64,1792]{1,0:T(8,128)(2,1)S(1)}, bf16[64,1792]{1,0:T(8,128)(2,1)S(1)}, u32[]{:S(2)}, u32[]{:S(2)}) collective-permute-start(bf16[64,1792]{1,0:T(8,128)(2,1)S(1)} %get-tuple-element.16), channel_id=1, source_target_pairs={{0,16},{8,24},{16,0},{24,8},{1,17},{9,25},{17,1},{25,9},{2,18},{10... | collective-permute-start | bytes 688136 | tf_op jit(solution)/shard_map/ppermute | solution.py:187
  58.2 5.8 %collective-permute-start = (bf16[64,1792]{1,0:T(8,128)(2,1)S(1)}, bf16[64,1792]{1,0:T(8,128)(2,1)S(1)}, u32[]{:S(2)}, u32[]{:S(2)}) collective-permute-start(bf16[64,1792]{1,0:T(8,128)(2,1)S(1)} %get-tuple-element.13), channel_id=1, source_target_pairs={{0,8},{8,16},{16,24},{24,0},{1,9},{9,17},{17,25},{25,1},{2,10},{10... | collective-permute-start | bytes 688136 | tf_op jit(solution)/shard_map/ppermute | solution.py:187
  64.1 1.9 %collective-permute-start.1 = (bf16[64,1792]{1,0:T(8,128)(2,1)S(1)}, bf16[64,1792]{1,0:T(8,128)(2,1)S(1)}, u32[]{:S(2)}, u32[]{:S(2)}) collective-permute-start(bf16[64,1792]{1,0:T(8,128)(2,1)S(1)} %get-tuple-element.14), channel_id=1, source_target_pairs={{0,24},{8,0},{16,8},{24,16},{1,25},{9,1},{17,9},{25,17},{2,26},{10... | collective-permute-start | bytes 688136 | tf_op jit(solution)/shard_map/ppermute | solution.py:187
  66.0 0.0 collective-permute-done.3.w_sib
  66.0 0.0 copy-done
  66.0 1.8 %shard_map.88.refs_2_ = bf16[4,256,1792]{2,1,0:T(8,128)(2,1)S(1)} custom-call(s32[5]{0:T(128)S(1)} %stack.23.place, bf16[1024,896]{1,0:T(8,128)(2,1)S(1)} %bitcast.20, bf16[1024,896]{1,0:T(8,128)(2,1)} %collective-permute-done.3.w_sib), custom_call_target="tpu_custom_call" | custom-call | tf_op jit(solution)/shard_map/pallas_call | solution.py:191
  67.8 0.0 collective-permute-done.2.refs_1_
  67.8 0.7 shard_map.89
  68.6 4.3 %collective-permute-start.4 = (bf16[128,512]{1,0:T(8,128)(2,1)S(1)}, bf16[128,512]{1,0:T(8,128)(2,1)S(1)}, u32[]{:S(2)}, u32[]{:S(2)}) collective-permute-start(bf16[128,512]{1,0:T(8,128)(2,1)S(1)} %shard_map.89), channel_id=1, source_target_pairs={{0,2},{2,0},{1,3},{3,1},{4,6},{6,4},{5,7},{7,5},{8,10},{10,8},{9,1... | collective-permute-start | bytes 393224 | tf_op jit(solution)/shard_map/ppermute | solution.py:212
  72.8 0.7 shard_map.90
  73.6 3.6 %collective-permute-done.refs_0_ = bf16[64,1792]{1,0:T(8,128)(2,1)S(1)} collective-permute-done((bf16[64,1792]{1,0:T(8,128)(2,1)S(1)}, bf16[64,1792]{1,0:T(8,128)(2,1)S(1)}, u32[]{:S(2)}, u32[]{:S(2)}) %collective-permute-start) | collective-permute-done | bytes 229408 | tf_op jit(solution)/shard_map/ppermute | solution.py:187
  77.2 1.9 %collective-permute-done.1.refs_1_ = bf16[64,1792]{1,0:T(8,128)(2,1)S(1)} collective-permute-done((bf16[64,1792]{1,0:T(8,128)(2,1)S(1)}, bf16[64,1792]{1,0:T(8,128)(2,1)S(1)}, u32[]{:S(2)}, u32[]{:S(2)}) %collective-permute-start.1) | collective-permute-done | bytes 229408 | tf_op jit(solution)/shard_map/ppermute | solution.py:187
  79.1 0.7 shard_map.92
  79.8 2.2 %collective-permute-start.6 = (bf16[128,512]{1,0:T(8,128)(2,1)S(1)}, bf16[128,512]{1,0:T(8,128)(2,1)S(1)}, u32[]{:S(2)}, u32[]{:S(2)}) collective-permute-start(bf16[128,512]{1,0:T(8,128)(2,1)S(1)} %shard_map.92), channel_id=1, source_target_pairs={{0,4},{4,0},{1,5},{5,1},{2,6},{6,2},{3,7},{7,3},{8,12},{12,8},{9,1... | collective-permute-start | bytes 393224 | tf_op jit(solution)/shard_map/ppermute | solution.py:218
  82.0 0.0 collective-permute-done.4
  82.1 0.0 copy-start.1
  82.1 0.0 copy-start.2
  82.1 0.7 shard_map.91
  82.8 2.7 %collective-permute-done.6 = bf16[128,512]{1,0:T(8,128)(2,1)S(1)} collective-permute-done((bf16[128,512]{1,0:T(8,128)(2,1)S(1)}, bf16[128,512]{1,0:T(8,128)(2,1)S(1)}, u32[]{:S(2)}, u32[]{:S(2)}) %collective-permute-start.6) | collective-permute-done | bytes 131104 | tf_op jit(solution)/shard_map/ppermute | solution.py:218
  85.5 4.5 %collective-permute-start.7 = (bf16[128,256]{1,0:T(8,128)(2,1)S(1)}, bf16[128,256]{1,0:T(8,128)(2,1)S(1)}, u32[]{:S(2)}, u32[]{:S(2)}) collective-permute-start(bf16[128,256]{1,0:T(8,128)(2,1)S(1)} %fusion.7), channel_id=1, source_target_pairs={{0,2},{2,0},{1,3},{3,1},{4,6},{6,4},{5,7},{7,5},{8,10},{10,8},{9,1... | collective-permute-start | bytes 196616 | tf_op jit(solution)/shard_map/ppermute | solution.py:226
  90.1 2.4 %collective-permute-start.5 = (bf16[128,256]{1,0:T(8,128)(2,1)S(1)}, bf16[128,256]{1,0:T(8,128)(2,1)S(1)}, u32[]{:S(2)}, u32[]{:S(2)}) collective-permute-start(bf16[128,256]{1,0:T(8,128)(2,1)S(1)} %add_convert_fusion), channel_id=1, source_target_pairs={{0,4},{4,0},{1,5},{5,1},{2,6},{6,2},{3,7},{7,3},{8,12},{12,8},{9,1... | collective-permute-start | bytes 196616 | tf_op jit(solution)/shard_map/ppermute | solution.py:222
  92.4 2.0 %collective-permute-done.7 = bf16[128,256]{1,0:T(8,128)(2,1)S(1)} collective-permute-done((bf16[128,256]{1,0:T(8,128)(2,1)S(1)}, bf16[128,256]{1,0:T(8,128)(2,1)S(1)}, u32[]{:S(2)}, u32[]{:S(2)}) %collective-permute-start.7) | collective-permute-done | bytes 65568 | tf_op jit(solution)/shard_map/ppermute | solution.py:226
  94.5 0.6 collective-permute-done.5
  95.1 5.5 %collective-permute-start.8 = (f32[256,128]{1,0:T(8,128)S(1)}, f32[256,128]{1,0:T(8,128)S(1)}, u32[]{:S(2)}, u32[]{:S(2)}) collective-permute-start(f32[256,128]{1,0:T(8,128)S(1)} %get-tuple-element.24), channel_id=1, source_target_pairs={{0,1},{1,0},{2,3},{3,2},{4,5},{5,4},{6,7},{7,6},{8,9},{9,8},{10,11... | collective-permute-start | bytes 393224 | tf_op jit(solution)/shard_map/ppermute | solution.py:230
  100.6 0.0 copy-done.1
  100.6 0.0 copy-done.2
  100.7 0.1 convert_multiply_fusion
  100.8 0.8 collective-permute-done.8
  101.6 1.3 %shard_map.93 = (bf16[4,4,2,16,128]{4,3,2,1,0:T(8,128)(2,1)}, bf16[4,4,2,16,128]{4,3,2,1,0:T(8,128)(2,1)}) custom-call(s32[5]{0:T(128)S(1)} %stack.23.place, f32[4,4,16,128]{3,2,1,0:T(8,128)S(1)} %bitcast.23, f32[4,4,16,128]{3,2,1,0:T(8,128)S(1)} %bitcast.24, f32[4,4,2,16,128]{4,3,2,1,0:T(8,128)S(1)} %bitcast.22, f32[4,4,2,16,128]{4,3,2,1,0:T(8,128)S(1)} %bitcast.21), custom_call_target="tpu_custom_call" | custom-call | tf_op jit(solution)/shard_map/pallas_call | solution.py:239
  (5 shorter events, 0.1 us)
Async XLA Ops:
  0.6 65.4 %copy-start = (bf16[1,1,1024,896]{3,2,1,0:T(8,128)(2,1)S(1)}, bf16[1,1,1024,896]{3,2,1,0:T(8,128)(2,1)}, u32[]{:S(2)}) copy-start(bf16[1,1,1024,896]{3,2,1,0:T(8,128)(2,1)} %param.11) | copy-start | bytes 5505028
  0.6 65.4 %collective-permute-start.3 = (bf16[1024,896]{1,0:T(8,128)(2,1)}, bf16[1024,896]{1,0:T(8,128)(2,1)}, u32[]{:S(2)}, u32[]{:S(2)}) collective-permute-start(bf16[1024,896]{1,0:T(8,128)(2,1)} %bitcast.19), channel_id=1, source_target_pairs={{0,1},{1,0},{2,3},{3,2},{4,5},{5,4},{6,7},{7,6},{8,9},{9,8},{10,11... | collective-permute-start | bytes 5505032 | tf_op jit(solution)/shard_map/ppermute | solution.py:171
  19.7 25.6 %all-to-all-start = ((bf16[128,2,1024]{2,1,0:T(2,128)(2,1)}), bf16[128,2,1024]{2,1,0:T(2,128)(2,1)S(1)}, u32[]{:S(2)}, u32[]{:S(2)}) async-start(bf16[128,2,1024]{2,1,0:T(2,128)(2,1)} %bitcast.26), calls=%async_computation | async-start | bytes 1048576 | tf_op jit(solution)/shard_map/all_to_all | solution.py:163
  47.2 20.7 %collective-permute-start.2 = (bf16[64,1792]{1,0:T(8,128)(2,1)S(1)}, bf16[64,1792]{1,0:T(8,128)(2,1)S(1)}, u32[]{:S(2)}, u32[]{:S(2)}) collective-permute-start(bf16[64,1792]{1,0:T(8,128)(2,1)S(1)} %get-tuple-element.16), channel_id=1, source_target_pairs={{0,16},{8,24},{16,0},{24,8},{1,17},{9,25},{17,1},{25,9},{2,18},{10... | collective-permute-start | bytes 688136 | tf_op jit(solution)/shard_map/ppermute | solution.py:187
  58.2 18.9 %collective-permute-start = (bf16[64,1792]{1,0:T(8,128)(2,1)S(1)}, bf16[64,1792]{1,0:T(8,128)(2,1)S(1)}, u32[]{:S(2)}, u32[]{:S(2)}) collective-permute-start(bf16[64,1792]{1,0:T(8,128)(2,1)S(1)} %get-tuple-element.13), channel_id=1, source_target_pairs={{0,8},{8,16},{16,24},{24,0},{1,9},{9,17},{17,25},{25,1},{2,10},{10... | collective-permute-start | bytes 688136 | tf_op jit(solution)/shard_map/ppermute | solution.py:187
  64.1 15.0 %collective-permute-start.1 = (bf16[64,1792]{1,0:T(8,128)(2,1)S(1)}, bf16[64,1792]{1,0:T(8,128)(2,1)S(1)}, u32[]{:S(2)}, u32[]{:S(2)}) collective-permute-start(bf16[64,1792]{1,0:T(8,128)(2,1)S(1)} %get-tuple-element.14), channel_id=1, source_target_pairs={{0,24},{8,0},{16,8},{24,16},{1,25},{9,1},{17,9},{25,17},{2,26},{10... | collective-permute-start | bytes 688136 | tf_op jit(solution)/shard_map/ppermute | solution.py:187
  68.6 13.5 %collective-permute-start.4 = (bf16[128,512]{1,0:T(8,128)(2,1)S(1)}, bf16[128,512]{1,0:T(8,128)(2,1)S(1)}, u32[]{:S(2)}, u32[]{:S(2)}) collective-permute-start(bf16[128,512]{1,0:T(8,128)(2,1)S(1)} %shard_map.89), channel_id=1, source_target_pairs={{0,2},{2,0},{1,3},{3,1},{4,6},{6,4},{5,7},{7,5},{8,10},{10,8},{9,1... | collective-permute-start | bytes 393224 | tf_op jit(solution)/shard_map/ppermute | solution.py:212
  79.8 5.7 %collective-permute-start.6 = (bf16[128,512]{1,0:T(8,128)(2,1)S(1)}, bf16[128,512]{1,0:T(8,128)(2,1)S(1)}, u32[]{:S(2)}, u32[]{:S(2)}) collective-permute-start(bf16[128,512]{1,0:T(8,128)(2,1)S(1)} %shard_map.92), channel_id=1, source_target_pairs={{0,4},{4,0},{1,5},{5,1},{2,6},{6,2},{3,7},{7,3},{8,12},{12,8},{9,1... | collective-permute-start | bytes 393224 | tf_op jit(solution)/shard_map/ppermute | solution.py:218
  82.1 18.6 %copy-start.1 = (bf16[1,1,32,16,128]{4,3,2,1,0:T(8,128)(2,1)S(1)}, bf16[1,1,32,16,128]{4,3,2,1,0:T(8,128)(2,1)}, u32[]{:S(2)}) copy-start(bf16[1,1,32,16,128]{4,3,2,1,0:T(8,128)(2,1)} %param.12) | copy-start | bytes 393220
  82.1 18.6 %copy-start.2 = (bf16[1,1,32,16,128]{4,3,2,1,0:T(8,128)(2,1)S(1)}, bf16[1,1,32,16,128]{4,3,2,1,0:T(8,128)(2,1)}, u32[]{:S(2)}) copy-start(bf16[1,1,32,16,128]{4,3,2,1,0:T(8,128)(2,1)} %param.13) | copy-start | bytes 393220
  85.5 8.9 %collective-permute-start.7 = (bf16[128,256]{1,0:T(8,128)(2,1)S(1)}, bf16[128,256]{1,0:T(8,128)(2,1)S(1)}, u32[]{:S(2)}, u32[]{:S(2)}) collective-permute-start(bf16[128,256]{1,0:T(8,128)(2,1)S(1)} %fusion.7), channel_id=1, source_target_pairs={{0,2},{2,0},{1,3},{3,1},{4,6},{6,4},{5,7},{7,5},{8,10},{10,8},{9,1... | collective-permute-start | bytes 196616 | tf_op jit(solution)/shard_map/ppermute | solution.py:226
  90.1 5.0 %collective-permute-start.5 = (bf16[128,256]{1,0:T(8,128)(2,1)S(1)}, bf16[128,256]{1,0:T(8,128)(2,1)S(1)}, u32[]{:S(2)}, u32[]{:S(2)}) collective-permute-start(bf16[128,256]{1,0:T(8,128)(2,1)S(1)} %add_convert_fusion), channel_id=1, source_target_pairs={{0,4},{4,0},{1,5},{5,1},{2,6},{6,2},{3,7},{7,3},{8,12},{12,8},{9,1... | collective-permute-start | bytes 196616 | tf_op jit(solution)/shard_map/ppermute | solution.py:222
  95.1 6.5 %collective-permute-start.8 = (f32[256,128]{1,0:T(8,128)S(1)}, f32[256,128]{1,0:T(8,128)S(1)}, u32[]{:S(2)}, u32[]{:S(2)}) collective-permute-start(f32[256,128]{1,0:T(8,128)S(1)} %get-tuple-element.24), channel_id=1, source_target_pairs={{0,1},{1,0},{2,3},{3,2},{4,5},{5,4},{6,7},{7,6},{8,9},{9,8},{10,11... | collective-permute-start | bytes 393224 | tf_op jit(solution)/shard_map/ppermute | solution.py:230

commit v4 on v3

--- a/solution.py
+++ b/solution.py
@@ -14,15 +14,15 @@
 
 
 def pack(crossing_in, slots_in, weights_in, tokens_in, packed, *held):
-    arrivals = held[4]
+    arrivals, built, leaving = held[4:]
     sources = (crossing_in, slots_in, weights_in, tokens_in)
     copies = [
         pltpu.make_async_copy(source, held[index], arrivals.at[index])
         for index, source in enumerate(sources)
     ]
-    for copy in copies:
+    for copy in copies[::-1]:
         copy.start()
-    for copy in copies:
+    for copy in copies[:3]:
         copy.wait()
     crossing, slot_rows, weights, tokens = held[:4]
     f32, bf16 = jnp.float32, jnp.bfloat16
@@ -50,6 +50,8 @@
     ]
     at = lax.broadcasted_iota(jnp.int32, (count, groups), 0)
     picker = (crossing[...] == at).astype(bf16)
+    copies[3].wait()
+    out_copies = []
     for pair in range(4):
         sides = []
         for side in range(2):
@@ -62,7 +64,12 @@
             )
             behind_it = jnp.broadcast_to(table[side], (groups, behind))
             sides.append(jnp.concatenate([value.astype(bf16), behind_it], 1)[:, None, :])
-        packed[:, pair, :, :] = jnp.concatenate(sides, 1)
+        built[pair] = jnp.concatenate(sides, 1)
+        copy = pltpu.make_async_copy(built.at[pair], packed.at[:, pair], leaving.at[pair])
+        copy.start()
+        out_copies.append(copy)
+    for copy in out_copies:
+        copy.wait()
 
 
 def choose(place, rows, *outs_and_scratch):
@@ -153,9 +160,13 @@
         pack,
         out_shape=jax.ShapeDtypeStruct((groups, 4, 2, span), bf16),
         in_specs=[pl.BlockSpec(memory_space=pl.ANY)] * 4,
-        out_specs=VMEM,
+        out_specs=pl.BlockSpec(memory_space=pl.ANY),
         scratch_shapes=[pltpu.VMEM(v.shape, v.dtype) for v in inputs]
-        + [pltpu.SemaphoreType.DMA((4,))],
+        + [
+            pltpu.SemaphoreType.DMA((4,)),
+            pltpu.VMEM((4, groups, 2, span), bf16),
+            pltpu.SemaphoreType.DMA((4,)),
+        ],
         compiler_params=pltpu.CompilerParams(vmem_limit_bytes=56 << 20),
     )(*inputs)
     outgoing = outgoing.reshape(groups * 4, 2, span)
@@ -180,6 +191,7 @@
             pltpu.VMEM((4, 4 * experts * slots), f32),
         ],
         compiler_params=pltpu.CompilerParams(vmem_limit_bytes=12 << 20),
+        cost_estimate=pl.CostEstimate(flops=20 << 30, bytes_accessed=2 << 20, transcendentals=0),
     )(place, received)
     pieces = [chosen[0]]
     for step, out in zip(STEPS[1:], chosen[1:]):
@@ -210,11 +222,10 @@
 
     give_a = multiply(pieces[0], pieces[1], (0, 2), bf16)
     got_a = lax.ppermute(give_a, "xhi", SWAP)
-    keep_a = multiply(pieces[0], pieces[1], (1, 3), f32)
-    third, fourth, give_a, keep_a = lax.optimization_barrier(
-        (pieces[2], pieces[3], give_a, keep_a)
-    )
+    third, fourth, give_a = lax.optimization_barrier((pieces[2], pieces[3], give_a))
     give_b = multiply(third, fourth, (0, 1), bf16)
+    first, give_b = lax.optimization_barrier((pieces[0], give_b))
+    keep_a = multiply(first, pieces[1], (1, 3), f32)
     got_b = lax.ppermute(give_b, "zlo", SWAP)
     give_a = (keep_a[:, :quarter] + got_a[:, :quarter].astype(f32)).astype(bf16)
     keep_a = keep_a[:, quarter:] + got_a[:, quarter:].astype(f32)

time: 104 us -> 100 us (0.962)
  waiting for transfers between devices: 31 us -> 26.2 us
  starting transfers between devices: 60 us -> 62.8 us
  Pallas kernels: 10.5 us -> 9.38 us
    ppermute x1, starting transfers between devices: 16.2 us -> 4.27 us  [on_device(): w_sib = lax.ppermute(w_own, 'core', SWAP)]
    all_to_all x1, starting transfers between devices: 6.19 us -> 18 us  [on_device(): lax.all_to_all(outgoing, ('y', 'xlo', 'zlo', 'xhi'), split_axis=0, concat...]
    all_to_all x1, waiting for transfers between devices: 19.3 us -> 12.2 us  [on_device(): lax.all_to_all(outgoing, ('y', 'xlo', 'zlo', 'xhi'), split_axis=0, concat...]
    ppermute x3, starting transfers between devices: 18.8 us -> 22.6 us  [on_device(): pieces.append(lax.ppermute(out, 'zhi', pairs))]
    ppermute x3, waiting for transfers between devices: 5.51 us -> 8.02 us  [on_device(): pieces.append(lax.ppermute(out, 'zhi', pairs))]
  transfers between devices with their start and end apart: 10 -> 10, of which waited for: 7 -> 7; matrix products, arithmetic and copies ran while one was open for 0% -> 0% of each run, Pallas kernels for 9% -> 5%
where the time goes in v4:
time: 100 us; the launch traced here: 99.7 us
  starting transfers between devices  62.8 us (63%)
  waiting for transfers between devices  26.2 us (26%)
  Pallas kernels  9.38 us (9%)
    ppermute x3, starting transfers between devices, on_device(): pieces.append(lax.ppermute(out, 'zhi', pairs))  22.6 us
    all_to_all x1, starting transfers between devices, on_device(): lax.all_to_all(outgoing, ('y', 'xlo', 'zlo', 'xhi'), split_axis=0, concat...  18 us
    all_to_all x1, waiting for transfers between devices, on_device(): lax.all_to_all(outgoing, ('y', 'xlo', 'zlo', 'xhi'), split_axis=0, concat...  12.2 us
    ppermute x3, waiting for transfers between devices, on_device(): pieces.append(lax.ppermute(out, 'zhi', pairs))  8.02 us
    ppermute x1, starting transfers between devices, on_device(): got = lax.ppermute(give, 'core', SWAP)  5.13 us
    ppermute x1, starting transfers between devices, on_device(): got_a = lax.ppermute(give_a, 'xhi', SWAP)  4.31 us
    ppermute x1, starting transfers between devices, on_device(): w_sib = lax.ppermute(w_own, 'core', SWAP)  4.27 us
    ppermute x1, starting transfers between devices, on_device(): got_b = lax.ppermute(give_b, 'xhi', SWAP)  4.1 us
  transfers between devices with their start and end apart: 10, of which 7 were waited for; matrix products, arithmetic and copies ran while one was open for 0% of the time, Pallas kernels for 5%

profile of v4, /device:TPU:1, one launch (start us, length us, event | category | flops | bytes accessed | tf_op | source)
XLA Modules:
  0.0 99.7 jit_solution(6752386044692386615)
XLA Ops:
  0.6 2.7 %shard_map.86 = bf16[32,4,2,1024]{3,2,1,0:T(2,128)(2,1)} custom-call(s32[1,32]{1,0:T(1,128)} %bitcast.29, s32[4,16]{1,0:T(4,128)} %bitcast.27, f32[4,16]{1,0:T(4,128)} %bitcast.28, bf16[8,7168]{1,0:T(8,128)(2,1)} %tokens_in.1), custom_call_target="tpu_custom_call" | custom-call | tf_op jit(solution)/shard_map/pallas_call | solution.py:159
  3.3 18.0 %all-to-all-start = ((bf16[128,2,1024]{2,1,0:T(2,128)(2,1)}), bf16[128,2,1024]{2,1,0:T(2,128)(2,1)S(1)}, u32[]{:S(2)}, u32[]{:S(2)}) async-start(bf16[128,2,1024]{2,1,0:T(2,128)(2,1)} %bitcast.26), calls=%async_computation | async-start | bytes 1048576 | tf_op jit(solution)/shard_map/all_to_all | solution.py:174
  21.3 4.3 %collective-permute-start.3 = (bf16[1024,896]{1,0:T(8,128)(2,1)}, bf16[1024,896]{1,0:T(8,128)(2,1)S(1)}, u32[]{:S(2)}, u32[]{:S(2)}) collective-permute-start(bf16[1024,896]{1,0:T(8,128)(2,1)} %bitcast.18), channel_id=1, source_target_pairs={{0,1},{1,0},{2,3},{3,2},{4,5},{5,4},{6,7},{7,6},{8,9},{9,8},{10,11... | collective-permute-start | bytes 5505032 | tf_op jit(solution)/shard_map/ppermute | solution.py:182
  25.6 0.1 stack.23.place
  25.7 12.2 %all-to-all-done = bf16[128,2,1024]{2,1,0:T(2,128)(2,1)S(1)} async-done(((bf16[128,2,1024]{2,1,0:T(2,128)(2,1)}), bf16[128,2,1024]{2,1,0:T(2,128)(2,1)S(1)}, u32[]{:S(2)}, u32[]{:S(2)}) %all-to-all-start) | async-done | bytes 524320 | tf_op jit(solution)/shard_map/all_to_all | solution.py:174
  37.9 0.1 copy.9
  38.0 0.0 copy-start
  38.0 1.7 %shard_map.87 = (bf16[64,1792]{1,0:T(8,128)(2,1)S(1)}, bf16[64,1792]{1,0:T(8,128)(2,1)S(1)}, bf16[64,1792]{1,0:T(8,128)(2,1)S(1)}, bf16[64,1792]{1,0:T(8,128)(2,1)S(1)}) custom-call(s32[5]{0:T(128)S(1)} %stack.23.place, bf16[128,2048]{1,0:T(8,128)(2,1)S(1)} %bitcast.22), custom_call_target="tpu_custom_call" | custom-call | flops 21474836480 | bytes 2097152 | tf_op jit(solution)/shard_map/pallas_call | solution.py:184
  39.8 14.8 %collective-permute-start.2 = (bf16[64,1792]{1,0:T(8,128)(2,1)S(1)}, bf16[64,1792]{1,0:T(8,128)(2,1)S(1)}, u32[]{:S(2)}, u32[]{:S(2)}) collective-permute-start(bf16[64,1792]{1,0:T(8,128)(2,1)S(1)} %get-tuple-element.17), channel_id=1, source_target_pairs={{0,16},{8,24},{16,0},{24,8},{1,17},{9,25},{17,1},{25,9},{2,18},{10... | collective-permute-start | bytes 688136 | tf_op jit(solution)/shard_map/ppermute | solution.py:199
  54.6 5.8 %collective-permute-start = (bf16[64,1792]{1,0:T(8,128)(2,1)S(1)}, bf16[64,1792]{1,0:T(8,128)(2,1)S(1)}, u32[]{:S(2)}, u32[]{:S(2)}) collective-permute-start(bf16[64,1792]{1,0:T(8,128)(2,1)S(1)} %get-tuple-element.15), channel_id=1, source_target_pairs={{0,8},{8,16},{16,24},{24,0},{1,9},{9,17},{17,25},{25,1},{2,10},{10... | collective-permute-start | bytes 688136 | tf_op jit(solution)/shard_map/ppermute | solution.py:199
  60.5 1.9 %collective-permute-start.1 = (bf16[64,1792]{1,0:T(8,128)(2,1)S(1)}, bf16[64,1792]{1,0:T(8,128)(2,1)S(1)}, u32[]{:S(2)}, u32[]{:S(2)}) collective-permute-start(bf16[64,1792]{1,0:T(8,128)(2,1)S(1)} %get-tuple-element.16), channel_id=1, source_target_pairs={{0,24},{8,0},{16,8},{24,16},{1,25},{9,1},{17,9},{25,17},{2,26},{10... | collective-permute-start | bytes 688136 | tf_op jit(solution)/shard_map/ppermute | solution.py:199
  62.4 0.0 collective-permute-done.3.w_sib
  62.4 0.0 copy-done
  62.4 0.8 shard_map.88.refs_2_
  63.3 0.0 collective-permute-done.2.refs_1_
  63.3 0.7 shard_map.89
  64.0 4.3 %collective-permute-start.4 = (bf16[128,512]{1,0:T(8,128)(2,1)S(1)}, bf16[128,512]{1,0:T(8,128)(2,1)S(1)}, u32[]{:S(2)}, u32[]{:S(2)}) collective-permute-start(bf16[128,512]{1,0:T(8,128)(2,1)S(1)} %shard_map.89), channel_id=1, source_target_pairs={{0,2},{2,0},{1,3},{3,1},{4,6},{6,4},{5,7},{7,5},{8,10},{10,8},{9,1... | collective-permute-start | bytes 393224 | tf_op jit(solution)/shard_map/ppermute | solution.py:224
  68.3 3.5 %collective-permute-done.refs_0_ = bf16[64,1792]{1,0:T(8,128)(2,1)S(1)} collective-permute-done((bf16[64,1792]{1,0:T(8,128)(2,1)S(1)}, bf16[64,1792]{1,0:T(8,128)(2,1)S(1)}, u32[]{:S(2)}, u32[]{:S(2)}) %collective-permute-start) | collective-permute-done | bytes 229408 | tf_op jit(solution)/shard_map/ppermute | solution.py:199
  71.8 4.5 %collective-permute-done.1.refs_1_ = bf16[64,1792]{1,0:T(8,128)(2,1)S(1)} collective-permute-done((bf16[64,1792]{1,0:T(8,128)(2,1)S(1)}, bf16[64,1792]{1,0:T(8,128)(2,1)S(1)}, u32[]{:S(2)}, u32[]{:S(2)}) %collective-permute-start.1) | collective-permute-done | bytes 229408 | tf_op jit(solution)/shard_map/ppermute | solution.py:199
  76.3 0.7 shard_map.90
  77.1 1.9 %collective-permute-start.6 = (bf16[128,512]{1,0:T(8,128)(2,1)S(1)}, bf16[128,512]{1,0:T(8,128)(2,1)S(1)}, u32[]{:S(2)}, u32[]{:S(2)}) collective-permute-start(bf16[128,512]{1,0:T(8,128)(2,1)S(1)} %shard_map.90), channel_id=1, source_target_pairs={{0,4},{4,0},{1,5},{5,1},{2,6},{6,2},{3,7},{7,3},{8,12},{12,8},{9,1... | collective-permute-start | bytes 393224 | tf_op jit(solution)/shard_map/ppermute | solution.py:229
  79.0 0.7 shard_map.91
  79.7 0.0 collective-permute-done.4
  79.7 0.0 copy-start.1
  79.8 0.0 copy-start.2
  79.8 0.7 shard_map.92
  80.5 2.6 %collective-permute-done.6 = bf16[128,512]{1,0:T(8,128)(2,1)S(1)} collective-permute-done((bf16[128,512]{1,0:T(8,128)(2,1)S(1)}, bf16[128,512]{1,0:T(8,128)(2,1)S(1)}, u32[]{:S(2)}, u32[]{:S(2)}) %collective-permute-start.6) | collective-permute-done | bytes 131104 | tf_op jit(solution)/shard_map/ppermute | solution.py:229
  83.1 4.1 %collective-permute-start.7 = (bf16[128,256]{1,0:T(8,128)(2,1)S(1)}, bf16[128,256]{1,0:T(8,128)(2,1)S(1)}, u32[]{:S(2)}, u32[]{:S(2)}) collective-permute-start(bf16[128,256]{1,0:T(8,128)(2,1)S(1)} %fusion.7), channel_id=1, source_target_pairs={{0,2},{2,0},{1,3},{3,1},{4,6},{6,4},{5,7},{7,5},{8,10},{10,8},{9,1... | collective-permute-start | bytes 196616 | tf_op jit(solution)/shard_map/ppermute | solution.py:237
  87.2 2.5 %collective-permute-start.5 = (bf16[128,256]{1,0:T(8,128)(2,1)S(1)}, bf16[128,256]{1,0:T(8,128)(2,1)S(1)}, u32[]{:S(2)}, u32[]{:S(2)}) collective-permute-start(bf16[128,256]{1,0:T(8,128)(2,1)S(1)} %fusion.9), channel_id=1, source_target_pairs={{0,4},{4,0},{1,5},{5,1},{2,6},{6,2},{3,7},{7,3},{8,12},{12,8},{9,1... | collective-permute-start | bytes 196616 | tf_op jit(solution)/shard_map/ppermute | solution.py:233
  89.7 2.3 %collective-permute-done.7 = bf16[128,256]{1,0:T(8,128)(2,1)S(1)} collective-permute-done((bf16[128,256]{1,0:T(8,128)(2,1)S(1)}, bf16[128,256]{1,0:T(8,128)(2,1)S(1)}, u32[]{:S(2)}, u32[]{:S(2)}) %collective-permute-start.7) | collective-permute-done | bytes 65568 | tf_op jit(solution)/shard_map/ppermute | solution.py:237
  92.0 0.2 collective-permute-done.5
  92.3 5.1 %collective-permute-start.8 = (f32[256,128]{1,0:T(8,128)S(1)}, f32[256,128]{1,0:T(8,128)S(1)}, u32[]{:S(2)}, u32[]{:S(2)}) collective-permute-start(f32[256,128]{1,0:T(8,128)S(1)} %get-tuple-element.26), channel_id=1, source_target_pairs={{0,1},{1,0},{2,3},{3,2},{4,5},{5,4},{6,7},{7,6},{8,9},{9,8},{10,11... | collective-permute-start | bytes 393224 | tf_op jit(solution)/shard_map/ppermute | solution.py:241
  97.4 0.0 copy-done.1
  97.4 0.0 copy-done.2
  97.4 0.1 convert_multiply_fusion
  97.6 0.8 collective-permute-done.8
  98.4 1.3 %shard_map.93 = (bf16[4,4,2,16,128]{4,3,2,1,0:T(8,128)(2,1)}, bf16[4,4,2,16,128]{4,3,2,1,0:T(8,128)(2,1)}) custom-call(s32[5]{0:T(128)S(1)} %stack.23.place, f32[4,4,16,128]{3,2,1,0:T(8,128)S(1)} %bitcast.23, f32[4,4,16,128]{3,2,1,0:T(8,128)S(1)} %bitcast.24, f32[4,4,2,16,128]{4,3,2,1,0:T(8,128)S(1)} %bitcast.21, f32[4,4,2,16,128]{4,3,2,1,0:T(8,128)S(1)} %bitcast.20), custom_call_target="tpu_custom_call" | custom-call | tf_op jit(solution)/shard_map/pallas_call | solution.py:250
  (5 shorter events, 0.1 us)
Async XLA Ops:
  3.3 34.6 %all-to-all-start = ((bf16[128,2,1024]{2,1,0:T(2,128)(2,1)}), bf16[128,2,1024]{2,1,0:T(2,128)(2,1)S(1)}, u32[]{:S(2)}, u32[]{:S(2)}) async-start(bf16[128,2,1024]{2,1,0:T(2,128)(2,1)} %bitcast.26), calls=%async_computation | async-start | bytes 1048576 | tf_op jit(solution)/shard_map/all_to_all | solution.py:174
  21.3 41.1 %collective-permute-start.3 = (bf16[1024,896]{1,0:T(8,128)(2,1)}, bf16[1024,896]{1,0:T(8,128)(2,1)S(1)}, u32[]{:S(2)}, u32[]{:S(2)}) collective-permute-start(bf16[1024,896]{1,0:T(8,128)(2,1)} %bitcast.18), channel_id=1, source_target_pairs={{0,1},{1,0},{2,3},{3,2},{4,5},{5,4},{6,7},{7,6},{8,9},{9,8},{10,11... | collective-permute-start | bytes 5505032 | tf_op jit(solution)/shard_map/ppermute | solution.py:182
  38.0 24.4 %copy-start = (bf16[1,1,1024,896]{3,2,1,0:T(8,128)(2,1)S(1)}, bf16[1,1,1024,896]{3,2,1,0:T(8,128)(2,1)}, u32[]{:S(2)}) copy-start(bf16[1,1,1024,896]{3,2,1,0:T(8,128)(2,1)} %param.11) | copy-start | bytes 5505028
  39.8 23.5 %collective-permute-start.2 = (bf16[64,1792]{1,0:T(8,128)(2,1)S(1)}, bf16[64,1792]{1,0:T(8,128)(2,1)S(1)}, u32[]{:S(2)}, u32[]{:S(2)}) collective-permute-start(bf16[64,1792]{1,0:T(8,128)(2,1)S(1)} %get-tuple-element.17), channel_id=1, source_target_pairs={{0,16},{8,24},{16,0},{24,8},{1,17},{9,25},{17,1},{25,9},{2,18},{10... | collective-permute-start | bytes 688136 | tf_op jit(solution)/shard_map/ppermute | solution.py:199
  54.6 17.2 %collective-permute-start = (bf16[64,1792]{1,0:T(8,128)(2,1)S(1)}, bf16[64,1792]{1,0:T(8,128)(2,1)S(1)}, u32[]{:S(2)}, u32[]{:S(2)}) collective-permute-start(bf16[64,1792]{1,0:T(8,128)(2,1)S(1)} %get-tuple-element.15), channel_id=1, source_target_pairs={{0,8},{8,16},{16,24},{24,0},{1,9},{9,17},{17,25},{25,1},{2,10},{10... | collective-permute-start | bytes 688136 | tf_op jit(solution)/shard_map/ppermute | solution.py:199
  60.5 15.9 %collective-permute-start.1 = (bf16[64,1792]{1,0:T(8,128)(2,1)S(1)}, bf16[64,1792]{1,0:T(8,128)(2,1)S(1)}, u32[]{:S(2)}, u32[]{:S(2)}) collective-permute-start(bf16[64,1792]{1,0:T(8,128)(2,1)S(1)} %get-tuple-element.16), channel_id=1, source_target_pairs={{0,24},{8,0},{16,8},{24,16},{1,25},{9,1},{17,9},{25,17},{2,26},{10... | collective-permute-start | bytes 688136 | tf_op jit(solution)/shard_map/ppermute | solution.py:199
  64.0 15.7 %collective-permute-start.4 = (bf16[128,512]{1,0:T(8,128)(2,1)S(1)}, bf16[128,512]{1,0:T(8,128)(2,1)S(1)}, u32[]{:S(2)}, u32[]{:S(2)}) collective-permute-start(bf16[128,512]{1,0:T(8,128)(2,1)S(1)} %shard_map.89), channel_id=1, source_target_pairs={{0,2},{2,0},{1,3},{3,1},{4,6},{6,4},{5,7},{7,5},{8,10},{10,8},{9,1... | collective-permute-start | bytes 393224 | tf_op jit(solution)/shard_map/ppermute | solution.py:224
  77.1 6.0 %collective-permute-start.6 = (bf16[128,512]{1,0:T(8,128)(2,1)S(1)}, bf16[128,512]{1,0:T(8,128)(2,1)S(1)}, u32[]{:S(2)}, u32[]{:S(2)}) collective-permute-start(bf16[128,512]{1,0:T(8,128)(2,1)S(1)} %shard_map.90), channel_id=1, source_target_pairs={{0,4},{4,0},{1,5},{5,1},{2,6},{6,2},{3,7},{7,3},{8,12},{12,8},{9,1... | collective-permute-start | bytes 393224 | tf_op jit(solution)/shard_map/ppermute | solution.py:229
  79.7 17.7 %copy-start.1 = (bf16[1,1,32,16,128]{4,3,2,1,0:T(8,128)(2,1)S(1)}, bf16[1,1,32,16,128]{4,3,2,1,0:T(8,128)(2,1)}, u32[]{:S(2)}) copy-start(bf16[1,1,32,16,128]{4,3,2,1,0:T(8,128)(2,1)} %param.12) | copy-start | bytes 393220
  79.8 17.7 %copy-start.2 = (bf16[1,1,32,16,128]{4,3,2,1,0:T(8,128)(2,1)S(1)}, bf16[1,1,32,16,128]{4,3,2,1,0:T(8,128)(2,1)}, u32[]{:S(2)}) copy-start(bf16[1,1,32,16,128]{4,3,2,1,0:T(8,128)(2,1)} %param.13) | copy-start | bytes 393220
  83.1 8.9 %collective-permute-start.7 = (bf16[128,256]{1,0:T(8,128)(2,1)S(1)}, bf16[128,256]{1,0:T(8,128)(2,1)S(1)}, u32[]{:S(2)}, u32[]{:S(2)}) collective-permute-start(bf16[128,256]{1,0:T(8,128)(2,1)S(1)} %fusion.7), channel_id=1, source_target_pairs={{0,2},{2,0},{1,3},{3,1},{4,6},{6,4},{5,7},{7,5},{8,10},{10,8},{9,1... | collective-permute-start | bytes 196616 | tf_op jit(solution)/shard_map/ppermute | solution.py:237
  87.2 5.0 %collective-permute-start.5 = (bf16[128,256]{1,0:T(8,128)(2,1)S(1)}, bf16[128,256]{1,0:T(8,128)(2,1)S(1)}, u32[]{:S(2)}, u32[]{:S(2)}) collective-permute-start(bf16[128,256]{1,0:T(8,128)(2,1)S(1)} %fusion.9), channel_id=1, source_target_pairs={{0,4},{4,0},{1,5},{5,1},{2,6},{6,2},{3,7},{7,3},{8,12},{12,8},{9,1... | collective-permute-start | bytes 196616 | tf_op jit(solution)/shard_map/ppermute | solution.py:233
  92.3 6.1 %collective-permute-start.8 = (f32[256,128]{1,0:T(8,128)S(1)}, f32[256,128]{1,0:T(8,128)S(1)}, u32[]{:S(2)}, u32[]{:S(2)}) collective-permute-start(f32[256,128]{1,0:T(8,128)S(1)} %get-tuple-element.26), channel_id=1, source_target_pairs={{0,1},{1,0},{2,3},{3,2},{4,5},{5,4},{6,7},{7,6},{8,9},{9,8},{10,11... | collective-permute-start | bytes 393224 | tf_op jit(solution)/shard_map/ppermute | solution.py:241

commit v5 on v4

--- a/solution.py
+++ b/solution.py
@@ -73,15 +73,15 @@
 
 
 def choose(place, rows, *outs_and_scratch):
-    outs, (held, tables) = outs_and_scratch[:4], outs_and_scratch[4:]
+    outs, tables = outs_and_scratch[:4], outs_and_scratch[4]
     zhi, node = place[0], place[4]
     total, span = rows.shape[0], rows.shape[1] // 2
     cols = outs[0].shape[1] // 2
-    slots = held.shape[1]
-    wide = 4 * slots
-    f32, bf16 = jnp.float32, jnp.bfloat16
-    lane = lax.broadcasted_iota(jnp.int32, (8, total), 1)
-    line = lax.broadcasted_iota(jnp.int32, (8, total), 0)
+    wide = outs[0].shape[0]
+    slots = wide // 4
+    f32, bf16, i32 = jnp.float32, jnp.bfloat16, jnp.int32
+    lane = lax.broadcasted_iota(i32, (8, total), 1)
+    line = lax.broadcasted_iota(i32, (8, total), 0)
     own = (lane == node * 4 + line).astype(bf16)
     first = jnp.dot(own, rows[:, cols:span], preferred_element_type=f32)
     second = jnp.dot(own, rows[:, span + cols :], preferred_element_type=f32)
@@ -91,23 +91,26 @@
             tables[part : part + 1, gate * wide : (gate + 1) * wide] = parts[part][
                 gate : gate + 1
             ]
-    at = lax.broadcasted_iota(jnp.int32, (total, 4 * wide), 0)
-    gate = lax.broadcasted_iota(jnp.int32, (1, 4 * wide), 1) // wide
-    match = at == tables[0:1, :].astype(jnp.int32) * 4 + gate
+    to = lax.broadcasted_iota(i32, (1, 4 * wide), 1)
+    step = jnp.zeros((1, 4 * wide), i32)
+    for index, value in enumerate(STEPS):
+        step = jnp.where(to // wide == index, value, step)
+    gate = (to % wide) // slots
+    source = gate * wide + ((zhi + step) % 4) * slots + to % slots
+    move = (lax.broadcasted_iota(i32, (4 * wide, 4 * wide), 0) == source).astype(bf16)
+    table = jnp.dot(tables[...].astype(bf16), move, preferred_element_type=f32)
+    at = lax.broadcasted_iota(i32, (total, 4 * wide), 0)
+    match = at == table[0:1, :].astype(i32) * 4 + gate
     pickers = [
-        jnp.where(match, tables[part : part + 1, :], 0.0).astype(bf16) for part in range(1, 4)
+        jnp.where(match, table[part : part + 1, :], 0.0).astype(bf16) for part in range(1, 4)
     ]
     dims = (((0,), (0,)), ((), ()))
     for side in range(2):
         block = rows[:, side * span : side * span + cols]
         value = sum(lax.dot_general(p, block, dims, preferred_element_type=f32) for p in pickers)
-        held[:, :, side * cols : (side + 1) * cols] = value.astype(bf16).reshape(
-            held.shape[0], slots, cols
-        )
-    for out, step in zip(outs, STEPS):
-        expert = lax.rem(zhi + step, 4)
-        for gate_at in range(4):
-            out[gate_at * slots : (gate_at + 1) * slots, :] = held[gate_at * 4 + expert]
+        value = value.astype(bf16)
+        for index, out in enumerate(outs):
+            out[:, side * cols : (side + 1) * cols] = value[index * wide : (index + 1) * wide]
 
 
 def arrange(place, w_own, w_sib, blocks):
@@ -132,14 +135,23 @@
         out[:, index * size : (index + 1) * size] = value.astype(out.dtype)
 
 
-def finish(place, keep, got, gate_factor, up_factor, grad_gate, grad_up):
+def finish(place, keep, got, gate_factor, up_factor, grad_gate, grad_up, built, leaving):
     zhi, core = place[0], place[1]
+    copies = []
     for piece, step in enumerate(STEPS):
         at = lax.rem(zhi + 4 - step, 4)
         for rows, whose in ((keep, core), (got, 1 - core)):
             value = rows[piece]
-            grad_gate[at, :, whose] = (value * gate_factor[at, :, whose]).astype(grad_gate.dtype)
-            grad_up[at, :, whose] = (value * up_factor[at, :, whose]).astype(grad_up.dtype)
+            built[0, piece, :, whose] = (value * gate_factor[at, :, whose]).astype(built.dtype)
+            built[1, piece, :, whose] = (value * up_factor[at, :, whose]).astype(built.dtype)
+        for index, out in enumerate((grad_gate, grad_up)):
+            copy = pltpu.make_async_copy(
+                built.at[index, piece], out.at[at], leaving.at[index, piece]
+            )
+            copy.start()
+            copies.append(copy)
+    for copy in copies:
+        copy.wait()
 
 
 def on_device(grad_out, cross_rows, slot_rows, route_prob, w_down, gate_pre, up_pre):
@@ -187,7 +199,6 @@
         in_specs=[SMEM, VMEM],
         out_specs=[VMEM] * 4,
         scratch_shapes=[
-            pltpu.VMEM((4 * experts, slots, 2 * cols), bf16),
             pltpu.VMEM((4, 4 * experts * slots), f32),
         ],
         compiler_params=pltpu.CompilerParams(vmem_limit_bytes=12 << 20),
@@ -251,7 +262,8 @@
         finish,
         out_shape=[jax.ShapeDtypeStruct(deep, bf16)] * 2,
         in_specs=[SMEM] + [VMEM] * 4,
-        out_specs=[VMEM] * 2,
+        out_specs=[pl.BlockSpec(memory_space=pl.ANY)] * 2,
+        scratch_shapes=[pltpu.VMEM((2,) + deep, bf16), pltpu.SemaphoreType.DMA((2, 4))],
         compiler_params=pltpu.CompilerParams(vmem_limit_bytes=8 << 20),
     )(
         place,

time: 100 us -> 100 us (level)
  no operation moved by 1% of the time
where the time goes in v5:
time: 100 us; the launch traced here: 99.9 us
  starting transfers between devices  62.4 us (62%)
  waiting for transfers between devices  26.6 us (27%)
  Pallas kernels  9.51 us (10%)
    ppermute x3, starting transfers between devices, on_device(): pieces.append(lax.ppermute(out, 'zhi', pairs))  22.6 us
    all_to_all x1, starting transfers between devices, on_device(): lax.all_to_all(outgoing, ('y', 'xlo', 'zlo', 'xhi'), split_axis=0, concat...  18 us
    all_to_all x1, waiting for transfers between devices, on_device(): lax.all_to_all(outgoing, ('y', 'xlo', 'zlo', 'xhi'), split_axis=0, concat...  12.2 us
    ppermute x3, waiting for transfers between devices, on_device(): pieces.append(lax.ppermute(out, 'zhi', pairs))  8.03 us
    ppermute x1, starting transfers between devices, on_device(): got = lax.ppermute(give, 'core', SWAP)  4.77 us
    ppermute x1, starting transfers between devices, on_device(): got_a = lax.ppermute(give_a, 'xhi', SWAP)  4.31 us
    ppermute x1, starting transfers between devices, on_device(): w_sib = lax.ppermute(w_own, 'core', SWAP)  4.27 us
    ppermute x1, starting transfers between devices, on_device(): got_b = lax.ppermute(give_b, 'xhi', SWAP)  4.22 us
  transfers between devices with their start and end apart: 10, of which 7 were waited for; matrix products, arithmetic and copies ran while one was open for 0% of the time, Pallas kernels for 5%

profile of v5, /device:TPU:1, one launch (start us, length us, event | category | flops | bytes accessed | tf_op | source)
XLA Modules:
  0.0 99.9 jit_solution(13793911121907291210)
XLA Ops:
  0.6 2.7 %shard_map.86 = bf16[32,4,2,1024]{3,2,1,0:T(2,128)(2,1)} custom-call(s32[1,32]{1,0:T(1,128)} %bitcast.29, s32[4,16]{1,0:T(4,128)} %bitcast.27, f32[4,16]{1,0:T(4,128)} %bitcast.28, bf16[8,7168]{1,0:T(8,128)(2,1)} %tokens_in.1), custom_call_target="tpu_custom_call" | custom-call | tf_op jit(solution)/shard_map/pallas_call | solution.py:171
  3.3 18.0 %all-to-all-start = ((bf16[128,2,1024]{2,1,0:T(2,128)(2,1)}), bf16[128,2,1024]{2,1,0:T(2,128)(2,1)S(1)}, u32[]{:S(2)}, u32[]{:S(2)}) async-start(bf16[128,2,1024]{2,1,0:T(2,128)(2,1)} %bitcast.26), calls=%async_computation | async-start | bytes 1048576 | tf_op jit(solution)/shard_map/all_to_all | solution.py:186
  21.3 4.3 %collective-permute-start.3 = (bf16[1024,896]{1,0:T(8,128)(2,1)}, bf16[1024,896]{1,0:T(8,128)(2,1)S(1)}, u32[]{:S(2)}, u32[]{:S(2)}) collective-permute-start(bf16[1024,896]{1,0:T(8,128)(2,1)} %bitcast.18), channel_id=1, source_target_pairs={{0,1},{1,0},{2,3},{3,2},{4,5},{5,4},{6,7},{7,6},{8,9},{9,8},{10,11... | collective-permute-start | bytes 5505032 | tf_op jit(solution)/shard_map/ppermute | solution.py:194
  25.6 0.1 stack.23.place
  25.7 12.2 %all-to-all-done = bf16[128,2,1024]{2,1,0:T(2,128)(2,1)S(1)} async-done(((bf16[128,2,1024]{2,1,0:T(2,128)(2,1)}), bf16[128,2,1024]{2,1,0:T(2,128)(2,1)S(1)}, u32[]{:S(2)}, u32[]{:S(2)}) %all-to-all-start) | async-done | bytes 524320 | tf_op jit(solution)/shard_map/all_to_all | solution.py:186
  37.9 0.1 copy.9
  38.0 0.0 copy-start
  38.0 1.8 %shard_map.87 = (bf16[64,1792]{1,0:T(8,128)(2,1)S(1)}, bf16[64,1792]{1,0:T(8,128)(2,1)S(1)}, bf16[64,1792]{1,0:T(8,128)(2,1)S(1)}, bf16[64,1792]{1,0:T(8,128)(2,1)S(1)}) custom-call(s32[5]{0:T(128)S(1)} %stack.23.place, bf16[128,2048]{1,0:T(8,128)(2,1)S(1)} %bitcast.22), custom_call_target="tpu_custom_call" | custom-call | flops 21474836480 | bytes 2097152 | tf_op jit(solution)/shard_map/pallas_call | solution.py:196
  39.8 14.8 %collective-permute-start.2 = (bf16[64,1792]{1,0:T(8,128)(2,1)S(1)}, bf16[64,1792]{1,0:T(8,128)(2,1)S(1)}, u32[]{:S(2)}, u32[]{:S(2)}) collective-permute-start(bf16[64,1792]{1,0:T(8,128)(2,1)S(1)} %get-tuple-element.17), channel_id=1, source_target_pairs={{0,16},{8,24},{16,0},{24,8},{1,17},{9,25},{17,1},{25,9},{2,18},{10... | collective-permute-start | bytes 688136 | tf_op jit(solution)/shard_map/ppermute | solution.py:210
  54.7 5.8 %collective-permute-start = (bf16[64,1792]{1,0:T(8,128)(2,1)S(1)}, bf16[64,1792]{1,0:T(8,128)(2,1)S(1)}, u32[]{:S(2)}, u32[]{:S(2)}) collective-permute-start(bf16[64,1792]{1,0:T(8,128)(2,1)S(1)} %get-tuple-element.15), channel_id=1, source_target_pairs={{0,8},{8,16},{16,24},{24,0},{1,9},{9,17},{17,25},{25,1},{2,10},{10... | collective-permute-start | bytes 688136 | tf_op jit(solution)/shard_map/ppermute | solution.py:210
  60.5 1.9 %collective-permute-start.1 = (bf16[64,1792]{1,0:T(8,128)(2,1)S(1)}, bf16[64,1792]{1,0:T(8,128)(2,1)S(1)}, u32[]{:S(2)}, u32[]{:S(2)}) collective-permute-start(bf16[64,1792]{1,0:T(8,128)(2,1)S(1)} %get-tuple-element.16), channel_id=1, source_target_pairs={{0,24},{8,0},{16,8},{24,16},{1,25},{9,1},{17,9},{25,17},{2,26},{10... | collective-permute-start | bytes 688136 | tf_op jit(solution)/shard_map/ppermute | solution.py:210
  62.5 0.0 collective-permute-done.3.w_sib
  62.5 0.0 copy-done
  62.5 0.8 shard_map.88.refs_2_
  63.3 0.0 collective-permute-done.2.refs_1_
  63.3 0.7 shard_map.89
  64.0 4.3 %collective-permute-start.4 = (bf16[128,512]{1,0:T(8,128)(2,1)S(1)}, bf16[128,512]{1,0:T(8,128)(2,1)S(1)}, u32[]{:S(2)}, u32[]{:S(2)}) collective-permute-start(bf16[128,512]{1,0:T(8,128)(2,1)S(1)} %shard_map.89), channel_id=1, source_target_pairs={{0,2},{2,0},{1,3},{3,1},{4,6},{6,4},{5,7},{7,5},{8,10},{10,8},{9,1... | collective-permute-start | bytes 393224 | tf_op jit(solution)/shard_map/ppermute | solution.py:235
  68.4 3.6 %collective-permute-done.refs_0_ = bf16[64,1792]{1,0:T(8,128)(2,1)S(1)} collective-permute-done((bf16[64,1792]{1,0:T(8,128)(2,1)S(1)}, bf16[64,1792]{1,0:T(8,128)(2,1)S(1)}, u32[]{:S(2)}, u32[]{:S(2)}) %collective-permute-start) | collective-permute-done | bytes 229408 | tf_op jit(solution)/shard_map/ppermute | solution.py:210
  72.0 4.4 %collective-permute-done.1.refs_1_ = bf16[64,1792]{1,0:T(8,128)(2,1)S(1)} collective-permute-done((bf16[64,1792]{1,0:T(8,128)(2,1)S(1)}, bf16[64,1792]{1,0:T(8,128)(2,1)S(1)}, u32[]{:S(2)}, u32[]{:S(2)}) %collective-permute-start.1) | collective-permute-done | bytes 229408 | tf_op jit(solution)/shard_map/ppermute | solution.py:210
  76.4 0.7 shard_map.90
  77.1 1.9 %collective-permute-start.6 = (bf16[128,512]{1,0:T(8,128)(2,1)S(1)}, bf16[128,512]{1,0:T(8,128)(2,1)S(1)}, u32[]{:S(2)}, u32[]{:S(2)}) collective-permute-start(bf16[128,512]{1,0:T(8,128)(2,1)S(1)} %shard_map.90), channel_id=1, source_target_pairs={{0,4},{4,0},{1,5},{5,1},{2,6},{6,2},{3,7},{7,3},{8,12},{12,8},{9,1... | collective-permute-start | bytes 393224 | tf_op jit(solution)/shard_map/ppermute | solution.py:240
  79.0 0.7 shard_map.91
  79.8 0.0 collective-permute-done.4
  79.8 0.0 copy-start.1
  79.8 0.0 copy-start.2
  79.8 0.7 shard_map.92
  80.5 2.6 %collective-permute-done.6 = bf16[128,512]{1,0:T(8,128)(2,1)S(1)} collective-permute-done((bf16[128,512]{1,0:T(8,128)(2,1)S(1)}, bf16[128,512]{1,0:T(8,128)(2,1)S(1)}, u32[]{:S(2)}, u32[]{:S(2)}) %collective-permute-start.6) | collective-permute-done | bytes 131104 | tf_op jit(solution)/shard_map/ppermute | solution.py:240
  83.2 4.2 %collective-permute-start.7 = (bf16[128,256]{1,0:T(8,128)(2,1)S(1)}, bf16[128,256]{1,0:T(8,128)(2,1)S(1)}, u32[]{:S(2)}, u32[]{:S(2)}) collective-permute-start(bf16[128,256]{1,0:T(8,128)(2,1)S(1)} %fusion.7), channel_id=1, source_target_pairs={{0,2},{2,0},{1,3},{3,1},{4,6},{6,4},{5,7},{7,5},{8,10},{10,8},{9,1... | collective-permute-start | bytes 196616 | tf_op jit(solution)/shard_map/ppermute | solution.py:248
  87.4 2.4 %collective-permute-start.5 = (bf16[128,256]{1,0:T(8,128)(2,1)S(1)}, bf16[128,256]{1,0:T(8,128)(2,1)S(1)}, u32[]{:S(2)}, u32[]{:S(2)}) collective-permute-start(bf16[128,256]{1,0:T(8,128)(2,1)S(1)} %fusion.9), channel_id=1, source_target_pairs={{0,4},{4,0},{1,5},{5,1},{2,6},{6,2},{3,7},{7,3},{8,12},{12,8},{9,1... | collective-permute-start | bytes 196616 | tf_op jit(solution)/shard_map/ppermute | solution.py:244
  89.8 2.3 %collective-permute-done.7 = bf16[128,256]{1,0:T(8,128)(2,1)S(1)} collective-permute-done((bf16[128,256]{1,0:T(8,128)(2,1)S(1)}, bf16[128,256]{1,0:T(8,128)(2,1)S(1)}, u32[]{:S(2)}, u32[]{:S(2)}) %collective-permute-start.7) | collective-permute-done | bytes 65568 | tf_op jit(solution)/shard_map/ppermute | solution.py:248
  92.1 0.6 collective-permute-done.5
  92.8 4.8 %collective-permute-start.8 = (f32[256,128]{1,0:T(8,128)S(1)}, f32[256,128]{1,0:T(8,128)S(1)}, u32[]{:S(2)}, u32[]{:S(2)}) collective-permute-start(f32[256,128]{1,0:T(8,128)S(1)} %get-tuple-element.26), channel_id=1, source_target_pairs={{0,1},{1,0},{2,3},{3,2},{4,5},{5,4},{6,7},{7,6},{8,9},{9,8},{10,11... | collective-permute-start | bytes 393224 | tf_op jit(solution)/shard_map/ppermute | solution.py:252
  97.5 0.0 copy-done.1
  97.5 0.0 copy-done.2
  97.6 0.1 convert_multiply_fusion
  97.7 0.8 collective-permute-done.8
  98.5 1.4 %shard_map.93 = (bf16[4,4,2,16,128]{4,3,2,1,0:T(8,128)(2,1)}, bf16[4,4,2,16,128]{4,3,2,1,0:T(8,128)(2,1)}) custom-call(s32[5]{0:T(128)S(1)} %stack.23.place, f32[4,4,16,128]{3,2,1,0:T(8,128)S(1)} %bitcast.23, f32[4,4,16,128]{3,2,1,0:T(8,128)S(1)} %bitcast.24, f32[4,4,2,16,128]{4,3,2,1,0:T(8,128)S(1)} %bitcast.21, f32[4,4,2,16,128]{4,3,2,1,0:T(8,128)S(1)} %bitcast.20), custom_call_target="tpu_custom_call" | custom-call | tf_op jit(solution)/shard_map/pallas_call | solution.py:261
  (5 shorter events, 0.1 us)
Async XLA Ops:
  3.3 34.6 %all-to-all-start = ((bf16[128,2,1024]{2,1,0:T(2,128)(2,1)}), bf16[128,2,1024]{2,1,0:T(2,128)(2,1)S(1)}, u32[]{:S(2)}, u32[]{:S(2)}) async-start(bf16[128,2,1024]{2,1,0:T(2,128)(2,1)} %bitcast.26), calls=%async_computation | async-start | bytes 1048576 | tf_op jit(solution)/shard_map/all_to_all | solution.py:186
  21.3 41.2 %collective-permute-start.3 = (bf16[1024,896]{1,0:T(8,128)(2,1)}, bf16[1024,896]{1,0:T(8,128)(2,1)S(1)}, u32[]{:S(2)}, u32[]{:S(2)}) collective-permute-start(bf16[1024,896]{1,0:T(8,128)(2,1)} %bitcast.18), channel_id=1, source_target_pairs={{0,1},{1,0},{2,3},{3,2},{4,5},{5,4},{6,7},{7,6},{8,9},{9,8},{10,11... | collective-permute-start | bytes 5505032 | tf_op jit(solution)/shard_map/ppermute | solution.py:194
  38.0 24.4 %copy-start = (bf16[1,1,1024,896]{3,2,1,0:T(8,128)(2,1)S(1)}, bf16[1,1,1024,896]{3,2,1,0:T(8,128)(2,1)}, u32[]{:S(2)}) copy-start(bf16[1,1,1024,896]{3,2,1,0:T(8,128)(2,1)} %param.11) | copy-start | bytes 5505028
  39.8 23.5 %collective-permute-start.2 = (bf16[64,1792]{1,0:T(8,128)(2,1)S(1)}, bf16[64,1792]{1,0:T(8,128)(2,1)S(1)}, u32[]{:S(2)}, u32[]{:S(2)}) collective-permute-start(bf16[64,1792]{1,0:T(8,128)(2,1)S(1)} %get-tuple-element.17), channel_id=1, source_target_pairs={{0,16},{8,24},{16,0},{24,8},{1,17},{9,25},{17,1},{25,9},{2,18},{10... | collective-permute-start | bytes 688136 | tf_op jit(solution)/shard_map/ppermute | solution.py:210
  54.7 17.3 %collective-permute-start = (bf16[64,1792]{1,0:T(8,128)(2,1)S(1)}, bf16[64,1792]{1,0:T(8,128)(2,1)S(1)}, u32[]{:S(2)}, u32[]{:S(2)}) collective-permute-start(bf16[64,1792]{1,0:T(8,128)(2,1)S(1)} %get-tuple-element.15), channel_id=1, source_target_pairs={{0,8},{8,16},{16,24},{24,0},{1,9},{9,17},{17,25},{25,1},{2,10},{10... | collective-permute-start | bytes 688136 | tf_op jit(solution)/shard_map/ppermute | solution.py:210
  60.5 15.9 %collective-permute-start.1 = (bf16[64,1792]{1,0:T(8,128)(2,1)S(1)}, bf16[64,1792]{1,0:T(8,128)(2,1)S(1)}, u32[]{:S(2)}, u32[]{:S(2)}) collective-permute-start(bf16[64,1792]{1,0:T(8,128)(2,1)S(1)} %get-tuple-element.16), channel_id=1, source_target_pairs={{0,24},{8,0},{16,8},{24,16},{1,25},{9,1},{17,9},{25,17},{2,26},{10... | collective-permute-start | bytes 688136 | tf_op jit(solution)/shard_map/ppermute | solution.py:210
  64.0 15.7 %collective-permute-start.4 = (bf16[128,512]{1,0:T(8,128)(2,1)S(1)}, bf16[128,512]{1,0:T(8,128)(2,1)S(1)}, u32[]{:S(2)}, u32[]{:S(2)}) collective-permute-start(bf16[128,512]{1,0:T(8,128)(2,1)S(1)} %shard_map.89), channel_id=1, source_target_pairs={{0,2},{2,0},{1,3},{3,1},{4,6},{6,4},{5,7},{7,5},{8,10},{10,8},{9,1... | collective-permute-start | bytes 393224 | tf_op jit(solution)/shard_map/ppermute | solution.py:235
  77.1 6.0 %collective-permute-start.6 = (bf16[128,512]{1,0:T(8,128)(2,1)S(1)}, bf16[128,512]{1,0:T(8,128)(2,1)S(1)}, u32[]{:S(2)}, u32[]{:S(2)}) collective-permute-start(bf16[128,512]{1,0:T(8,128)(2,1)S(1)} %shard_map.90), channel_id=1, source_target_pairs={{0,4},{4,0},{1,5},{5,1},{2,6},{6,2},{3,7},{7,3},{8,12},{12,8},{9,1... | collective-permute-start | bytes 393224 | tf_op jit(solution)/shard_map/ppermute | solution.py:240
  79.8 17.7 %copy-start.1 = (bf16[1,1,32,16,128]{4,3,2,1,0:T(8,128)(2,1)S(1)}, bf16[1,1,32,16,128]{4,3,2,1,0:T(8,128)(2,1)}, u32[]{:S(2)}) copy-start(bf16[1,1,32,16,128]{4,3,2,1,0:T(8,128)(2,1)} %param.12) | copy-start | bytes 393220
  79.8 17.7 %copy-start.2 = (bf16[1,1,32,16,128]{4,3,2,1,0:T(8,128)(2,1)S(1)}, bf16[1,1,32,16,128]{4,3,2,1,0:T(8,128)(2,1)}, u32[]{:S(2)}) copy-start(bf16[1,1,32,16,128]{4,3,2,1,0:T(8,128)(2,1)} %param.13) | copy-start | bytes 393220
  83.2 8.9 %collective-permute-start.7 = (bf16[128,256]{1,0:T(8,128)(2,1)S(1)}, bf16[128,256]{1,0:T(8,128)(2,1)S(1)}, u32[]{:S(2)}, u32[]{:S(2)}) collective-permute-start(bf16[128,256]{1,0:T(8,128)(2,1)S(1)} %fusion.7), channel_id=1, source_target_pairs={{0,2},{2,0},{1,3},{3,1},{4,6},{6,4},{5,7},{7,5},{8,10},{10,8},{9,1... | collective-permute-start | bytes 196616 | tf_op jit(solution)/shard_map/ppermute | solution.py:248
  87.4 5.3 %collective-permute-start.5 = (bf16[128,256]{1,0:T(8,128)(2,1)S(1)}, bf16[128,256]{1,0:T(8,128)(2,1)S(1)}, u32[]{:S(2)}, u32[]{:S(2)}) collective-permute-start(bf16[128,256]{1,0:T(8,128)(2,1)S(1)} %fusion.9), channel_id=1, source_target_pairs={{0,4},{4,0},{1,5},{5,1},{2,6},{6,2},{3,7},{7,3},{8,12},{12,8},{9,1... | collective-permute-start | bytes 196616 | tf_op jit(solution)/shard_map/ppermute | solution.py:244
  92.8 5.7 %collective-permute-start.8 = (f32[256,128]{1,0:T(8,128)S(1)}, f32[256,128]{1,0:T(8,128)S(1)}, u32[]{:S(2)}, u32[]{:S(2)}) collective-permute-start(f32[256,128]{1,0:T(8,128)S(1)} %get-tuple-element.26), channel_id=1, source_target_pairs={{0,1},{1,0},{2,3},{3,2},{4,5},{5,4},{6,7},{7,6},{8,9},{9,8},{10,11... | collective-permute-start | bytes 393224 | tf_op jit(solution)/shard_map/ppermute | solution.py:252

commit v6 on v4

--- a/solution.py
+++ b/solution.py
@@ -48,23 +48,26 @@
         ).astype(bf16)
         for side in range(2)
     ]
-    at = lax.broadcasted_iota(jnp.int32, (count, groups), 0)
-    picker = (crossing[...] == at).astype(bf16)
+    half = lax.broadcasted_iota(jnp.int32, (groups, 2 * groups), 1) // 2
+    twice = (half == lax.broadcasted_iota(jnp.int32, (groups, 2 * groups), 0)).astype(bf16)
+    token = jnp.dot(crossing[...].astype(bf16), twice, preferred_element_type=f32)
+    side = lax.broadcasted_iota(jnp.int32, (1, 2 * groups), 1) % 2
+    at = lax.broadcasted_iota(jnp.int32, (2 * count, 2 * groups), 0)
+    picker = (at == side * count + token.astype(jnp.int32)).astype(bf16)
+    odd = lax.broadcasted_iota(jnp.int32, (2 * groups, behind), 0) % 2 == 1
+    tail = jnp.where(odd, table[1].astype(f32), table[0].astype(f32)).astype(bf16)
     copies[3].wait()
     out_copies = []
     for pair in range(4):
-        sides = []
-        for side in range(2):
-            start = (2 * pair + side) * cols
-            value = lax.dot_general(
-                picker,
-                tokens[:, start : start + cols],
-                (((0,), (0,)), ((), ())),
-                preferred_element_type=f32,
-            )
-            behind_it = jnp.broadcast_to(table[side], (groups, behind))
-            sides.append(jnp.concatenate([value.astype(bf16), behind_it], 1)[:, None, :])
-        built[pair] = jnp.concatenate(sides, 1)
+        start = 2 * pair * cols
+        both = jnp.concatenate(
+            [tokens[:, start : start + cols], tokens[:, start + cols : start + 2 * cols]], 0
+        )
+        value = lax.dot_general(
+            picker, both, (((0,), (0,)), ((), ())), preferred_element_type=f32
+        )
+        rows = jnp.concatenate([value.astype(bf16), tail], 1)
+        built[pair] = rows.reshape(groups, 2, cols + behind)
         copy = pltpu.make_async_copy(built.at[pair], packed.at[:, pair], leaving.at[pair])
         copy.start()
         out_copies.append(copy)

time: 100 us -> 99.5 us (level)
  transfers between devices with their start and end apart: 10 -> 10, of which waited for: 7 -> 6; matrix products, arithmetic and copies ran while one was open for 0% -> 0% of each run, Pallas kernels for 5% -> 5%
where the time goes in v6:
time: 99.5 us; the launch traced here: 99 us
  starting transfers between devices  63.1 us (63%)
  waiting for transfers between devices  25.9 us (26%)
  Pallas kernels  8.73 us (9%)
    ppermute x3, starting transfers between devices, on_device(): pieces.append(lax.ppermute(out, 'zhi', pairs))  22.6 us
    all_to_all x1, starting transfers between devices, on_device(): lax.all_to_all(outgoing, ('y', 'xlo', 'zlo', 'xhi'), split_axis=0, concat...  18 us
    all_to_all x1, waiting for transfers between devices, on_device(): lax.all_to_all(outgoing, ('y', 'xlo', 'zlo', 'xhi'), split_axis=0, concat...  12.2 us
    ppermute x3, waiting for transfers between devices, on_device(): pieces.append(lax.ppermute(out, 'zhi', pairs))  8 us
    ppermute x1, starting transfers between devices, on_device(): got = lax.ppermute(give, 'core', SWAP)  5.3 us
    ppermute x1, starting transfers between devices, on_device(): got_a = lax.ppermute(give_a, 'xhi', SWAP)  4.32 us
    ppermute x1, starting transfers between devices, on_device(): w_sib = lax.ppermute(w_own, 'core', SWAP)  4.26 us
    ppermute x1, starting transfers between devices, on_device(): got_b = lax.ppermute(give_b, 'xhi', SWAP)  3.8 us
  transfers between devices with their start and end apart: 10, of which 6 were waited for; matrix products, arithmetic and copies ran while one was open for 0% of the time, Pallas kernels for 5%

profile of v6, /device:TPU:1, one launch (start us, length us, event | category | flops | bytes accessed | tf_op | source)
XLA Modules:
  0.0 99.0 jit_solution(17331315389379216610)
XLA Ops:
  0.6 2.0 %shard_map.86 = bf16[32,4,2,1024]{3,2,1,0:T(2,128)(2,1)} custom-call(s32[1,32]{1,0:T(1,128)} %bitcast.29, s32[4,16]{1,0:T(4,128)} %bitcast.27, f32[4,16]{1,0:T(4,128)} %bitcast.28, bf16[8,7168]{1,0:T(8,128)(2,1)} %tokens_in.1), custom_call_target="tpu_custom_call" | custom-call | tf_op jit(solution)/shard_map/pallas_call | solution.py:162
  2.6 18.0 %all-to-all-start = ((bf16[128,2,1024]{2,1,0:T(2,128)(2,1)}), bf16[128,2,1024]{2,1,0:T(2,128)(2,1)S(1)}, u32[]{:S(2)}, u32[]{:S(2)}) async-start(bf16[128,2,1024]{2,1,0:T(2,128)(2,1)} %bitcast.26), calls=%async_computation | async-start | bytes 1048576 | tf_op jit(solution)/shard_map/all_to_all | solution.py:177
  20.6 4.3 %collective-permute-start.3 = (bf16[1024,896]{1,0:T(8,128)(2,1)}, bf16[1024,896]{1,0:T(8,128)(2,1)S(1)}, u32[]{:S(2)}, u32[]{:S(2)}) collective-permute-start(bf16[1024,896]{1,0:T(8,128)(2,1)} %bitcast.18), channel_id=1, source_target_pairs={{0,1},{1,0},{2,3},{3,2},{4,5},{5,4},{6,7},{7,6},{8,9},{9,8},{10,11... | collective-permute-start | bytes 5505032 | tf_op jit(solution)/shard_map/ppermute | solution.py:185
  24.9 0.1 stack.23.place
  25.0 12.2 %all-to-all-done = bf16[128,2,1024]{2,1,0:T(2,128)(2,1)S(1)} async-done(((bf16[128,2,1024]{2,1,0:T(2,128)(2,1)}), bf16[128,2,1024]{2,1,0:T(2,128)(2,1)S(1)}, u32[]{:S(2)}, u32[]{:S(2)}) %all-to-all-start) | async-done | bytes 524320 | tf_op jit(solution)/shard_map/all_to_all | solution.py:177
  37.2 0.1 copy.9
  37.3 0.0 copy-start
  37.4 1.7 %shard_map.87 = (bf16[64,1792]{1,0:T(8,128)(2,1)S(1)}, bf16[64,1792]{1,0:T(8,128)(2,1)S(1)}, bf16[64,1792]{1,0:T(8,128)(2,1)S(1)}, bf16[64,1792]{1,0:T(8,128)(2,1)S(1)}) custom-call(s32[5]{0:T(128)S(1)} %stack.23.place, bf16[128,2048]{1,0:T(8,128)(2,1)S(1)} %bitcast.22), custom_call_target="tpu_custom_call" | custom-call | flops 21474836480 | bytes 2097152 | tf_op jit(solution)/shard_map/pallas_call | solution.py:187
  39.1 14.9 %collective-permute-start.2 = (bf16[64,1792]{1,0:T(8,128)(2,1)S(1)}, bf16[64,1792]{1,0:T(8,128)(2,1)S(1)}, u32[]{:S(2)}, u32[]{:S(2)}) collective-permute-start(bf16[64,1792]{1,0:T(8,128)(2,1)S(1)} %get-tuple-element.17), channel_id=1, source_target_pairs={{0,16},{8,24},{16,0},{24,8},{1,17},{9,25},{17,1},{25,9},{2,18},{10... | collective-permute-start | bytes 688136 | tf_op jit(solution)/shard_map/ppermute | solution.py:202
  54.0 5.8 %collective-permute-start = (bf16[64,1792]{1,0:T(8,128)(2,1)S(1)}, bf16[64,1792]{1,0:T(8,128)(2,1)S(1)}, u32[]{:S(2)}, u32[]{:S(2)}) collective-permute-start(bf16[64,1792]{1,0:T(8,128)(2,1)S(1)} %get-tuple-element.15), channel_id=1, source_target_pairs={{0,8},{8,16},{16,24},{24,0},{1,9},{9,17},{17,25},{25,1},{2,10},{10... | collective-permute-start | bytes 688136 | tf_op jit(solution)/shard_map/ppermute | solution.py:202
  59.8 1.9 %collective-permute-start.1 = (bf16[64,1792]{1,0:T(8,128)(2,1)S(1)}, bf16[64,1792]{1,0:T(8,128)(2,1)S(1)}, u32[]{:S(2)}, u32[]{:S(2)}) collective-permute-start(bf16[64,1792]{1,0:T(8,128)(2,1)S(1)} %get-tuple-element.16), channel_id=1, source_target_pairs={{0,24},{8,0},{16,8},{24,16},{1,25},{9,1},{17,9},{25,17},{2,26},{10... | collective-permute-start | bytes 688136 | tf_op jit(solution)/shard_map/ppermute | solution.py:202
  61.7 0.0 collective-permute-done.3.w_sib
  61.7 0.0 copy-done
  61.8 0.8 shard_map.88.refs_2_
  62.6 0.0 collective-permute-done.2.refs_1_
  62.6 0.7 shard_map.89
  63.3 4.3 %collective-permute-start.4 = (bf16[128,512]{1,0:T(8,128)(2,1)S(1)}, bf16[128,512]{1,0:T(8,128)(2,1)S(1)}, u32[]{:S(2)}, u32[]{:S(2)}) collective-permute-start(bf16[128,512]{1,0:T(8,128)(2,1)S(1)} %shard_map.89), channel_id=1, source_target_pairs={{0,2},{2,0},{1,3},{3,1},{4,6},{6,4},{5,7},{7,5},{8,10},{10,8},{9,1... | collective-permute-start | bytes 393224 | tf_op jit(solution)/shard_map/ppermute | solution.py:227
  67.7 3.5 %collective-permute-done.refs_0_ = bf16[64,1792]{1,0:T(8,128)(2,1)S(1)} collective-permute-done((bf16[64,1792]{1,0:T(8,128)(2,1)S(1)}, bf16[64,1792]{1,0:T(8,128)(2,1)S(1)}, u32[]{:S(2)}, u32[]{:S(2)}) %collective-permute-start) | collective-permute-done | bytes 229408 | tf_op jit(solution)/shard_map/ppermute | solution.py:202
  71.2 4.5 %collective-permute-done.1.refs_1_ = bf16[64,1792]{1,0:T(8,128)(2,1)S(1)} collective-permute-done((bf16[64,1792]{1,0:T(8,128)(2,1)S(1)}, bf16[64,1792]{1,0:T(8,128)(2,1)S(1)}, u32[]{:S(2)}, u32[]{:S(2)}) %collective-permute-start.1) | collective-permute-done | bytes 229408 | tf_op jit(solution)/shard_map/ppermute | solution.py:202
  75.7 0.7 shard_map.90
  76.4 1.9 %collective-permute-start.6 = (bf16[128,512]{1,0:T(8,128)(2,1)S(1)}, bf16[128,512]{1,0:T(8,128)(2,1)S(1)}, u32[]{:S(2)}, u32[]{:S(2)}) collective-permute-start(bf16[128,512]{1,0:T(8,128)(2,1)S(1)} %shard_map.90), channel_id=1, source_target_pairs={{0,4},{4,0},{1,5},{5,1},{2,6},{6,2},{3,7},{7,3},{8,12},{12,8},{9,1... | collective-permute-start | bytes 393224 | tf_op jit(solution)/shard_map/ppermute | solution.py:232
  78.3 0.7 shard_map.91
  79.0 0.0 collective-permute-done.4
  79.1 0.0 copy-start.1
  79.1 0.0 copy-start.2
  79.1 0.7 shard_map.92
  79.8 2.6 %collective-permute-done.6 = bf16[128,512]{1,0:T(8,128)(2,1)S(1)} collective-permute-done((bf16[128,512]{1,0:T(8,128)(2,1)S(1)}, bf16[128,512]{1,0:T(8,128)(2,1)S(1)}, u32[]{:S(2)}, u32[]{:S(2)}) %collective-permute-start.6) | collective-permute-done | bytes 131104 | tf_op jit(solution)/shard_map/ppermute | solution.py:232
  82.4 3.8 %collective-permute-start.7 = (bf16[128,256]{1,0:T(8,128)(2,1)S(1)}, bf16[128,256]{1,0:T(8,128)(2,1)S(1)}, u32[]{:S(2)}, u32[]{:S(2)}) collective-permute-start(bf16[128,256]{1,0:T(8,128)(2,1)S(1)} %fusion.7), channel_id=1, source_target_pairs={{0,2},{2,0},{1,3},{3,1},{4,6},{6,4},{5,7},{7,5},{8,10},{10,8},{9,1... | collective-permute-start | bytes 196616 | tf_op jit(solution)/shard_map/ppermute | solution.py:240
  86.3 2.8 %collective-permute-start.5 = (bf16[128,256]{1,0:T(8,128)(2,1)S(1)}, bf16[128,256]{1,0:T(8,128)(2,1)S(1)}, u32[]{:S(2)}, u32[]{:S(2)}) collective-permute-start(bf16[128,256]{1,0:T(8,128)(2,1)S(1)} %fusion.9), channel_id=1, source_target_pairs={{0,4},{4,0},{1,5},{5,1},{2,6},{6,2},{3,7},{7,3},{8,12},{12,8},{9,1... | collective-permute-start | bytes 196616 | tf_op jit(solution)/shard_map/ppermute | solution.py:236
  89.1 2.3 %collective-permute-done.7 = bf16[128,256]{1,0:T(8,128)(2,1)S(1)} collective-permute-done((bf16[128,256]{1,0:T(8,128)(2,1)S(1)}, bf16[128,256]{1,0:T(8,128)(2,1)S(1)}, u32[]{:S(2)}, u32[]{:S(2)}) %collective-permute-start.7) | collective-permute-done | bytes 65568 | tf_op jit(solution)/shard_map/ppermute | solution.py:240
  91.4 0.0 collective-permute-done.5
  91.5 5.3 %collective-permute-start.8 = (f32[256,128]{1,0:T(8,128)S(1)}, f32[256,128]{1,0:T(8,128)S(1)}, u32[]{:S(2)}, u32[]{:S(2)}) collective-permute-start(f32[256,128]{1,0:T(8,128)S(1)} %get-tuple-element.26), channel_id=1, source_target_pairs={{0,1},{1,0},{2,3},{3,2},{4,5},{5,4},{6,7},{7,6},{8,9},{9,8},{10,11... | collective-permute-start | bytes 393224 | tf_op jit(solution)/shard_map/ppermute | solution.py:244
  96.8 0.0 copy-done.1
  96.8 0.0 copy-done.2
  96.8 0.1 convert_multiply_fusion
  96.9 0.8 collective-permute-done.8
  97.7 1.3 %shard_map.93 = (bf16[4,4,2,16,128]{4,3,2,1,0:T(8,128)(2,1)}, bf16[4,4,2,16,128]{4,3,2,1,0:T(8,128)(2,1)}) custom-call(s32[5]{0:T(128)S(1)} %stack.23.place, f32[4,4,16,128]{3,2,1,0:T(8,128)S(1)} %bitcast.23, f32[4,4,16,128]{3,2,1,0:T(8,128)S(1)} %bitcast.24, f32[4,4,2,16,128]{4,3,2,1,0:T(8,128)S(1)} %bitcast.21, f32[4,4,2,16,128]{4,3,2,1,0:T(8,128)S(1)} %bitcast.20), custom_call_target="tpu_custom_call" | custom-call | tf_op jit(solution)/shard_map/pallas_call | solution.py:253
  (5 shorter events, 0.1 us)
Async XLA Ops:
  2.6 34.6 %all-to-all-start = ((bf16[128,2,1024]{2,1,0:T(2,128)(2,1)}), bf16[128,2,1024]{2,1,0:T(2,128)(2,1)S(1)}, u32[]{:S(2)}, u32[]{:S(2)}) async-start(bf16[128,2,1024]{2,1,0:T(2,128)(2,1)} %bitcast.26), calls=%async_computation | async-start | bytes 1048576 | tf_op jit(solution)/shard_map/all_to_all | solution.py:177
  20.6 41.1 %collective-permute-start.3 = (bf16[1024,896]{1,0:T(8,128)(2,1)}, bf16[1024,896]{1,0:T(8,128)(2,1)S(1)}, u32[]{:S(2)}, u32[]{:S(2)}) collective-permute-start(bf16[1024,896]{1,0:T(8,128)(2,1)} %bitcast.18), channel_id=1, source_target_pairs={{0,1},{1,0},{2,3},{3,2},{4,5},{5,4},{6,7},{7,6},{8,9},{9,8},{10,11... | collective-permute-start | bytes 5505032 | tf_op jit(solution)/shard_map/ppermute | solution.py:185
  37.3 24.4 %copy-start = (bf16[1,1,1024,896]{3,2,1,0:T(8,128)(2,1)S(1)}, bf16[1,1,1024,896]{3,2,1,0:T(8,128)(2,1)}, u32[]{:S(2)}) copy-start(bf16[1,1,1024,896]{3,2,1,0:T(8,128)(2,1)} %param.11) | copy-start | bytes 5505028
  39.1 23.5 %collective-permute-start.2 = (bf16[64,1792]{1,0:T(8,128)(2,1)S(1)}, bf16[64,1792]{1,0:T(8,128)(2,1)S(1)}, u32[]{:S(2)}, u32[]{:S(2)}) collective-permute-start(bf16[64,1792]{1,0:T(8,128)(2,1)S(1)} %get-tuple-element.17), channel_id=1, source_target_pairs={{0,16},{8,24},{16,0},{24,8},{1,17},{9,25},{17,1},{25,9},{2,18},{10... | collective-permute-start | bytes 688136 | tf_op jit(solution)/shard_map/ppermute | solution.py:202
  54.0 17.2 %collective-permute-start = (bf16[64,1792]{1,0:T(8,128)(2,1)S(1)}, bf16[64,1792]{1,0:T(8,128)(2,1)S(1)}, u32[]{:S(2)}, u32[]{:S(2)}) collective-permute-start(bf16[64,1792]{1,0:T(8,128)(2,1)S(1)} %get-tuple-element.15), channel_id=1, source_target_pairs={{0,8},{8,16},{16,24},{24,0},{1,9},{9,17},{17,25},{25,1},{2,10},{10... | collective-permute-start | bytes 688136 | tf_op jit(solution)/shard_map/ppermute | solution.py:202
  59.8 15.8 %collective-permute-start.1 = (bf16[64,1792]{1,0:T(8,128)(2,1)S(1)}, bf16[64,1792]{1,0:T(8,128)(2,1)S(1)}, u32[]{:S(2)}, u32[]{:S(2)}) collective-permute-start(bf16[64,1792]{1,0:T(8,128)(2,1)S(1)} %get-tuple-element.16), channel_id=1, source_target_pairs={{0,24},{8,0},{16,8},{24,16},{1,25},{9,1},{17,9},{25,17},{2,26},{10... | collective-permute-start | bytes 688136 | tf_op jit(solution)/shard_map/ppermute | solution.py:202
  63.3 15.7 %collective-permute-start.4 = (bf16[128,512]{1,0:T(8,128)(2,1)S(1)}, bf16[128,512]{1,0:T(8,128)(2,1)S(1)}, u32[]{:S(2)}, u32[]{:S(2)}) collective-permute-start(bf16[128,512]{1,0:T(8,128)(2,1)S(1)} %shard_map.89), channel_id=1, source_target_pairs={{0,2},{2,0},{1,3},{3,1},{4,6},{6,4},{5,7},{7,5},{8,10},{10,8},{9,1... | collective-permute-start | bytes 393224 | tf_op jit(solution)/shard_map/ppermute | solution.py:227
  76.4 6.0 %collective-permute-start.6 = (bf16[128,512]{1,0:T(8,128)(2,1)S(1)}, bf16[128,512]{1,0:T(8,128)(2,1)S(1)}, u32[]{:S(2)}, u32[]{:S(2)}) collective-permute-start(bf16[128,512]{1,0:T(8,128)(2,1)S(1)} %shard_map.90), channel_id=1, source_target_pairs={{0,4},{4,0},{1,5},{5,1},{2,6},{6,2},{3,7},{7,3},{8,12},{12,8},{9,1... | collective-permute-start | bytes 393224 | tf_op jit(solution)/shard_map/ppermute | solution.py:232
  79.1 17.7 %copy-start.1 = (bf16[1,1,32,16,128]{4,3,2,1,0:T(8,128)(2,1)S(1)}, bf16[1,1,32,16,128]{4,3,2,1,0:T(8,128)(2,1)}, u32[]{:S(2)}) copy-start(bf16[1,1,32,16,128]{4,3,2,1,0:T(8,128)(2,1)} %param.12) | copy-start | bytes 393220
  79.1 17.7 %copy-start.2 = (bf16[1,1,32,16,128]{4,3,2,1,0:T(8,128)(2,1)S(1)}, bf16[1,1,32,16,128]{4,3,2,1,0:T(8,128)(2,1)}, u32[]{:S(2)}) copy-start(bf16[1,1,32,16,128]{4,3,2,1,0:T(8,128)(2,1)} %param.13) | copy-start | bytes 393220
  82.4 8.9 %collective-permute-start.7 = (bf16[128,256]{1,0:T(8,128)(2,1)S(1)}, bf16[128,256]{1,0:T(8,128)(2,1)S(1)}, u32[]{:S(2)}, u32[]{:S(2)}) collective-permute-start(bf16[128,256]{1,0:T(8,128)(2,1)S(1)} %fusion.7), channel_id=1, source_target_pairs={{0,2},{2,0},{1,3},{3,1},{4,6},{6,4},{5,7},{7,5},{8,10},{10,8},{9,1... | collective-permute-start | bytes 196616 | tf_op jit(solution)/shard_map/ppermute | solution.py:240
  86.3 5.1 %collective-permute-start.5 = (bf16[128,256]{1,0:T(8,128)(2,1)S(1)}, bf16[128,256]{1,0:T(8,128)(2,1)S(1)}, u32[]{:S(2)}, u32[]{:S(2)}) collective-permute-start(bf16[128,256]{1,0:T(8,128)(2,1)S(1)} %fusion.9), channel_id=1, source_target_pairs={{0,4},{4,0},{1,5},{5,1},{2,6},{6,2},{3,7},{7,3},{8,12},{12,8},{9,1... | collective-permute-start | bytes 196616 | tf_op jit(solution)/shard_map/ppermute | solution.py:236
  91.5 6.3 %collective-permute-start.8 = (f32[256,128]{1,0:T(8,128)S(1)}, f32[256,128]{1,0:T(8,128)S(1)}, u32[]{:S(2)}, u32[]{:S(2)}) collective-permute-start(f32[256,128]{1,0:T(8,128)S(1)} %get-tuple-element.26), channel_id=1, source_target_pairs={{0,1},{1,0},{2,3},{3,2},{4,5},{5,4},{6,7},{7,6},{8,9},{9,8},{10,11... | collective-permute-start | bytes 393224 | tf_op jit(solution)/shard_map/ppermute | solution.py:244

commit v7 on v6

--- a/solution.py
+++ b/solution.py
@@ -8,7 +8,7 @@
 NAMES = ("y", "xlo", "zhi", "zlo", "xhi", "core")
 EXTENTS = (8, 4, 4, 2, 2, 2)
 SWAP = ((0, 1), (1, 0))
-STEPS = (0, 2, 1, 3)
+STEPS = (0, 1, 2, 3)
 SMEM = pl.BlockSpec(memory_space=pltpu.SMEM)
 VMEM = pl.BlockSpec(memory_space=pltpu.VMEM)
 

time: 99.5 us -> 106 us (1.065)
  waiting for transfers between devices: 25.9 us -> 33.8 us
  starting transfers between devices: 63.1 us -> 61.2 us
    ppermute x3, waiting for transfers between devices: 8 us -> 14.7 us  [on_device(): pieces.append(lax.ppermute(out, 'zhi', pairs))]
    ppermute x1, starting transfers between devices: 4.32 us -> 2.47 us  [on_device(): got_a = lax.ppermute(give_a, 'xhi', SWAP)]
    ppermute x1, waiting for transfers between devices: 0.01 us -> 1.61 us  [on_device(): got_a = lax.ppermute(give_a, 'zlo', SWAP)]
    ppermute x1, starting transfers between devices: 3.8 us -> 5.27 us  [on_device(): got_b = lax.ppermute(give_b, 'xhi', SWAP)]
  transfers between devices with their start and end apart: 10 -> 10, of which waited for: 6 -> 8; matrix products, arithmetic and copies ran while one was open for 0% -> 0% of each run, Pallas kernels for 5% -> 5%
where the time goes in v7:
time: 106 us; the launch traced here: 105 us
  starting transfers between devices  61.2 us (58%)
  waiting for transfers between devices  33.8 us (32%)
  Pallas kernels  8.72 us (8%)
    ppermute x3, starting transfers between devices, on_device(): pieces.append(lax.ppermute(out, 'zhi', pairs))  22.6 us
    all_to_all x1, starting transfers between devices, on_device(): lax.all_to_all(outgoing, ('y', 'xlo', 'zlo', 'xhi'), split_axis=0, concat...  18 us
    ppermute x3, waiting for transfers between devices, on_device(): pieces.append(lax.ppermute(out, 'zhi', pairs))  14.7 us
    all_to_all x1, waiting for transfers between devices, on_device(): lax.all_to_all(outgoing, ('y', 'xlo', 'zlo', 'xhi'), split_axis=0, concat...  12.2 us
    ppermute x1, starting transfers between devices, on_device(): got_b = lax.ppermute(give_b, 'xhi', SWAP)  5.27 us
    ppermute x1, starting transfers between devices, on_device(): got = lax.ppermute(give, 'core', SWAP)  4.45 us
    ppermute x1, starting transfers between devices, on_device(): w_sib = lax.ppermute(w_own, 'core', SWAP)  4.26 us
    ppermute x1, waiting for transfers between devices, on_device(): got_b = lax.ppermute(give_b, 'zlo', SWAP)  2.96 us
  transfers between devices with their start and end apart: 10, of which 8 were waited for; matrix products, arithmetic and copies ran while one was open for 0% of the time, Pallas kernels for 5%

profile of v7, /device:TPU:1, one launch (start us, length us, event | category | flops | bytes accessed | tf_op | source)
XLA Modules:
  0.0 105.0 jit_solution(8391591974307639489)
XLA Ops:
  0.6 2.0 %shard_map.86 = bf16[32,4,2,1024]{3,2,1,0:T(2,128)(2,1)} custom-call(s32[1,32]{1,0:T(1,128)} %bitcast.29, s32[4,16]{1,0:T(4,128)} %bitcast.27, f32[4,16]{1,0:T(4,128)} %bitcast.28, bf16[8,7168]{1,0:T(8,128)(2,1)} %tokens_in.1), custom_call_target="tpu_custom_call" | custom-call | tf_op jit(solution)/shard_map/pallas_call | solution.py:162
  2.6 18.0 %all-to-all-start = ((bf16[128,2,1024]{2,1,0:T(2,128)(2,1)}), bf16[128,2,1024]{2,1,0:T(2,128)(2,1)S(1)}, u32[]{:S(2)}, u32[]{:S(2)}) async-start(bf16[128,2,1024]{2,1,0:T(2,128)(2,1)} %bitcast.26), calls=%async_computation | async-start | bytes 1048576 | tf_op jit(solution)/shard_map/all_to_all | solution.py:177
  20.6 4.3 %collective-permute-start.3 = (bf16[1024,896]{1,0:T(8,128)(2,1)}, bf16[1024,896]{1,0:T(8,128)(2,1)S(1)}, u32[]{:S(2)}, u32[]{:S(2)}) collective-permute-start(bf16[1024,896]{1,0:T(8,128)(2,1)} %bitcast.18), channel_id=1, source_target_pairs={{0,1},{1,0},{2,3},{3,2},{4,5},{5,4},{6,7},{7,6},{8,9},{9,8},{10,11... | collective-permute-start | bytes 5505032 | tf_op jit(solution)/shard_map/ppermute | solution.py:185
  24.9 0.1 stack.23.place
  25.0 12.2 %all-to-all-done = bf16[128,2,1024]{2,1,0:T(2,128)(2,1)S(1)} async-done(((bf16[128,2,1024]{2,1,0:T(2,128)(2,1)}), bf16[128,2,1024]{2,1,0:T(2,128)(2,1)S(1)}, u32[]{:S(2)}, u32[]{:S(2)}) %all-to-all-start) | async-done | bytes 524320 | tf_op jit(solution)/shard_map/all_to_all | solution.py:177
  37.2 0.1 copy.9
  37.3 0.0 copy-start
  37.4 1.7 %shard_map.87 = (bf16[64,1792]{1,0:T(8,128)(2,1)S(1)}, bf16[64,1792]{1,0:T(8,128)(2,1)S(1)}, bf16[64,1792]{1,0:T(8,128)(2,1)S(1)}, bf16[64,1792]{1,0:T(8,128)(2,1)S(1)}) custom-call(s32[5]{0:T(128)S(1)} %stack.23.place, bf16[128,2048]{1,0:T(8,128)(2,1)S(1)} %bitcast.22), custom_call_target="tpu_custom_call" | custom-call | flops 21474836480 | bytes 2097152 | tf_op jit(solution)/shard_map/pallas_call | solution.py:187
  39.1 9.1 %collective-permute-start.2 = (bf16[64,1792]{1,0:T(8,128)(2,1)S(1)}, bf16[64,1792]{1,0:T(8,128)(2,1)S(1)}, u32[]{:S(2)}, u32[]{:S(2)}) collective-permute-start(bf16[64,1792]{1,0:T(8,128)(2,1)S(1)} %get-tuple-element.17), channel_id=1, source_target_pairs={{0,8},{8,16},{16,24},{24,0},{1,9},{9,17},{17,25},{25,1},{2,10},{10... | collective-permute-start | bytes 688136 | tf_op jit(solution)/shard_map/ppermute | solution.py:202
  48.2 11.6 %collective-permute-start = (bf16[64,1792]{1,0:T(8,128)(2,1)S(1)}, bf16[64,1792]{1,0:T(8,128)(2,1)S(1)}, u32[]{:S(2)}, u32[]{:S(2)}) collective-permute-start(bf16[64,1792]{1,0:T(8,128)(2,1)S(1)} %get-tuple-element.15), channel_id=1, source_target_pairs={{0,16},{8,24},{16,0},{24,8},{1,17},{9,25},{17,1},{25,9},{2,18},{10... | collective-permute-start | bytes 688136 | tf_op jit(solution)/shard_map/ppermute | solution.py:202
  59.8 1.9 %collective-permute-start.1 = (bf16[64,1792]{1,0:T(8,128)(2,1)S(1)}, bf16[64,1792]{1,0:T(8,128)(2,1)S(1)}, u32[]{:S(2)}, u32[]{:S(2)}) collective-permute-start(bf16[64,1792]{1,0:T(8,128)(2,1)S(1)} %get-tuple-element.16), channel_id=1, source_target_pairs={{0,24},{8,0},{16,8},{24,16},{1,25},{9,1},{17,9},{25,17},{2,26},{10... | collective-permute-start | bytes 688136 | tf_op jit(solution)/shard_map/ppermute | solution.py:202
  61.7 0.0 collective-permute-done.3.w_sib
  61.8 0.0 copy-done
  61.8 0.8 shard_map.88.refs_2_
  62.6 1.9 %collective-permute-done.2.refs_1_ = bf16[64,1792]{1,0:T(8,128)(2,1)S(1)} collective-permute-done((bf16[64,1792]{1,0:T(8,128)(2,1)S(1)}, bf16[64,1792]{1,0:T(8,128)(2,1)S(1)}, u32[]{:S(2)}, u32[]{:S(2)}) %collective-permute-start.2) | collective-permute-done | bytes 229408 | tf_op jit(solution)/shard_map/ppermute | solution.py:202
  64.4 0.7 shard_map.89
  65.2 2.5 %collective-permute-start.4 = (bf16[128,512]{1,0:T(8,128)(2,1)S(1)}, bf16[128,512]{1,0:T(8,128)(2,1)S(1)}, u32[]{:S(2)}, u32[]{:S(2)}) collective-permute-start(bf16[128,512]{1,0:T(8,128)(2,1)S(1)} %shard_map.89), channel_id=1, source_target_pairs={{0,2},{2,0},{1,3},{3,1},{4,6},{6,4},{5,7},{7,5},{8,10},{10,8},{9,1... | collective-permute-start | bytes 393224 | tf_op jit(solution)/shard_map/ppermute | solution.py:227
  67.7 7.3 %collective-permute-done.refs_0_ = bf16[64,1792]{1,0:T(8,128)(2,1)S(1)} collective-permute-done((bf16[64,1792]{1,0:T(8,128)(2,1)S(1)}, bf16[64,1792]{1,0:T(8,128)(2,1)S(1)}, u32[]{:S(2)}, u32[]{:S(2)}) %collective-permute-start) | collective-permute-done | bytes 229408 | tf_op jit(solution)/shard_map/ppermute | solution.py:202
  75.0 5.6 %collective-permute-done.1.refs_1_ = bf16[64,1792]{1,0:T(8,128)(2,1)S(1)} collective-permute-done((bf16[64,1792]{1,0:T(8,128)(2,1)S(1)}, bf16[64,1792]{1,0:T(8,128)(2,1)S(1)}, u32[]{:S(2)}, u32[]{:S(2)}) %collective-permute-start.1) | collective-permute-done | bytes 229408 | tf_op jit(solution)/shard_map/ppermute | solution.py:202
  80.5 0.7 shard_map.90
  81.2 1.9 %collective-permute-start.6 = (bf16[128,512]{1,0:T(8,128)(2,1)S(1)}, bf16[128,512]{1,0:T(8,128)(2,1)S(1)}, u32[]{:S(2)}, u32[]{:S(2)}) collective-permute-start(bf16[128,512]{1,0:T(8,128)(2,1)S(1)} %shard_map.90), channel_id=1, source_target_pairs={{0,4},{4,0},{1,5},{5,1},{2,6},{6,2},{3,7},{7,3},{8,12},{12,8},{9,1... | collective-permute-start | bytes 393224 | tf_op jit(solution)/shard_map/ppermute | solution.py:232
  83.2 0.7 shard_map.91
  83.9 0.0 collective-permute-done.4
  83.9 0.0 copy-start.1
  84.0 0.0 copy-start.2
  84.0 0.7 shard_map.92
  84.7 3.0 %collective-permute-done.6 = bf16[128,512]{1,0:T(8,128)(2,1)S(1)} collective-permute-done((bf16[128,512]{1,0:T(8,128)(2,1)S(1)}, bf16[128,512]{1,0:T(8,128)(2,1)S(1)}, u32[]{:S(2)}, u32[]{:S(2)}) %collective-permute-start.6) | collective-permute-done | bytes 131104 | tf_op jit(solution)/shard_map/ppermute | solution.py:232
  87.7 5.3 %collective-permute-start.7 = (bf16[128,256]{1,0:T(8,128)(2,1)S(1)}, bf16[128,256]{1,0:T(8,128)(2,1)S(1)}, u32[]{:S(2)}, u32[]{:S(2)}) collective-permute-start(bf16[128,256]{1,0:T(8,128)(2,1)S(1)} %fusion.7), channel_id=1, source_target_pairs={{0,2},{2,0},{1,3},{3,1},{4,6},{6,4},{5,7},{7,5},{8,10},{10,8},{9,1... | collective-permute-start | bytes 196616 | tf_op jit(solution)/shard_map/ppermute | solution.py:240
  93.0 2.2 %collective-permute-start.5 = (bf16[128,256]{1,0:T(8,128)(2,1)S(1)}, bf16[128,256]{1,0:T(8,128)(2,1)S(1)}, u32[]{:S(2)}, u32[]{:S(2)}) collective-permute-start(bf16[128,256]{1,0:T(8,128)(2,1)S(1)} %fusion.9), channel_id=1, source_target_pairs={{0,4},{4,0},{1,5},{5,1},{2,6},{6,2},{3,7},{7,3},{8,12},{12,8},{9,1... | collective-permute-start | bytes 196616 | tf_op jit(solution)/shard_map/ppermute | solution.py:236
  95.2 1.4 %collective-permute-done.7 = bf16[128,256]{1,0:T(8,128)(2,1)S(1)} collective-permute-done((bf16[128,256]{1,0:T(8,128)(2,1)S(1)}, bf16[128,256]{1,0:T(8,128)(2,1)S(1)}, u32[]{:S(2)}, u32[]{:S(2)}) %collective-permute-start.7) | collective-permute-done | bytes 65568 | tf_op jit(solution)/shard_map/ppermute | solution.py:240
  96.7 1.6 %collective-permute-done.5 = bf16[128,256]{1,0:T(8,128)(2,1)S(1)} collective-permute-done((bf16[128,256]{1,0:T(8,128)(2,1)S(1)}, bf16[128,256]{1,0:T(8,128)(2,1)S(1)}, u32[]{:S(2)}, u32[]{:S(2)}) %collective-permute-start.5) | collective-permute-done | bytes 65568 | tf_op jit(solution)/shard_map/ppermute | solution.py:236
  98.3 4.4 %collective-permute-start.8 = (f32[256,128]{1,0:T(8,128)S(1)}, f32[256,128]{1,0:T(8,128)S(1)}, u32[]{:S(2)}, u32[]{:S(2)}) collective-permute-start(f32[256,128]{1,0:T(8,128)S(1)} %get-tuple-element.26), channel_id=1, source_target_pairs={{0,1},{1,0},{2,3},{3,2},{4,5},{5,4},{6,7},{7,6},{8,9},{9,8},{10,11... | collective-permute-start | bytes 393224 | tf_op jit(solution)/shard_map/ppermute | solution.py:244
  102.8 0.0 copy-done.1
  102.8 0.0 copy-done.2
  102.8 0.1 convert_multiply_fusion
  102.9 0.8 collective-permute-done.8
  103.7 1.3 %shard_map.93 = (bf16[4,4,2,16,128]{4,3,2,1,0:T(8,128)(2,1)}, bf16[4,4,2,16,128]{4,3,2,1,0:T(8,128)(2,1)}) custom-call(s32[5]{0:T(128)S(1)} %stack.23.place, f32[4,4,16,128]{3,2,1,0:T(8,128)S(1)} %bitcast.23, f32[4,4,16,128]{3,2,1,0:T(8,128)S(1)} %bitcast.24, f32[4,4,2,16,128]{4,3,2,1,0:T(8,128)S(1)} %bitcast.21, f32[4,4,2,16,128]{4,3,2,1,0:T(8,128)S(1)} %bitcast.20), custom_call_target="tpu_custom_call" | custom-call | tf_op jit(solution)/shard_map/pallas_call | solution.py:253
  (5 shorter events, 0.1 us)
Async XLA Ops:
  2.6 34.6 %all-to-all-start = ((bf16[128,2,1024]{2,1,0:T(2,128)(2,1)}), bf16[128,2,1024]{2,1,0:T(2,128)(2,1)S(1)}, u32[]{:S(2)}, u32[]{:S(2)}) async-start(bf16[128,2,1024]{2,1,0:T(2,128)(2,1)} %bitcast.26), calls=%async_computation | async-start | bytes 1048576 | tf_op jit(solution)/shard_map/all_to_all | solution.py:177
  20.6 41.1 %collective-permute-start.3 = (bf16[1024,896]{1,0:T(8,128)(2,1)}, bf16[1024,896]{1,0:T(8,128)(2,1)S(1)}, u32[]{:S(2)}, u32[]{:S(2)}) collective-permute-start(bf16[1024,896]{1,0:T(8,128)(2,1)} %bitcast.18), channel_id=1, source_target_pairs={{0,1},{1,0},{2,3},{3,2},{4,5},{5,4},{6,7},{7,6},{8,9},{9,8},{10,11... | collective-permute-start | bytes 5505032 | tf_op jit(solution)/shard_map/ppermute | solution.py:185
  37.3 24.4 %copy-start = (bf16[1,1,1024,896]{3,2,1,0:T(8,128)(2,1)S(1)}, bf16[1,1,1024,896]{3,2,1,0:T(8,128)(2,1)}, u32[]{:S(2)}) copy-start(bf16[1,1,1024,896]{3,2,1,0:T(8,128)(2,1)} %param.11) | copy-start | bytes 5505028
  39.1 25.4 %collective-permute-start.2 = (bf16[64,1792]{1,0:T(8,128)(2,1)S(1)}, bf16[64,1792]{1,0:T(8,128)(2,1)S(1)}, u32[]{:S(2)}, u32[]{:S(2)}) collective-permute-start(bf16[64,1792]{1,0:T(8,128)(2,1)S(1)} %get-tuple-element.17), channel_id=1, source_target_pairs={{0,8},{8,16},{16,24},{24,0},{1,9},{9,17},{17,25},{25,1},{2,10},{10... | collective-permute-start | bytes 688136 | tf_op jit(solution)/shard_map/ppermute | solution.py:202
  48.2 26.7 %collective-permute-start = (bf16[64,1792]{1,0:T(8,128)(2,1)S(1)}, bf16[64,1792]{1,0:T(8,128)(2,1)S(1)}, u32[]{:S(2)}, u32[]{:S(2)}) collective-permute-start(bf16[64,1792]{1,0:T(8,128)(2,1)S(1)} %get-tuple-element.15), channel_id=1, source_target_pairs={{0,16},{8,24},{16,0},{24,8},{1,17},{9,25},{17,1},{25,9},{2,18},{10... | collective-permute-start | bytes 688136 | tf_op jit(solution)/shard_map/ppermute | solution.py:202
  59.8 20.7 %collective-permute-start.1 = (bf16[64,1792]{1,0:T(8,128)(2,1)S(1)}, bf16[64,1792]{1,0:T(8,128)(2,1)S(1)}, u32[]{:S(2)}, u32[]{:S(2)}) collective-permute-start(bf16[64,1792]{1,0:T(8,128)(2,1)S(1)} %get-tuple-element.16), channel_id=1, source_target_pairs={{0,24},{8,0},{16,8},{24,16},{1,25},{9,1},{17,9},{25,17},{2,26},{10... | collective-permute-start | bytes 688136 | tf_op jit(solution)/shard_map/ppermute | solution.py:202
  65.2 18.7 %collective-permute-start.4 = (bf16[128,512]{1,0:T(8,128)(2,1)S(1)}, bf16[128,512]{1,0:T(8,128)(2,1)S(1)}, u32[]{:S(2)}, u32[]{:S(2)}) collective-permute-start(bf16[128,512]{1,0:T(8,128)(2,1)S(1)} %shard_map.89), channel_id=1, source_target_pairs={{0,2},{2,0},{1,3},{3,1},{4,6},{6,4},{5,7},{7,5},{8,10},{10,8},{9,1... | collective-permute-start | bytes 393224 | tf_op jit(solution)/shard_map/ppermute | solution.py:227
  81.2 6.4 %collective-permute-start.6 = (bf16[128,512]{1,0:T(8,128)(2,1)S(1)}, bf16[128,512]{1,0:T(8,128)(2,1)S(1)}, u32[]{:S(2)}, u32[]{:S(2)}) collective-permute-start(bf16[128,512]{1,0:T(8,128)(2,1)S(1)} %shard_map.90), channel_id=1, source_target_pairs={{0,4},{4,0},{1,5},{5,1},{2,6},{6,2},{3,7},{7,3},{8,12},{12,8},{9,1... | collective-permute-start | bytes 393224 | tf_op jit(solution)/shard_map/ppermute | solution.py:232
  83.9 18.8 %copy-start.1 = (bf16[1,1,32,16,128]{4,3,2,1,0:T(8,128)(2,1)S(1)}, bf16[1,1,32,16,128]{4,3,2,1,0:T(8,128)(2,1)}, u32[]{:S(2)}) copy-start(bf16[1,1,32,16,128]{4,3,2,1,0:T(8,128)(2,1)} %param.12) | copy-start | bytes 393220
  84.0 18.8 %copy-start.2 = (bf16[1,1,32,16,128]{4,3,2,1,0:T(8,128)(2,1)S(1)}, bf16[1,1,32,16,128]{4,3,2,1,0:T(8,128)(2,1)}, u32[]{:S(2)}) copy-start(bf16[1,1,32,16,128]{4,3,2,1,0:T(8,128)(2,1)} %param.13) | copy-start | bytes 393220
  87.7 9.0 %collective-permute-start.7 = (bf16[128,256]{1,0:T(8,128)(2,1)S(1)}, bf16[128,256]{1,0:T(8,128)(2,1)S(1)}, u32[]{:S(2)}, u32[]{:S(2)}) collective-permute-start(bf16[128,256]{1,0:T(8,128)(2,1)S(1)} %fusion.7), channel_id=1, source_target_pairs={{0,2},{2,0},{1,3},{3,1},{4,6},{6,4},{5,7},{7,5},{8,10},{10,8},{9,1... | collective-permute-start | bytes 196616 | tf_op jit(solution)/shard_map/ppermute | solution.py:240
  93.0 5.3 %collective-permute-start.5 = (bf16[128,256]{1,0:T(8,128)(2,1)S(1)}, bf16[128,256]{1,0:T(8,128)(2,1)S(1)}, u32[]{:S(2)}, u32[]{:S(2)}) collective-permute-start(bf16[128,256]{1,0:T(8,128)(2,1)S(1)} %fusion.9), channel_id=1, source_target_pairs={{0,4},{4,0},{1,5},{5,1},{2,6},{6,2},{3,7},{7,3},{8,12},{12,8},{9,1... | collective-permute-start | bytes 196616 | tf_op jit(solution)/shard_map/ppermute | solution.py:236
  98.3 5.4 %collective-permute-start.8 = (f32[256,128]{1,0:T(8,128)S(1)}, f32[256,128]{1,0:T(8,128)S(1)}, u32[]{:S(2)}, u32[]{:S(2)}) collective-permute-start(f32[256,128]{1,0:T(8,128)S(1)} %get-tuple-element.26), channel_id=1, source_target_pairs={{0,1},{1,0},{2,3},{3,2},{4,5},{5,4},{6,7},{7,6},{8,9},{9,8},{10,11... | collective-permute-start | bytes 393224 | tf_op jit(solution)/shard_map/ppermute | solution.py:244
